TPU v7x, 32 devices: a whole 2x2x4 slice. The times are simulated.
32 devices in a mesh: row: 8 (over z, core), seq: 4 (over y, x).
Axes of the slice: x: 2, y: 2, z: 4, core: 2. Of those that a mesh axis runs over, the one named last changes fastest.
Arguments:
- tokens_in: bfloat16 [24, 1024, 768], P('row', 'seq'), may hold values from -6 to 6
- lengths: int32 [24, 8], P('row'), may hold values from 1 to 1017, as said below
- ln1_gain: float32 [768], replicated, may hold values from 0.1 to 1.9
- ln1_bias: float32 [768], replicated, may hold values from -1.75 to 1.75
- qkv_weight: bfloat16 [768, 2304], replicated, may hold values from -0.21875 to 0.21875
- qv_bias: float32 [1536], replicated, may hold values from -3 to 3
- proj_weight: bfloat16 [768, 768], replicated, may hold values from -3.5 to 3.5
- proj_bias: float32 [768], replicated, may hold values from -3 to 3
- ln2_gain: float32 [768], replicated, may hold values from 0.1 to 1.9
- ln2_bias: float32 [768], replicated, may hold values from -1.75 to 1.75
- fc_weight: bfloat16 [768, 3072], replicated, may hold values from -0.21875 to 0.21875
- fc_bias: float32 [3072], replicated, may hold values from -3 to 3
- out_weight: bfloat16 [3072, 768], replicated, may hold values from -0.4375 to 0.4375
- out_bias: float32 [768], replicated, may hold values from -3 to 3
- cotangent: bfloat16 [24, 1024, 768], P('row', 'seq'), may hold values from -6 to 6
Outputs:
- layer_out: bfloat16 [24, 1024, 768], P('row', 'seq')
- input_grad: float32 [24, 1024, 768], P('row', 'seq')
- ln1_gain_grad: float32 [768], replicated
- ln1_bias_grad: float32 [768], replicated
- qkv_weight_grad: float32 [768, 2304], replicated
- qv_bias_grad: float32 [1536], replicated
- proj_weight_grad: float32 [768, 768], replicated
- proj_bias_grad: float32 [768], replicated
- ln2_gain_grad: float32 [768], replicated
- ln2_bias_grad: float32 [768], replicated
- fc_weight_grad: float32 [768, 3072], replicated
- fc_bias_grad: float32 [3072], replicated
- out_weight_grad: float32 [3072, 768], replicated
- out_bias_grad: float32 [768], replicated
Inputs may be any that keep to these rules, and one draw needn't show every extreme that they name: Each row's 8 lengths are positive, sum to at most 1024 and to at least 95 percent of it; the rest of the row is padding.
All inputs are finite; a program needn't handle non-finite values.
Results may differ from a plain program's by a relative error of at most 0.04.
Values may be sent and summed in bfloat16 or wider, within the bound.
A program may use at most 448 MiB of HBM per device.

v0:
```python
import jax
import jax.numpy as jnp
from jax import lax
from jax.sharding import PartitionSpec as P

HEAD = 64


branch_scale = 12.0 ** (-0.5)
masked_value = -1e30
norm_eps = 1e-05


def layer_norm(values, gain, shift):
    center = values - jnp.mean(values, axis=-1, keepdims=True)
    spread = jnp.mean(center * center, axis=-1, keepdims=True)
    return center * lax.rsqrt(spread + norm_eps) * gain + shift


def gelu_tanh(values):
    return jax.nn.gelu(values, approximate=True)


def left_dot(left, right):
    return lax.dot_general(
        left, right, (((0,), (0,)), ((), ())), preferred_element_type=jnp.float32
    )


def right_dot(left, right):
    return lax.dot_general(
        left, right, (((1,), (1,)), ((), ())), preferred_element_type=jnp.float32
    )


def allowed_mask(query_pos, query_seg, key_pos, key_seg):
    return (key_pos[None, None, :] <= query_pos[None, :, None]) & (
        key_seg[:, None, :] == query_seg[:, :, None]
    )


def local(
    tokens_in,
    lengths,
    ln1_gain,
    ln1_bias,
    qkv_weight,
    qv_bias,
    proj_weight,
    proj_bias,
    ln2_gain,
    ln2_bias,
    fc_weight,
    fc_bias,
    out_weight,
    out_bias,
    cotangent,
):
    row_count, span_len, model_width = tokens_in.shape
    head_count = model_width // HEAD
    scale = HEAD ** (-0.5)
    seq_parts = lax.axis_size("seq")
    row_len = span_len * seq_parts
    first_pos = lax.axis_index("seq") * span_len
    doc_count = lengths.shape[1]
    positions = jnp.arange(row_len, dtype=jnp.int32)
    ends = jnp.cumsum(lengths, axis=1)
    segments = jnp.sum((positions[None, :, None] >= ends[:, None, :]).astype(jnp.int32), axis=2)
    my_segs = lax.dynamic_slice_in_dim(segments, first_pos, span_len, 1)
    my_pos = first_pos + jnp.arange(span_len, dtype=jnp.int32)
    token_count = row_count * span_len
    keep_flat = (my_segs < doc_count).astype(jnp.float32).reshape(token_count, 1)
    inputs = tokens_in.astype(jnp.float32).reshape(token_count, model_width)
    normed = layer_norm(inputs, ln1_gain, ln1_bias)
    normed_low = normed.astype(jnp.bfloat16)
    bias_full = jnp.concatenate(
        [qv_bias[:model_width], jnp.zeros((model_width,), jnp.float32), qv_bias[model_width:]]
    )
    projected = (
        jnp.dot(normed_low, qkv_weight, preferred_element_type=jnp.float32) + bias_full
    ).astype(jnp.bfloat16)
    projected = projected.reshape(row_count, span_len, 3 * model_width)
    queries = projected[..., :model_width]
    keys = projected[..., model_width : 2 * model_width]
    values = projected[..., 2 * model_width :]
    query_heads = queries.reshape(row_count, span_len, head_count, HEAD)
    key_heads = keys.reshape(row_count, span_len, head_count, HEAD)
    value_heads = values.reshape(row_count, span_len, head_count, HEAD)
    last_pos = first_pos + span_len - 1
    start_state = (
        jnp.full((row_count, head_count, span_len), masked_value, jnp.float32),
        jnp.zeros((row_count, head_count, span_len), jnp.float32),
        jnp.zeros((row_count, span_len, model_width), jnp.float32),
    )
    key_piece = lax.all_gather(keys, "seq", axis=1, tiled=True)
    value_piece = lax.all_gather(values, "seq", axis=1, tiled=True)
    count = key_piece.shape[1]

    def forward_update(state):
        top, total, accum = state
        piece_keys = key_piece.reshape(row_count, count, head_count, HEAD)
        piece_values = value_piece.reshape(row_count, count, head_count, HEAD)
        scores = (
            jnp.einsum(
                "rqhd,rkhd->rhqk", query_heads, piece_keys, preferred_element_type=jnp.float32
            )
            * scale
        )
        key_pos = jnp.arange(count, dtype=jnp.int32)
        allowed = allowed_mask(my_pos, my_segs, key_pos, segments)[:, None]
        scores = jnp.where(allowed, scores, masked_value)
        new_top = jnp.maximum(top, jnp.max(scores, axis=-1))
        weights = jnp.where(allowed, jnp.exp(scores - new_top[..., None]), 0.0)
        total = jnp.sum(weights, axis=-1)
        added = jnp.einsum(
            "rhqk,rkhd->rqhd",
            weights.astype(jnp.bfloat16),
            piece_values,
            preferred_element_type=jnp.float32,
        )
        accum = added.reshape(row_count, span_len, model_width)
        return (new_top, total, accum)

    top, total, accum = lax.cond(
        jnp.int32(0) > last_pos, lambda state: state, forward_update, start_state
    )
    log_total = top + jnp.log(total)
    attended_heads = (
        accum.reshape(row_count, span_len, head_count, HEAD) / total.transpose(0, 2, 1)[..., None]
    )
    attended = attended_heads.reshape(token_count, model_width)
    attended_low = attended.astype(jnp.bfloat16)
    attn_out = jnp.dot(attended_low, proj_weight, preferred_element_type=jnp.float32) + proj_bias
    middle = inputs + branch_scale * attn_out
    normed_two = layer_norm(middle, ln2_gain, ln2_bias)
    normed_two_low = normed_two.astype(jnp.bfloat16)
    hidden_pre = jnp.dot(normed_two_low, fc_weight, preferred_element_type=jnp.float32) + fc_bias
    hidden_low = gelu_tanh(hidden_pre).astype(jnp.bfloat16)
    branch_out = jnp.dot(hidden_low, out_weight, preferred_element_type=jnp.float32) + out_bias
    layer_out = (
        ((middle + branch_scale * branch_out) * keep_flat)
        .astype(jnp.bfloat16)
        .reshape(row_count, span_len, model_width)
    )
    grad_final = keep_flat * cotangent.astype(jnp.float32).reshape(token_count, model_width)
    grad_branch = (branch_scale * grad_final).astype(jnp.bfloat16)
    grad_out_weight = left_dot(hidden_low, grad_branch)
    grad_out_bias = jnp.sum(grad_branch.astype(jnp.float32), axis=0)
    grad_hidden = right_dot(grad_branch, out_weight)
    gelu_value, gelu_pull = jax.vjp(gelu_tanh, hidden_pre)
    grad_pre = gelu_pull(grad_hidden)[0].astype(jnp.bfloat16)
    grad_fc_weight = left_dot(normed_two_low, grad_pre)
    grad_fc_bias = jnp.sum(grad_pre.astype(jnp.float32), axis=0)
    grad_normed_two = right_dot(grad_pre, fc_weight)
    norm_value, norm_pull = jax.vjp(layer_norm, middle, ln2_gain, ln2_bias)
    grad_mid_norm, grad_ln2_gain, grad_ln2_bias = norm_pull(grad_normed_two)
    grad_middle = grad_final + grad_mid_norm
    grad_attn = (branch_scale * grad_middle).astype(jnp.bfloat16)
    grad_proj_weight = left_dot(attended_low, grad_attn)
    grad_proj_bias = jnp.sum(grad_attn.astype(jnp.float32), axis=0)
    grad_attended = (
        right_dot(grad_attn, proj_weight)
        .astype(jnp.bfloat16)
        .reshape(row_count, span_len, model_width)
    )
    grad_att_heads = grad_attended.reshape(row_count, span_len, head_count, HEAD)
    delta = jnp.sum(grad_att_heads.astype(jnp.float32) * attended_heads, axis=-1)
    delta_t = delta.transpose(0, 2, 1)
    zero_grad = jnp.zeros((row_count, span_len, model_width), jnp.float32)
    query_key_piece = lax.all_gather(keys, "seq", axis=1, tiled=True)
    query_value_piece = lax.all_gather(values, "seq", axis=1, tiled=True)
    query_count = query_key_piece.shape[1]

    def query_update(carry):
        piece_keys = query_key_piece.reshape(row_count, query_count, head_count, HEAD)
        piece_values = query_value_piece.reshape(row_count, query_count, head_count, HEAD)
        scores = (
            jnp.einsum(
                "rqhd,rkhd->rhqk", query_heads, piece_keys, preferred_element_type=jnp.float32
            )
            * scale
        )
        key_pos = jnp.arange(query_count, dtype=jnp.int32)
        allowed = allowed_mask(my_pos, my_segs, key_pos, segments)[:, None]
        probs = jnp.where(allowed, jnp.exp(scores - log_total[..., None]), 0.0)
        grad_probs = jnp.einsum(
            "rqhd,rkhd->rhqk", grad_att_heads, piece_values, preferred_element_type=jnp.float32
        )
        grad_scores = (probs * (grad_probs - delta_t[..., None])).astype(jnp.bfloat16)
        added = jnp.einsum(
            "rhqk,rkhd->rqhd", grad_scores, piece_keys, preferred_element_type=jnp.float32
        )
        return scale * added.reshape(row_count, span_len, model_width)

    grad_queries = lax.cond(jnp.int32(0) > last_pos, lambda carry: carry, query_update, zero_grad)
    stats_lse, stats_delta = (
        lax.all_gather(
            log_total.transpose(0, 2, 1).astype(jnp.bfloat16), "seq", axis=1, tiled=True
        ).astype(jnp.float32),
        lax.all_gather(delta.astype(jnp.bfloat16), "seq", axis=1, tiled=True).astype(delta.dtype),
    )
    query_piece_in = lax.all_gather(queries, "seq", axis=1, tiled=True)
    grad_piece_in = lax.all_gather(grad_attended, "seq", axis=1, tiled=True)
    key_count = query_piece_in.shape[1]

    def key_update(state):
        piece_queries = query_piece_in.reshape(row_count, key_count, head_count, HEAD)
        piece_grads = grad_piece_in.reshape(row_count, key_count, head_count, HEAD)
        scores = (
            jnp.einsum(
                "rqhd,rkhd->rhqk", piece_queries, key_heads, preferred_element_type=jnp.float32
            )
            * scale
        )
        query_pos = jnp.arange(key_count, dtype=jnp.int32)
        allowed = allowed_mask(query_pos, segments, my_pos, my_segs)[:, None]
        piece_lse = stats_lse.transpose(0, 2, 1)
        piece_delta = stats_delta.transpose(0, 2, 1)
        probs = jnp.where(allowed, jnp.exp(scores - piece_lse[..., None]), 0.0)
        add_v = jnp.einsum(
            "rhqk,rqhd->rkhd",
            probs.astype(jnp.bfloat16),
            piece_grads,
            preferred_element_type=jnp.float32,
        )
        grad_probs = jnp.einsum(
            "rqhd,rkhd->rhqk", piece_grads, value_heads, preferred_element_type=jnp.float32
        )
        grad_scores = (probs * (grad_probs - piece_delta[..., None])).astype(jnp.bfloat16)
        add_k = jnp.einsum(
            "rhqk,rqhd->rkhd", grad_scores, piece_queries, preferred_element_type=jnp.float32
        )
        return (
            scale * add_k.reshape(row_count, span_len, model_width),
            add_v.reshape(row_count, span_len, model_width),
        )

    grad_keys, grad_values = lax.cond(
        jnp.int32(0) + key_count <= first_pos,
        lambda state: state,
        key_update,
        (zero_grad, zero_grad),
    )
    grad_projected = (
        jnp.concatenate([grad_queries, grad_keys, grad_values], axis=-1)
        .astype(jnp.bfloat16)
        .reshape(token_count, 3 * model_width)
    )
    grad_qkv_weight = left_dot(normed_low, grad_projected)
    column_sums = jnp.sum(grad_projected.astype(jnp.float32), axis=0)
    grad_qv_bias = jnp.concatenate([column_sums[:model_width], column_sums[2 * model_width :]])
    grad_normed = right_dot(grad_projected, qkv_weight)
    first_value, first_pull = jax.vjp(layer_norm, inputs, ln1_gain, ln1_bias)
    grad_in_norm, grad_ln1_gain, grad_ln1_bias = first_pull(grad_normed)
    input_grad = (grad_middle + grad_in_norm).reshape(row_count, span_len, model_width)
    local_grads = (
        grad_ln1_gain,
        grad_ln1_bias,
        grad_qkv_weight,
        grad_qv_bias,
        grad_proj_weight,
        grad_proj_bias,
        grad_ln2_gain,
        grad_ln2_bias,
        grad_fc_weight,
        grad_fc_bias,
        grad_out_weight,
        grad_out_bias,
    )
    shares = (
        lax.psum_scatter(
            local_grads[0].astype(jnp.bfloat16), "row", scatter_dimension=0, tiled=True
        ).astype(jnp.float32),
        lax.psum_scatter(
            local_grads[1].astype(jnp.bfloat16), "row", scatter_dimension=0, tiled=True
        ).astype(jnp.float32),
        lax.psum_scatter(
            local_grads[2].astype(jnp.bfloat16), "row", scatter_dimension=0, tiled=True
        ).astype(jnp.float32),
        lax.psum_scatter(
            local_grads[3].astype(jnp.bfloat16), "row", scatter_dimension=0, tiled=True
        ).astype(jnp.float32),
        lax.psum_scatter(
            local_grads[4].astype(jnp.bfloat16), "row", scatter_dimension=0, tiled=True
        ).astype(jnp.float32),
        lax.psum_scatter(
            local_grads[5].astype(jnp.bfloat16), "row", scatter_dimension=0, tiled=True
        ).astype(jnp.float32),
        lax.psum_scatter(
            local_grads[6].astype(jnp.bfloat16), "row", scatter_dimension=0, tiled=True
        ).astype(jnp.float32),
        lax.psum_scatter(
            local_grads[7].astype(jnp.bfloat16), "row", scatter_dimension=0, tiled=True
        ).astype(jnp.float32),
        lax.psum_scatter(
            local_grads[8].astype(jnp.bfloat16), "row", scatter_dimension=0, tiled=True
        ).astype(jnp.float32),
        lax.psum_scatter(
            local_grads[9].astype(jnp.bfloat16), "row", scatter_dimension=0, tiled=True
        ).astype(jnp.float32),
        lax.psum_scatter(
            local_grads[10].astype(jnp.bfloat16), "row", scatter_dimension=0, tiled=True
        ).astype(jnp.float32),
        lax.psum_scatter(
            local_grads[11].astype(jnp.bfloat16), "row", scatter_dimension=0, tiled=True
        ).astype(jnp.float32),
    )
    totals = (
        lax.psum(shares[0].astype(jnp.bfloat16), "seq").astype(jnp.float32),
        lax.psum(shares[1].astype(jnp.bfloat16), "seq").astype(jnp.float32),
        lax.psum(shares[2].astype(jnp.bfloat16), "seq").astype(jnp.float32),
        lax.psum(shares[3].astype(jnp.bfloat16), "seq").astype(jnp.float32),
        lax.psum(shares[4].astype(jnp.bfloat16), "seq").astype(jnp.float32),
        lax.psum(shares[5].astype(jnp.bfloat16), "seq").astype(jnp.float32),
        lax.psum(shares[6].astype(jnp.bfloat16), "seq").astype(jnp.float32),
        lax.psum(shares[7].astype(jnp.bfloat16), "seq").astype(jnp.float32),
        lax.psum(shares[8].astype(jnp.bfloat16), "seq").astype(jnp.float32),
        lax.psum(shares[9].astype(jnp.bfloat16), "seq").astype(jnp.float32),
        lax.psum(shares[10].astype(jnp.bfloat16), "seq").astype(jnp.float32),
        lax.psum(shares[11].astype(jnp.bfloat16), "seq").astype(jnp.float32),
    )
    summed = (
        lax.all_gather(totals[0].astype(jnp.bfloat16), "row", axis=0, tiled=True).astype(
            jnp.float32
        ),
        lax.all_gather(totals[1].astype(jnp.bfloat16), "row", axis=0, tiled=True).astype(
            jnp.float32
        ),
        lax.all_gather(totals[2].astype(jnp.bfloat16), "row", axis=0, tiled=True).astype(
            jnp.float32
        ),
        lax.all_gather(totals[3].astype(jnp.bfloat16), "row", axis=0, tiled=True).astype(
            jnp.float32
        ),
        lax.all_gather(totals[4].astype(jnp.bfloat16), "row", axis=0, tiled=True).astype(
            jnp.float32
        ),
        lax.all_gather(totals[5].astype(jnp.bfloat16), "row", axis=0, tiled=True).astype(
            jnp.float32
        ),
        lax.all_gather(totals[6].astype(jnp.bfloat16), "row", axis=0, tiled=True).astype(
            jnp.float32
        ),
        lax.all_gather(totals[7].astype(jnp.bfloat16), "row", axis=0, tiled=True).astype(
            jnp.float32
        ),
        lax.all_gather(totals[8].astype(jnp.bfloat16), "row", axis=0, tiled=True).astype(
            jnp.float32
        ),
        lax.all_gather(totals[9].astype(jnp.bfloat16), "row", axis=0, tiled=True).astype(
            jnp.float32
        ),
        lax.all_gather(totals[10].astype(jnp.bfloat16), "row", axis=0, tiled=True).astype(
            jnp.float32
        ),
        lax.all_gather(totals[11].astype(jnp.bfloat16), "row", axis=0, tiled=True).astype(
            jnp.float32
        ),
    )
    return (
        layer_out,
        input_grad,
        summed[0],
        summed[1],
        summed[2],
        summed[3],
        summed[4],
        summed[5],
        summed[6],
        summed[7],
        summed[8],
        summed[9],
        summed[10],
        summed[11],
    )


def solution(mesh):
    in_specs = (
        P("row", "seq", None),
        P("row", None),
        P(),
        P(),
        P(),
        P(),
        P(),
        P(),
        P(),
        P(),
        P(),
        P(),
        P(),
        P(),
        P("row", "seq", None),
    )
    out_specs = (
        P("row", "seq", None),
        P("row", "seq", None),
        P(),
        P(),
        P(),
        P(),
        P(),
        P(),
        P(),
        P(),
        P(),
        P(),
        P(),
        P(),
    )
    return jax.shard_map(local, mesh=mesh, in_specs=in_specs, out_specs=out_specs, check_vma=False)
```

profile of v0, /device:TPU:0, one launch (start us, length us, event | category | flops | bytes accessed | tf_op | source)
XLA Modules:
  0.0 759.6 jit_solution(12803837758067459575)
XLA Ops:
  32.5 48.0 %all-gather.12.cloned.1.call-done = bf16[3,1024,768]{1,2,0:T(8,128)(2,1)} async-done(((bf16[3,256,768]{1,2,0:T(8,128)(2,1)}), bf16[3,1024,768]{1,2,0:T(8,128)(2,1)}) %all-gather.12.cloned.1.call-update) | async-done | bytes 4718608 | tf_op jit(solution)/shard_map/all_gather | solution.py:96
  80.5 59.4 %all-gather.10.cloned.1.call-done = bf16[3,1024,768]{1,2,0:T(8,128)(2,1)} async-done(((bf16[3,256,768]{1,2,0:T(8,128)(2,1)}), bf16[3,1024,768]{1,2,0:T(8,128)(2,1)}) %all-gather.10.cloned.1.call-update) | async-done | bytes 4718608 | tf_op jit(solution)/shard_map/all_gather | solution.py:95
  139.9 62.8 %conditional.3 = (f32[3,12,256]{2,1,0:T(8,128)}, f32[3,12,256]{2,1,0:T(8,128)S(1)}, f32[3,256,768]{1,2,0:T(8,128)}, f32[3,12,256]{2,1,0:T(8,128)S(1)}) conditional(s32[]{:T(128)} %convert_element_type.104, (s32[256]{0:T(256)}, s32[3,1024]{1,0:T(4,128)S(1)}, s32[3,256]{1,0:T(4,128)}, bf16[3,1024,768]{1,2,0:T(8,128)(2,1)}, ...), branch_computations={%region_4.7_spmd, %region_7.8_spmd} | conditional | flops 2540428288 | bytes 133349440 | solution.py:124
  142.9 19.1 %fusion = (f32[3,12,256]{2,1,0:T(8,128)}, f32[3,12,256,1024]{3,2,1,0:T(8,128)}) fusion(pred[3,256,1024]{2,1,0:T(8,128)(4,1)} %compare_and_fusion, bf16[3,256,12,64]{1,3,2,0:T(8,128)(2,1)} %get-tuple-element.60, bf16[3,1024,12,64]{1,3,2,0:T(8,128)(2,1)} %bitcast.138), kind=kOutput, calls=%fused_computation.2 | convolution fusion | flops 1236261888 | bytes 44470272 | tf_op jit(solution)/shard_map/cond/branch_0_fun/rqhd,rkhd->rhqk/dot_general | solution.py:104
  163.5 20.8 %fusion.3 = f32[3,12,256,64]{2,3,1,0:T(8,128)} fusion(bf16[3,1024,12,64]{1,3,2,0:T(8,128)(2,1)} %bitcast.164, f32[3,12,256,1024]{3,2,1,0:T(8,128)} %get-tuple-element.222, f32[3,12,256]{2,1,0:T(8,128)} %broadcast_maximum_fusion, pred[3,256,1024]{2,1,0:T(8,128)(4,1)} %compare_and_fusion), kind=kOutput, calls=%fused_computation.5 | convolution fusion | flops 1255145472 | bytes 45649920 | tf_op jit(solution)/shard_map/cond/branch_0_fun/rhqk,rkhd->rqhd/dot_general | solution.py:115
  184.3 18.3 %fusion.2 = f32[3,12,256]{2,1,0:T(8,128)S(1)} fusion(f32[3,12,256,1024]{3,2,1,0:T(8,128)} %get-tuple-element.222, f32[3,12,256]{2,1,0:T(8,128)} %broadcast_maximum_fusion, pred[3,256,1024]{2,1,0:T(8,128)(4,1)S(1)} %copy-done.9), kind=kLoop, calls=%fused_computation.4 | loop fusion | flops 47176704 | bytes 38608896 | tf_op jit(solution)/shard_map/cond/branch_0_fun/reduce_sum | solution.py:114
  226.3 12.1 %fusion.63 = (bf16[3072]{0:T(1024)(128)(2,1)}, bf16[768,3072]{1,0:T(8,128)(2,1)S(1)}) fusion(f32[768,3072]{1,0:T(8,128)} %fusion.61, f32[3072]{0:T(1024)S(1)} %copy-done.38, bf16[768,768]{1,0:T(8,128)(2,1)S(1)} %copy-done.12, bf16[3072,768]{1,0:T(8,128)(2,1)S(1)} %bitcast.163), kind=kOutput, calls=%fused_computation.114 | convolution fusion | flops 3675780096 | bytes 20072448 | tf_op jit(solution)/shard_map/dot_general | solution.py:31
  255.0 12.4 %convolution_convert_fusion.1 = bf16[3072,768]{1,0:T(8,128)(2,1)} fusion(bf16[768,768]{1,0:T(8,128)(2,1)} %multiply_convert_fusion.14, f32[768,3072]{1,0:T(8,128)} %fusion.61, f32[3072]{0:T(1024)} %param.32), kind=kOutput, calls=%fused_computation.54 | convolution fusion | flops 3649830912 | bytes 15347712 | tf_op jit(solution)/shard_map/dot_general | solution.py:25
  280.9 10.2 %all_gather.59 = bf16[3,1024,12]{1,2,0:T(8,128)(2,1)S(1)} all-gather(bf16[3,256,12]{1,2,0:T(8,128)(2,1)S(1)} %get-tuple-element.217), channel_id=1, replica_groups=mesh['row'=8,'seq'=4] {'seq'}, dimensions={1}, use_global_device_ids=true | all-gather | bytes 92160 | tf_op jit(solution)/shard_map/all_gather | solution.py:197
  309.1 46.8 %conditional.4 = (bf16[768,768]{0,1:T(8,128)(2,1)}) conditional(s32[]{:T(128)} %convert_element_type.104, (s32[256]{0:T(256)S(1)}, s32[3,1024]{1,0:T(4,128)S(1)}, s32[3,256]{1,0:T(4,128)S(1)}, bf16[3,1024,768]{1,2,0:T(8,128)(2,1)}, bf16[3,256,12,64]{1,3,2,0:T(8,128)(2,1)S(1)}, /*index=5*/f32[3,12,256]{2,1,0:T(8,128)}, ...), branch_computations={%region_13.14_spmd, %region_14.15_spmd} | conditional | flops 3683516416 | bytes 100171784 | solution.py:195
  311.4 17.5 %fusion.72 = f32[3,12,256,1024]{3,2,1,0:T(8,128)} fusion(bf16[3,256,12,64]{1,3,2,0:T(8,128)(2,1)S(1)} %get-tuple-element.66, bf16[3,1024,12,64]{1,3,2,0:T(8,128)(2,1)} %bitcast.139), kind=kOutput, calls=%fused_computation.122 | convolution fusion | flops 1207959552 | bytes 43646976 | tf_op jit(solution)/shard_map/cond/branch_0_fun/rqhd,rkhd->rhqk/dot_general | solution.py:178
  328.9 23.3 %multiply_bitcast_fusion = bf16[3,256,12,64]{1,3,2,0:T(8,128)(2,1)} fusion(bf16[3,1024,12,64]{1,3,2,0:T(8,128)(2,1)} %bitcast.140, f32[3,12,256,1024]{3,2,1,0:T(8,128)} %fusion.72, f32[3,12,256]{2,1,0:T(8,128)} %copy.79, f32[3,12,256]{2,1,0:T(8,128)} %get-tuple-element.68, pred[3,256,1024]{2,1,0:T(8,128)(4,1)} %compare_and_fusion.1, ...), kind=kOutput, calls=%fused_computation.18 | convolution fusion | flops 2473721856 | bytes 50405376 | tf_op jit(solution)/shard_map/cond/branch_0_fun/rhqk,rkhd->rqhd/dot_general | solution.py:190
  355.9 65.6 %conditional.5 = (bf16[768,768]{0,1:T(8,128)(2,1)}, bf16[768,768]{0,1:T(8,128)(2,1)}) conditional(s32[]{:T(128)} %convert_element_type.218, (s32[256]{0:T(256)}, s32[3,256]{1,0:T(4,128)}, s32[3,1024]{1,0:T(4,128)S(1)}, bf16[3,1024,768]{1,2,0:T(8,128)(2,1)}, bf16[3,256,768]{1,2,0:T(8,128)(2,1)}, /*index=5*/f32[3,1024,12]{1,2,0:T(8,128)}, ...), branch_computations={%region_15.16_spmd, %region_16.17_spmd} | conditional | flops 4929814528 | bytes 159350864 | solution.py:238
  360.7 16.9 %fusion.73 = f32[3,12,1024,256]{3,2,1,0:T(8,128)} fusion(bf16[3,1024,12,64]{1,3,2,0:T(8,128)(2,1)} %bitcast.149, bf16[3,256,12,64]{1,3,2,0:T(8,128)(2,1)S(1)} %bitcast.142), kind=kOutput, calls=%fused_computation.123 | convolution fusion | flops 1207959552 | bytes 43646976 | tf_op jit(solution)/shard_map/cond/branch_0_fun/rqhd,rkhd->rhqk/dot_general | solution.py:210
  377.5 22.9 %fusion.31 = bf16[3,256,12,64]{1,3,2,0:T(8,128)(2,1)} fusion(bf16[3,1024,12,64]{1,3,2,0:T(8,128)(2,1)} %bitcast.150, f32[3,12,1024,256]{3,2,1,0:T(8,128)} %fusion.73, f32[3,12,1024]{2,1,0:T(8,128)} %bitcast.158, f32[3,12,1024]{2,1,0:T(8,128)} %bitcast.156, pred[3,1024,256]{2,1,0:T(8,128)(4,1)} %compare_and_fusion.2, ...), kind=kOutput, calls=%fused_computation.35 | convolution fusion | flops 2473721856 | bytes 50626560 | tf_op jit(solution)/shard_map/cond/branch_0_fun/rhqk,rqhd->rkhd/dot_general | solution.py:230
  400.4 16.4 %fusion.28 = bf16[3,256,12,64]{1,3,2,0:T(8,128)(2,1)S(1)} fusion(bf16[3,1024,12,64]{1,3,2,0:T(8,128)(2,1)} %bitcast.167, f32[3,12,1024,256]{3,2,1,0:T(8,128)} %fusion.73, f32[3,12,1024]{2,1,0:T(8,128)} %bitcast.157, pred[3,1024,256]{2,1,0:T(8,128)(4,1)} %compare_and_fusion.2), kind=kOutput, calls=%fused_computation.34 | convolution fusion | flops 1246298112 | bytes 44580864 | tf_op jit(solution)/shard_map/cond/branch_0_fun/rhqk,rqhd->rkhd/dot_general | solution.py:220
  428.7 28.2 %reduce-scatter.9.cloned.1.call-done = bf16[96,3072]{1,0:T(8,128)(2,1)} async-done(((bf16[768,3072]{1,0:T(8,128)(2,1)}), bf16[96,3072]{1,0:T(8,128)(2,1)}) %reduce-scatter.9.cloned.1.call-update) | async-done | bytes 589840 | tf_op jit(solution)/shard_map/reduce_scatter | solution.py:295
  456.9 45.1 %reduce-scatter.5.cloned.1.call-done = bf16[96,2304]{1,0:T(8,128)(2,1)} async-done(((bf16[768,2304]{1,0:T(8,128)(2,1)}), bf16[96,2304]{1,0:T(8,128)(2,1)}) %reduce-scatter.5.cloned.1.call-update) | async-done | bytes 442384 | tf_op jit(solution)/shard_map/reduce_scatter | solution.py:277
  502.1 67.1 %all-reduce.21.cloned.1.call-done = (bf16[96,2304]{1,0:T(8,128)(2,1)}, bf16[96,768]{1,0:T(8,128)(2,1)}, bf16[96,3072]{1,0:T(8,128)(2,1)}, bf16[384,768]{1,0:T(8,128)(2,1)}) async-done(((bf16[96,2304]{1,0:T(8,128)(2,1)}, bf16[96,768]{1,0:T(8,128)(2,1)}, bf16[96,3072]{1,0:T(8,128)(2,1)}, bf16[384,768]{1,0:T(8,128)(2,1)}), (bf16[96,2304]{1,0:T(8,128)(2,1)}, bf16[96,768]{1,0:T(8,128)(2,1)}, ...) | async-done | bytes 1769488 | tf_op jit(solution)/shard_map/psum | solution.py:311
  577.3 11.4 %multiply_convert_fusion.15 = bf16[768,768]{1,0:T(8,128)(2,1)} fusion(f32[768,768]{1,0:T(8,128)} %copy-done.7, bf16[3072,768]{1,0:T(8,128)(2,1)} %param.33, f32[768]{0:T(1024)S(1)} %copy-done.22, f32[768]{0:T(1024)S(1)} %copy-done.41, f32[768,3072]{1,0:T(8,128)} %fusion.61, f32[3072]{0:T(1024)} %param.32), kind=kOutput, calls=%fused_computation.86 | convolution fusion | flops 3650420736 | bytes 17713152 | tf_op jit(solution)/shard_map/dot_general | solution.py:139
  599.1 30.6 %all-reduce.16 = (bf16[768]{0:T(1024)(128)(2,1)}, bf16[768]{0:T(1024)(128)(2,1)}, bf16[1536]{0:T(1024)(128)(2,1)}, bf16[768]{0:T(1024)(128)(2,1)}, bf16[768]{0:T...) all-reduce(bf16[768]{0:T(1024)(128)(2,1)} %get-tuple-element.180, ...), channel_id=2, replica_groups=mesh['row'=8,'seq'=4] {'row'}, use_global_device_ids=true, to_apply=%region_20.21.clone | all-reduce | flops 6144 | bytes 24576
  638.5 9.6 %all-reduce.17 = (bf16[96]{0:T(256)(128)(2,1)}, bf16[96]{0:T(256)(128)(2,1)}, bf16[192]{0:T(256)(128)(2,1)}, bf16[96]{0:T(256)(128)(2,1)}, bf16[96]{0:T(256)(128...) all-reduce(bf16[96]{0:T(256)(128)(2,1)} %dynamic-slice.8, ...), channel_id=1, replica_groups=mesh['row'=8,'seq'=4] {'seq'}, use_global_device_ids=true, to_apply=%region_21.22 | all-reduce | flops 768 | bytes 3072 | tf_op jit(solution)/shard_map/psum | solution.py:309
  661.7 28.1 %all-reduce.15 = (bf16[768]{0:T(1024)(128)(2,1)}, bf16[768]{0:T(1024)(128)(2,1)}, bf16[1536]{0:T(1024)(128)(2,1)}, bf16[768]{0:T(1024)(128)(2,1)}, bf16[768]{0:T...) all-reduce(bf16[768]{0:T(1024)(128)(2,1)} %dynamic-update-slice, ...), channel_id=1, replica_groups=mesh['row'=8,'seq'=4] {'row'}, use_global_device_ids=true, to_apply=%add | all-reduce | flops 9216 | bytes 36864
  710.2 12.9 %all-gather = bf16[8,1,384]{2,1,0:T(2,128)(2,1)S(1)} all-gather(bf16[1,1,384]{2,1,0:T(2,128)(2,1)S(1)} %reshape.324), channel_id=1, replica_groups=mesh['row'=8,'seq'=4] {'row'}, dimensions={0}, use_global_device_ids=true | all-gather | bytes 6912 | tf_op jit(solution)/shard_map/all_gather | solution.py:350
  (243 shorter events, 211.3 us)
Async XLA Ops:
  7.2 73.3 %all-gather.12.cloned.1.call-start = ((), (), s32[]{:S(2)}) async-start(), calls=%async_computation.5 | async-start | bytes 5898240 | tf_op jit(solution)/shard_map/all_gather | solution.py:96
  20.7 119.1 %all-gather.10.cloned.1.call-start = ((), (), s32[]{:S(2)}) async-start(), calls=%async_computation.4 | async-start | bytes 5898240 | tf_op jit(solution)/shard_map/all_gather | solution.py:95
  23.2 332.7 %all-gather.14.cloned.1.call-start = ((), (), s32[]{:S(2)}) async-start(), calls=%async_computation.6 | async-start | bytes 5898240 | tf_op jit(solution)/shard_map/all_gather | solution.py:202
  25.7 330.2 %all-gather.16.cloned.1.call-start = ((), (), s32[]{:S(2)}) async-start(), calls=%async_computation.7 | async-start | bytes 5898240 | tf_op jit(solution)/shard_map/all_gather | solution.py:203
  163.5 20.8 %copy-start.9 = (pred[3,256,1024]{2,1,0:T(8,128)(4,1)S(1)}, pred[3,256,1024]{2,1,0:T(8,128)(4,1)}, u32[]{:S(2)}) copy-start(pred[3,256,1024]{2,1,0:T(8,128)(4,1)} %compare_and_fusion) | copy-start | bytes 2359300 | tf_op jit(solution)/shard_map/cond
  218.6 24.7 %copy-start.7 = (f32[768,768]{1,0:T(8,128)}, f32[768,768]{1,0:T(8,128)S(1)}, u32[]{:S(2)}) copy-start(f32[768,768]{1,0:T(8,128)S(1)} %get-tuple-element.233) | copy-start | bytes 7077892
  218.6 24.6 %copy-start.28 = (f32[768]{0:T(1024)}, f32[768]{0:T(1024)S(1)}, u32[]{:S(2)}) copy-start(f32[768]{0:T(1024)S(1)} %broadcast_multiply_fusion) | copy-start | bytes 9220
  219.4 23.9 %copy-start.32 = (f32[768]{0:T(1024)}, f32[768]{0:T(1024)S(1)}, u32[]{:S(2)}) copy-start(f32[768]{0:T(1024)S(1)} %fusion.57) | copy-start | bytes 9220
  250.9 177.8 %reduce-scatter.7.cloned.1.call-start = ((), (), s32[]{:S(2)}) async-start(), calls=%async_computation.10 | async-start | bytes 1327104 | tf_op jit(solution)/shard_map/reduce_scatter | solution.py:283
  254.8 173.9 %reduce-scatter.11.cloned.1.call-start = ((), (), s32[]{:S(2)}) async-start(), calls=%async_computation.14 | async-start | bytes 5308416 | tf_op jit(solution)/shard_map/reduce_scatter | solution.py:301
  267.4 189.5 %reduce-scatter.9.cloned.1.call-start = ((), (), s32[]{:S(2)}) async-start(), calls=%async_computation.12 | async-start | bytes 5308416 | tf_op jit(solution)/shard_map/reduce_scatter | solution.py:295
  277.0 225.0 %reduce-scatter.5.cloned.1.call-start = ((), (), s32[]{:S(2)}) async-start(), calls=%async_computation.8 | async-start | bytes 3981312 | tf_op jit(solution)/shard_map/reduce_scatter | solution.py:277
  295.5 13.6 %copy-start.4 = (bf16[3,256,768]{1,2,0:T(8,128)(2,1)S(1)}, bf16[3,256,768]{1,2,0:T(8,128)(2,1)}, u32[]{:S(2)}) copy-start(bf16[3,256,768]{1,2,0:T(8,128)(2,1)} %copy.83) | copy-start | bytes 3538948
  295.5 13.6 %copy-start.23 = (s32[3,256]{1,0:T(4,128)S(1)}, s32[3,256]{1,0:T(4,128)}, u32[]{:S(2)}) copy-start(s32[3,256]{1,0:T(4,128)} %get-tuple-element.220) | copy-start | bytes 9220
  295.5 13.6 %copy-start.33 = (s32[256]{0:T(256)S(1)}, s32[256]{0:T(256)}, u32[]{:S(2)}) copy-start(s32[256]{0:T(256)} %iota_add_fusion) | copy-start | bytes 3076
  428.6 142.6 %copy-start.35 = (u32[32]{0:T(128)S(1)}, u32[32]{0:T(128)}, u32[]{:S(2)}) copy-start(u32[32]{0:T(128)} %constant.91) | copy-start | bytes 388
  428.6 146.5 %copy-start.29 = (f32[3,256]{1,0:T(4,128)S(1)}, f32[3,256]{1,0:T(4,128)}, u32[]{:S(2)}) copy-start(f32[3,256]{1,0:T(4,128)} %get-tuple-element.219) | copy-start | bytes 9220
  428.6 140.5 %all-reduce.21.cloned.1.call-start = ((), (), s32[]{:S(2)}) async-start(), calls=%async_computation.16 | async-start | bytes 3538944 | tf_op jit(solution)/shard_map/psum | solution.py:311
  502.0 75.3 %copy-start.22 = (f32[768]{0:T(1024)S(1)}, f32[768]{0:T(1024)}, u32[]{:S(2)}) copy-start(f32[768]{0:T(1024)} %mul.258) | copy-start | bytes 9220
  502.0 75.3 %copy-start.41 = (f32[768]{0:T(1024)S(1)}, f32[768]{0:T(1024)}, u32[]{:S(2)}) copy-start(f32[768]{0:T(1024)} %param.34) | copy-start | bytes 9220
  502.0 228.3 %all-gather.20.cloned.1.call-start = ((), (), s32[]{:S(2)}) async-start(), calls=%async_computation.11 | async-start | bytes 1327104 | tf_op jit(solution)/shard_map/all_gather | solution.py:335
  569.2 164.0 %all-gather.18.cloned.1.call-start = ((), (), s32[]{:S(2)}) async-start(), calls=%async_computation.9 | async-start | bytes 3981312 | tf_op jit(solution)/shard_map/all_gather | solution.py:329
  569.9 168.7 %all-gather.24.cloned.1.call-start = ((), (), s32[]{:S(2)}) async-start(), calls=%async_computation.15 | async-start | bytes 5308416 | tf_op jit(solution)/shard_map/all_gather | solution.py:353
  570.5 175.0 %all-gather.22.cloned.1.call-start = ((), (), s32[]{:S(2)}) async-start(), calls=%async_computation.13 | async-start | bytes 5308416 | tf_op jit(solution)/shard_map/all_gather | solution.py:347
  (36 other events, 140.2 us)
Sparse Core Ops, SparseCore 0:
  20.9 59.6 all-gather.11
  82.9 56.9 all-gather.9
  141.7 56.9 all-gather.13
  251.0 59.2 all-gather.15
  312.4 32.6 reduce-scatter.6
  347.3 53.2 reduce-scatter.10
  403.5 53.3 reduce-scatter.8
  459.8 42.1 reduce-scatter.4
  505.8 63.2 all-reduce.20
  570.7 22.6 all-gather.19
  595.2 41.8 all-gather.17
  638.6 50.9 all-gather.23
  691.3 50.6 all-gather.21
where the time goes:
time: 766 us; the launch traced here: 760 us
  waiting for transfers between devices  250 us (33%)
  matrix products  219 us (29%)
  blocking collectives  109 us (14%)
  other arithmetic  96.3 us (13%)
  local copies, waits for them, and re-layouts  66.6 us (9%)
  between operations  18 us (2%)
    psum x1, waiting for transfers between devices, local(): lax.psum(shares[2].astype(jnp.bfloat16), 'seq').astype(jnp.float32)  67.1 us
    all_gather x1, waiting for transfers between devices, local(): key_piece = lax.all_gather(keys, 'seq', axis=1, tiled=True)  59.4 us
    unnamed x2, blocking collectives  58.6 us
    all_gather x1, waiting for transfers between devices, local(): value_piece = lax.all_gather(values, 'seq', axis=1, tiled=True)  48 us
    reduce_scatter x1, waiting for transfers between devices, local(): lax.psum_scatter(local_grads[2].astype(jnp.bfloat16), 'row', scatter_dime...  45.1 us
    unnamed x116, local copies, waits for them, and re-layouts  35.6 us
    dot_general x4, matrix products, left_dot(): lax.dot_general(left, right, (((0,), (0,)), ((), ())), preferred_element_...  32.9 us
    reduce_scatter x1, waiting for transfers between devices, local(): lax.psum_scatter(local_grads[8].astype(jnp.bfloat16), 'row', scatter_dime...  28.2 us
  transfers between devices with their start and end apart: 13, of which 5 were waited for; matrix products, arithmetic and copies ran while one was open for 47% of the time, Pallas kernels for 0%

commit v1 on v0

--- a/solution.py
+++ b/solution.py
@@ -1,14 +1,851 @@
+import functools
+
 import jax
 import jax.numpy as jnp
 from jax import lax
+from jax.experimental import pallas as pl
+from jax.experimental.pallas import tpu as pltpu
 from jax.sharding import PartitionSpec as P
 
 HEAD = 64
-
-
 branch_scale = 12.0 ** (-0.5)
 masked_value = -1e30
 norm_eps = 1e-05
+F32, BF16 = jnp.float32, jnp.bfloat16
+VMEM_LIMIT = 60 * 1024 * 1024
+
+
+MESH = pl.DeviceIdType.MESH
+
+
+class Place:
+    def __init__(self):
+        row, seq = lax.axis_index("row"), lax.axis_index("seq")
+        self.row, self.seq = row, seq
+        self.core, self.z = lax.rem(row, 2), lax.div(row, 2)
+        self.x, self.y = lax.rem(seq, 2), lax.div(seq, 2)
+        self.sibling = (row + 1 - 2 * self.core, seq)
+        self.across_x = (row, seq + 1 - 2 * self.x)
+        self.across_y = (row, seq + 2 - 4 * self.y)
+        step_x, step_y = 1 - 2 * self.x, 2 - 4 * self.y
+        self.first_bit = self.x + self.core * (self.y - self.x)
+        self.second_bit = self.y + self.core * (self.x - self.y)
+        self.first = (row, seq + step_x + self.core * (step_y - step_x))
+        self.second = (row, seq + step_y + self.core * (step_x - step_y))
+
+        own = seq + self.core * (3 - 2 * seq)
+        self.active = own < 3
+        self.my_row = jnp.minimum(own, 2)
+
+    def in_plane(self, hop):
+        across_x, across_y = hop % 2, hop // 2
+        x = self.x + across_x * (1 - 2 * self.x)
+        y = self.y + across_y * (1 - 2 * self.y)
+        seq = 2 * y + x
+        return (self.row, seq), seq + self.core * (3 - 2 * seq)
+
+    def greet_plane(self):
+        barrier = pltpu.get_barrier_semaphore()
+        for hop in (1, 2, 3):
+            pl.semaphore_signal(barrier, inc=1, device_id=self.in_plane(hop)[0], device_id_type=MESH)
+        pl.semaphore_wait(barrier, 3)
+
+    def along_z(self, hop):
+        return (2 * lax.rem(self.z + hop, 4) + self.core, self.seq)
+
+    def greet(self):
+        barrier = pltpu.get_barrier_semaphore()
+        others = [self.sibling, self.across_x, self.across_y] + [self.along_z(hop) for hop in (1, 2, 3)]
+        for other in others:
+            pl.semaphore_signal(barrier, inc=1, device_id=other, device_id_type=MESH)
+        pl.semaphore_wait(barrier, len(others))
+
+
+def send(source, target, send_sem, recv_sem, device):
+    return pltpu.make_async_remote_copy(
+        src_ref=source, dst_ref=target, send_sem=send_sem, recv_sem=recv_sem,
+        device_id=device, device_id_type=MESH,
+    )
+
+
+class Reducer:
+    def __init__(self, place, work, recv0, recv1, recv2, recv3, part, out, send_sem, recv_sem, copy_sem):
+        self.place, self.work, self.out, self.part = place, work, out, part
+        self.recv = (recv0, recv1, recv2, recv3)
+        self.send_sem, self.recv_sem, self.copy_sem = send_sem, recv_sem, copy_sem
+        rows = work.shape[2]
+        self.size = (rows // 2, rows // 4, rows // 8, rows // 16)
+        half, quarter, eighth, piece = self.size
+        self.own0 = place.core * half
+        self.own1 = self.own0 + place.first_bit * quarter
+        self.own2 = self.own1 + place.second_bit * eighth
+        self.away0 = (1 - place.core) * half
+        self.away1 = self.own0 + (1 - place.first_bit) * quarter
+        self.away2 = self.own1 + (1 - place.second_bit) * eighth
+
+    def rows(self, start, size):
+        return pl.ds(pl.multiple_of(start, self.size[3]), size)
+
+    def piece(self, z):
+        return lax.div(z, 2), self.rows(self.own2 + lax.rem(z, 2) * self.size[3], self.size[3])
+
+    def copies(self, phase, u):
+        place, work, out, size = self.place, self.work, self.out, self.size
+        sems = lambda slot: (self.send_sem.at[u, slot], self.recv_sem.at[u, slot])
+        if phase == 0:
+            return [send(work.at[u, :, self.rows(self.away0, size[0])], self.recv[0].at[u], *sems(0), place.sibling)]
+        if phase == 1:
+            return [send(work.at[u, :, self.rows(self.away1, size[1])], self.recv[1].at[u], *sems(1), place.first)]
+        if phase == 2:
+            return [send(work.at[u, :, self.rows(self.away2, size[2])], self.recv[2].at[u], *sems(2), place.second)]
+        if phase == 3:
+            made = []
+            for hop in (1, 2, 3):
+                panel, rows = self.piece(lax.rem(place.z + hop, 4))
+                made.append(send(work.at[u, panel, rows], self.recv[3].at[u, hop - 1], *sems(2 + hop), place.along_z(hop)))
+            return made
+        if phase == 4:
+            panel, rows = self.piece(place.z)
+            return [
+                send(self.part.at[u], out.at[u, panel, rows], *sems(5 + hop), place.along_z(hop)) for hop in (1, 2, 3)
+            ]
+        start, count, other = {
+            5: (self.own2, size[2], place.second),
+            6: (self.own1, size[1], place.first),
+            7: (self.own0, size[0], place.sibling),
+        }[phase]
+        rows = self.rows(start, count)
+        return [send(out.at[u, :, rows], out.at[u, :, rows], *sems(4 + phase), other)]
+
+    def local(self, u):
+        panel, rows = self.piece(self.place.z)
+        return pltpu.make_async_copy(self.part.at[u], self.out.at[u, panel, rows], self.copy_sem.at[u])
+
+    def start(self, phase, u):
+        for copy in self.copies(phase, u):
+            copy.start()
+        if phase == 4:
+            self.local(u).start()
+
+    def wait(self, phase, u):
+        for copy in self.copies(phase, u):
+            copy.wait()
+        if phase == 4:
+            self.local(u).wait()
+
+    def add(self, target, source, u, start, count):
+        step = self.size[3]
+
+        def one(i, carry):
+            here = self.rows(start + i * step, step)
+            there = pl.ds(pl.multiple_of(i * step, step), step)
+            for panel in range(2):
+                total = target[u, panel, here, :].astype(F32) + source[u, panel, there, :].astype(F32)
+                target[u, panel, here, :] = total.astype(BF16)
+            return carry
+
+        lax.fori_loop(0, count // step, one, 0)
+
+    def step(self, phase, u):
+        if phase > 0:
+            self.wait(phase - 1, u)
+        if phase == 1:
+            self.add(self.work, self.recv[0], u, self.own0, self.size[0])
+        elif phase == 2:
+            self.add(self.work, self.recv[1], u, self.own1, self.size[1])
+        elif phase == 3:
+            self.add(self.work, self.recv[2], u, self.own2, self.size[2])
+        elif phase == 4:
+            panel, rows = self.piece(self.place.z)
+            total = self.work[u, panel, rows, :].astype(F32)
+            for hop in range(3):
+                total = total + self.recv[3][u, hop].astype(F32)
+            self.part[u] = total.astype(BF16)
+        if phase < 8:
+            self.start(phase, u)
+
+
+class SmallReducer:
+    def __init__(self, place, sums, recv, line, send_sem, recv_sem):
+        self.place, self.sums, self.recv, self.line = place, sums, recv, line
+        self.send_sem, self.recv_sem = send_sem, recv_sem
+
+    def copies(self, phase):
+        place = self.place
+        if phase < 3:
+            other = (place.sibling, place.across_x, place.across_y)[phase]
+            return [send(self.sums.at[phase], self.recv.at[phase], self.send_sem.at[phase], self.recv_sem.at[phase], other)]
+        return [
+            send(self.sums.at[3], self.line.at[place.z], self.send_sem.at[2 + hop], self.recv_sem.at[2 + hop], place.along_z(hop))
+            for hop in (1, 2, 3)
+        ]
+
+    def step(self, phase):
+        if phase > 0:
+            for copy in self.copies(phase - 1):
+                copy.wait()
+        if 0 < phase < 4:
+            self.sums[phase] = self.sums[phase - 1] + self.recv[phase - 1]
+        if phase < 4:
+            for copy in self.copies(phase):
+                copy.start()
+        if phase == 3:
+            self.line[self.place.z] = self.sums[3]
+
+    def total(self):
+        return (self.line[0] + self.line[1]) + (self.line[2] + self.line[3])
+
+
+def dot_nn(left, right):
+    return lax.dot_general(left, right, (((1,), (0,)), ((), ())), preferred_element_type=F32)
+
+
+def dot_nt(left, right):
+    return lax.dot_general(left, right, (((1,), (1,)), ((), ())), preferred_element_type=F32)
+
+
+def dot_tn(left, right):
+    return lax.dot_general(left, right, (((0,), (0,)), ((), ())), preferred_element_type=F32)
+
+
+def row_mean(values):
+    return jnp.mean(values, axis=-1, keepdims=True)
+
+
+def normalise(values):
+    center = values - row_mean(values)
+    inverse = lax.rsqrt(row_mean(center * center) + norm_eps)
+    return center * inverse, inverse
+
+
+def fill_bias(lens_ref, row, bias_ref, block):
+    tokens = bias_ref.shape[0]
+    ends, total = [], jnp.int32(0)
+    for j in range(lens_ref.shape[1]):
+        total = total + lens_ref[row, j]
+        ends.append(total)
+    query_pos = lax.broadcasted_iota(jnp.int32, (1, tokens), 1)
+    query_seg = jnp.zeros((1, tokens), jnp.int32)
+    for end in ends:
+        query_seg = query_seg + (query_pos >= end).astype(jnp.int32)
+
+    def one(i, carry):
+        start = pl.multiple_of(i * block, block)
+        key_pos = start + lax.broadcasted_iota(jnp.int32, (block, 1), 0)
+        key_seg = jnp.zeros((block, 1), jnp.int32)
+        for end in ends:
+            key_seg = key_seg + (key_pos >= end).astype(jnp.int32)
+        allowed = (key_pos <= query_pos) & (key_seg == query_seg)
+        bias_ref[pl.ds(start, block), :] = jnp.where(allowed, 0.0, masked_value)
+        return carry
+
+    lax.fori_loop(0, tokens // block, one, 0)
+
+
+def keep_column(lens_ref, row, start, block):
+    total = jnp.int32(0)
+    for j in range(lens_ref.shape[1]):
+        total = total + lens_ref[row, j]
+    pos = start + lax.broadcasted_iota(jnp.int32, (block, 1), 0)
+    return (pos < total).astype(F32)
+
+
+def head_row(h, value):
+    lane = lax.broadcasted_iota(jnp.int32, (1, 2 * HEAD), 1)
+    low = h % 2 * HEAD
+    return jnp.where((lane >= low) & (lane < low + HEAD), value, 0.0).astype(BF16)
+
+
+def front_kernel(
+    lens_ref, tokens_ref, cot_in_ref, gain_ref, shift_ref, wq_ref, wk_ref, wv_ref, bq_ref, bv_ref,
+    q_ref, k_ref, v_ref, o_ref, lse_ref, x_ref, cot_ref,
+    arrived, normed, bias, value_t, out_t, send_sem, recv_sem, copy_sem,
+):
+    tokens, width = x_ref.shape
+    lanes = wq_ref.shape[1]
+    block = tokens_ref.shape[1]
+    blocks = tokens // block
+    place = Place()
+    mine = pl.ds(place.seq, 1)
+    sources, targets = (tokens_ref, cot_in_ref), (arrived, cot_ref)
+
+    def outgoing(which, hop):
+        other, row = place.in_plane(hop)
+        return row, send(
+            sources[which].at[jnp.minimum(row, 2)], targets[which].at[place.seq],
+            send_sem.at[which, hop - 1], recv_sem.at[which, hop - 1], other,
+        )
+
+    def local(which):
+        return pltpu.make_async_copy(
+            sources[which].at[place.my_row], targets[which].at[place.seq], copy_sem.at[which]
+        )
+
+    def start(which):
+        for hop in (1, 2, 3):
+            row, copy = outgoing(which, hop)
+            pl.when(row < 3)(copy.start)
+        pl.when(place.active)(local(which).start)
+
+    def finish(which):
+        for hop in (1, 2, 3):
+            row, copy = outgoing(which, hop)
+            pl.when(row < 3)(copy.wait_send)
+            pl.when(place.active)(copy.wait_recv)
+        pl.when(place.active)(local(which).wait)
+
+    @pl.when(pl.program_id(0) == 0)
+    def _():
+        place.greet_plane()
+        start(0)
+        start(1)
+        fill_bias(lens_ref, place.my_row, bias, block)
+
+        @pl.when(jnp.logical_not(place.active))
+        def _():
+            arrived[...] = jnp.zeros_like(arrived)
+
+        finish(0)
+
+        def one(i, carry):
+            rows = pl.ds(pl.multiple_of(i * block, block), block)
+            x = arrived[i]
+            x_ref[rows, :] = x
+            unit, _ = normalise(x.astype(F32))
+            normed[rows, :] = (unit * gain_ref[...] + shift_ref[...]).astype(BF16)
+            return carry
+
+        lax.fori_loop(0, blocks, one, 0)
+
+    def project(i, carry):
+        rows = pl.ds(pl.multiple_of(i * block, block), block)
+        h1 = normed[rows, :]
+        q_ref[rows, :] = (dot_nn(h1, wq_ref[...]) + bq_ref[...]).astype(BF16)
+        k_ref[rows, :] = dot_nn(h1, wk_ref[...]).astype(BF16)
+        values = dot_nn(h1, wv_ref[...]) + bv_ref[...]
+        v_ref[rows, :] = values.astype(BF16)
+        value_t[:, rows] = values.T.astype(BF16)
+        return carry
+
+    lax.fori_loop(0, blocks, project, 0)
+
+    for i in range(blocks):
+        rows = slice(i * block, (i + 1) * block)
+        count = (i + 1) * block
+        for h in range(lanes // HEAD):
+            pair = slice(h // 2 * 2 * HEAD, (h // 2 + 1) * 2 * HEAD)
+            own = slice(h * HEAD, (h + 1) * HEAD)
+            queries = q_ref[rows, pair] * head_row(h, HEAD ** (-0.5))
+            scores = dot_nt(k_ref[:count, pair], queries) + bias[:count, rows]
+            top = jnp.max(scores, axis=0, keepdims=True)
+            probs = jnp.exp(scores - top)
+            total = jnp.sum(probs, axis=0, keepdims=True)
+            mixed = dot_nn(value_t[own, :count], probs.astype(BF16))
+            out_t[own, :] = mixed * (1.0 / total)
+            lse_ref[0, h : h + 1, rows] = top + jnp.log(total)
+        o_ref[rows, :] = out_t[...].T.astype(BF16)
+
+    @pl.when(pl.program_id(0) == pl.num_programs(0) - 1)
+    def _():
+        finish(1)
+
+        @pl.when(jnp.logical_not(place.active))
+        def _():
+            copy = pltpu.make_async_copy(arrived, cot_ref, copy_sem.at[1])
+            copy.start()
+            copy.wait()
+
+
+def front(lens, tokens_in, cotangent, gain, shift, qkv_weight, qv_bias):
+    rows, span, width = tokens_in.shape
+    spans = lax.axis_size("seq")
+    tokens = spans * span
+    lanes = min(256, width)
+    groups = width // lanes
+    heads = max(8, lanes // HEAD)
+    whole = lambda shape: pl.BlockSpec(shape, lambda g: (0,) * len(shape))
+    columns = lambda shape, first: pl.BlockSpec(shape, lambda g: (0, first + g))
+    act = jax.ShapeDtypeStruct((tokens, width), BF16)
+    sem = lambda *shape: pltpu.SemaphoreType.DMA(shape)
+    return pl.pallas_call(
+        front_kernel,
+        grid=(groups,),
+        out_shape=(
+            act, act, act, act, jax.ShapeDtypeStruct((groups, heads, tokens), F32), act,
+            jax.ShapeDtypeStruct((spans, span, width), BF16),
+        ),
+        in_specs=[
+            pl.BlockSpec(memory_space=pltpu.SMEM),
+            pl.BlockSpec(memory_space=pl.ANY),
+            pl.BlockSpec(memory_space=pl.ANY),
+            whole((1, width)),
+            whole((1, width)),
+            columns((width, lanes), 0),
+            columns((width, lanes), groups),
+            columns((width, lanes), 2 * groups),
+            columns((1, lanes), 0),
+            columns((1, lanes), groups),
+        ],
+        out_specs=[columns((tokens, lanes), 0)] * 4
+        + [
+            pl.BlockSpec((1, heads, tokens), lambda g: (g, 0, 0)),
+            whole((tokens, width)),
+            pl.BlockSpec(memory_space=pl.ANY),
+        ],
+        scratch_shapes=[
+            pltpu.VMEM((spans, span, width), BF16),
+            pltpu.VMEM((tokens, width), BF16),
+            pltpu.VMEM((tokens, tokens), F32),
+            pltpu.VMEM((lanes, tokens), BF16),
+            pltpu.VMEM((lanes, span), F32),
+            sem(2, 3), sem(2, 3), sem(2),
+        ],
+        compiler_params=pltpu.CompilerParams(
+            collective_id=1, has_side_effects=True, vmem_limit_bytes=VMEM_LIMIT
+        ),
+        name="front",
+    )(lens, tokens_in, cotangent, gain, shift, qkv_weight, qkv_weight, qkv_weight, qv_bias, qv_bias)
+
+
+def feed_kernel(
+    lens_ref, o_ref, x_ref, cot_ref, wp_ref, bp_ref, gain_ref, shift_ref,
+    wf_ref, bf_ref, wo_ref, bo_ref,
+    lo_ref, dy_ref, do_ref, gp_ref, gf_ref, go_ref, gbf_ref, small_ref,
+    middle, normed, normed_t, cot_low, out_acc, back_acc, hidden, back_low,
+):
+    tokens, width = x_ref.shape
+    step, last = pl.program_id(0), pl.num_programs(0) - 1
+    block = min(256, tokens)
+    blocks = tokens // block
+
+    def each(body):
+        def run(i, carry):
+            start = pl.multiple_of(i * block, block)
+            body(start, pl.ds(start, block))
+            return carry
+
+        lax.fori_loop(0, blocks, run, 0)
+
+    @pl.when(step == 0)
+    def _():
+        small_ref[...] = jnp.zeros_like(small_ref)
+
+        def begin(start, rows):
+            attn = dot_nn(o_ref[rows, :], wp_ref[...]) + bp_ref[...]
+            mid = x_ref[rows, :].astype(F32) + branch_scale * attn
+            middle[rows, :] = mid
+            unit, _ = normalise(mid)
+            h2 = unit * gain_ref[...] + shift_ref[...]
+            normed[rows, :] = h2.astype(BF16)
+            normed_t[:, rows] = h2.T.astype(BF16)
+            keep = keep_column(lens_ref, Place().my_row, start, block)
+            low = (branch_scale * (keep * cot_ref[rows, :].astype(F32))).astype(BF16)
+            cot_low[rows, :] = low
+            small_ref[0:1, :] += jnp.sum(low.astype(F32), axis=0, keepdims=True)
+
+        each(begin)
+
+    gbf_ref[...] = jnp.zeros_like(gbf_ref)
+
+    def chunk(start, rows):
+        pre = dot_nn(normed[rows, :], wf_ref[...]) + bf_ref[...]
+        back = dot_nt(cot_low[rows, :], wo_ref[...])
+        square = pre * pre
+        root = (2.0 / jnp.pi) ** 0.5
+        bend = jnp.tanh(pre * (root + (root * 0.044715) * square))
+        half = 0.5 * pre
+        hid = (half + half * bend).astype(BF16)
+        slope = (0.5 + 0.5 * bend) + half * (1.0 - bend * bend) * (root + (3.0 * root * 0.044715) * square)
+        grad = (back * slope).astype(BF16)
+        hidden[rows, :] = hid
+        back_low[rows, :] = grad
+        gbf_ref[0:1, :] += jnp.sum(grad.astype(F32), axis=0, keepdims=True)
+        added = dot_nn(hid, wo_ref[...])
+        backed = dot_nt(grad, wf_ref[...])
+
+        @pl.when(step == 0)
+        def _():
+            out_acc[rows, :] = added
+            back_acc[rows, :] = backed
+
+        @pl.when(step > 0)
+        def _():
+            out_acc[rows, :] += added
+            back_acc[rows, :] += backed
+
+    each(chunk)
+    go_ref[0] = dot_tn(hidden[...], cot_low[...]).astype(BF16)
+    gf_ref[0] = dot_nn(normed_t[...], back_low[...]).astype(BF16)
+
+    @pl.when(step == last)
+    def _():
+        def end(start, rows):
+            keep = keep_column(lens_ref, Place().my_row, start, block)
+            mid = middle[rows, :]
+            lo_ref[rows, :] = (
+                keep * (mid + branch_scale * (out_acc[rows, :] + bo_ref[...]))
+            ).astype(BF16)
+            unit, inverse = normalise(mid)
+            back = back_acc[rows, :]
+            small_ref[1:2, :] += jnp.sum(back * unit, axis=0, keepdims=True)
+            small_ref[2:3, :] += jnp.sum(back, axis=0, keepdims=True)
+            scaled = back * gain_ref[...]
+            grad = keep * cot_ref[rows, :].astype(F32) + inverse * (
+                scaled - row_mean(scaled) - unit * row_mean(scaled * unit)
+            )
+            dy_ref[rows, :] = grad
+            low = (branch_scale * grad).astype(BF16)
+            hidden[rows, :] = low
+            small_ref[3:4, :] += jnp.sum(low.astype(F32), axis=0, keepdims=True)
+            do_ref[rows, :] = dot_nt(low, wp_ref[...]).astype(BF16)
+
+        each(end)
+        gp_ref[...] = dot_tn(o_ref[...], hidden[...]).astype(BF16)
+
+
+def feed(lens, o, x, cot, proj_weight, proj_bias, gain, shift, fc_weight, fc_bias, out_weight, out_bias):
+    tokens, width = x.shape
+    steps = fc_weight.shape[1] // width
+    whole = lambda shape: pl.BlockSpec(shape, lambda f: (0,) * len(shape))
+    act, vec, mat = whole((tokens, width)), whole((1, width)), whole((width, width))
+    panel = pl.BlockSpec((1, width, width), lambda f: (f, 0, 0))
+    shape = jax.ShapeDtypeStruct
+    return pl.pallas_call(
+        feed_kernel,
+        grid=(steps,),
+        out_shape=(
+            shape((tokens, width), BF16),
+            shape((tokens, width), F32),
+            shape((tokens, width), BF16),
+            shape((width, width), BF16),
+            shape((steps, width, width), BF16),
+            shape((steps, width, width), BF16),
+            shape((8, steps * width), F32),
+            shape((8, width), F32),
+        ),
+        in_specs=[
+            pl.BlockSpec(memory_space=pltpu.SMEM),
+            act, act, act, mat, vec, vec, vec,
+            pl.BlockSpec((width, width), lambda f: (0, f)),
+            pl.BlockSpec((1, width), lambda f: (0, f)),
+            pl.BlockSpec((width, width), lambda f: (f, 0)),
+            vec,
+        ],
+        out_specs=[
+            act, act, act, mat, panel, panel,
+            pl.BlockSpec((8, width), lambda f: (0, f)),
+            whole((8, width)),
+        ],
+        scratch_shapes=[
+            pltpu.VMEM((tokens, width), F32),
+            pltpu.VMEM((tokens, width), BF16),
+            pltpu.VMEM((width, tokens), BF16),
+            pltpu.VMEM((tokens, width), BF16),
+            pltpu.VMEM((tokens, width), F32),
+            pltpu.VMEM((tokens, width), F32),
+            pltpu.VMEM((tokens, width), BF16),
+            pltpu.VMEM((tokens, width), BF16),
+        ],
+        compiler_params=pltpu.CompilerParams(vmem_limit_bytes=VMEM_LIMIT),
+        name="feed",
+    )(lens, o, x, cot, proj_weight, proj_bias, gain, shift, fc_weight, fc_bias, out_weight, out_bias)
+
+
+def back_kernel(
+    lens_ref, x_ref, dy_ref, gain_ref, shift_ref, q_ref, k_ref, v_ref, o_ref, do_ref, lse_ref,
+    wq_ref, wk_ref, wv_ref,
+    dx_ref, gq_ref, gk_ref, gv_ref, gb_ref, small_ref,
+    bias, normed_t, back_acc, key_t, grad_q_t, grad_q, grad_k, grad_v,
+):
+    tokens, width = x_ref.shape
+    lanes = wq_ref.shape[1]
+    step, last = pl.program_id(0), pl.num_programs(0) - 1
+    block = min(256, tokens)
+    blocks = tokens // block
+
+    def each(body):
+        def run(i, carry):
+            start = pl.multiple_of(i * block, block)
+            body(start, pl.ds(start, block))
+            return carry
+
+        lax.fori_loop(0, blocks, run, 0)
+
+    @pl.when(step == 0)
+    def _():
+        fill_bias(lens_ref, Place().my_row, bias, block)
+        small_ref[...] = jnp.zeros_like(small_ref)
+
+        def begin(start, rows):
+            unit, _ = normalise(x_ref[rows, :].astype(F32))
+            h1 = unit * gain_ref[...] + shift_ref[...]
+            normed_t[:, rows] = h1.T.astype(BF16)
+
+        each(begin)
+
+    gb_ref[...] = jnp.zeros_like(gb_ref)
+    grad_k[...] = jnp.zeros_like(grad_k)
+    grad_v[...] = jnp.zeros_like(grad_v)
+    key_t[...] = k_ref[...].astype(F32).T.astype(BF16)
+    head_id = lax.broadcasted_iota(jnp.int32, (8, lanes), 0)
+    lane_id = lax.broadcasted_iota(jnp.int32, (8, lanes), 1)
+    member = ((lane_id >= head_id * HEAD) & (lane_id < (head_id + 1) * HEAD)).astype(F32)
+
+    for i in range(blocks):
+        rows = slice(i * block, (i + 1) * block)
+        count = (i + 1) * block
+        product = do_ref[rows, :].astype(F32) * o_ref[rows, :].astype(F32)
+        delta = lax.dot_general(
+            member, product, (((1,), (1,)), ((), ())),
+            precision=lax.Precision.HIGHEST, preferred_element_type=F32,
+        )
+        for h in range(lanes // HEAD):
+            pair = slice(h // 2 * 2 * HEAD, (h // 2 + 1) * 2 * HEAD)
+            own = slice(h * HEAD, (h + 1) * HEAD)
+            queries = q_ref[rows, pair] * head_row(h, HEAD ** (-0.5))
+            grads = do_ref[rows, pair] * head_row(h, 1.0)
+            scores = dot_nt(k_ref[:count, pair], queries) + bias[:count, rows]
+            probs = jnp.exp(scores - lse_ref[0, h : h + 1, rows])
+            grad_probs = dot_nt(v_ref[:count, pair], grads)
+            grad_scores = (probs * (grad_probs - delta[h : h + 1, :])).astype(BF16)
+            grad_v[:count, pair] += dot_nn(probs.astype(BF16), grads)
+            grad_k[:count, pair] += dot_nn(grad_scores, queries)
+            grad_q_t[own, rows] = dot_nn(key_t[own, :count], grad_scores)
+
+    def finish(start, rows):
+        dq = (grad_q_t[:, rows].T * HEAD ** (-0.5)).astype(BF16)
+        grad_q[rows, :] = dq
+        dk = grad_k[rows, :].astype(BF16)
+        dv = grad_v[rows, :].astype(BF16)
+        gb_ref[0:1, :] += jnp.sum(dq.astype(F32), axis=0, keepdims=True)
+        gb_ref[1:2, :] += jnp.sum(dv.astype(F32), axis=0, keepdims=True)
+        added = dot_nt(dq, wq_ref[...]) + dot_nt(dk, wk_ref[...]) + dot_nt(dv, wv_ref[...])
+
+        @pl.when(step == 0)
+        def _():
+            back_acc[rows, :] = added
+
+        @pl.when(step > 0)
+        def _():
+            back_acc[rows, :] += added
+
+    each(finish)
+    gq_ref[...] = dot_nn(normed_t[...], grad_q[...]).astype(BF16)
+    gk_ref[...] = dot_nn(normed_t[...], grad_k[...].astype(BF16)).astype(BF16)
+    gv_ref[...] = dot_nn(normed_t[...], grad_v[...].astype(BF16)).astype(BF16)
+
+    @pl.when(step == last)
+    def _():
+        def end(start, rows):
+            unit, inverse = normalise(x_ref[rows, :].astype(F32))
+            back = back_acc[rows, :]
+            small_ref[0:1, :] += jnp.sum(back * unit, axis=0, keepdims=True)
+            small_ref[1:2, :] += jnp.sum(back, axis=0, keepdims=True)
+            scaled = back * gain_ref[...]
+            grad = dy_ref[rows, :] + inverse * (
+                scaled - row_mean(scaled) - unit * row_mean(scaled * unit)
+            )
+            dx_ref[rows, :] = grad.astype(dx_ref.dtype)
+
+        each(end)
+
+
+def back(lens, x, dy, gain, shift, q, k, v, o, do, lse, qkv_weight):
+    tokens, width = x.shape
+    lanes = min(256, width)
+    groups = width // lanes
+    heads = lse.shape[1]
+    whole = lambda shape: pl.BlockSpec(shape, lambda g: (0,) * len(shape))
+    columns = lambda shape, first: pl.BlockSpec(shape, lambda g: (0, first + g))
+    act, vec = whole((tokens, width)), whole((1, width))
+    shape = jax.ShapeDtypeStruct
+    mat = shape((width, width), BF16)
+    return pl.pallas_call(
+        back_kernel,
+        grid=(groups,),
+        out_shape=(shape((tokens, width), BF16), mat, mat, mat, shape((8, width), F32), shape((8, width), F32)),
+        in_specs=[pl.BlockSpec(memory_space=pltpu.SMEM), act, act, vec, vec]
+        + [columns((tokens, lanes), 0)] * 5
+        + [
+            pl.BlockSpec((1, heads, tokens), lambda g: (g, 0, 0)),
+            columns((width, lanes), 0),
+            columns((width, lanes), groups),
+            columns((width, lanes), 2 * groups),
+        ],
+        out_specs=[act]
+        + [columns((width, lanes), 0)] * 3
+        + [columns((8, lanes), 0), whole((8, width))],
+        scratch_shapes=[
+            pltpu.VMEM((tokens, tokens), F32),
+            pltpu.VMEM((width, tokens), BF16),
+            pltpu.VMEM((tokens, width), F32),
+            pltpu.VMEM((lanes, tokens), BF16),
+            pltpu.VMEM((lanes, tokens), F32),
+            pltpu.VMEM((tokens, lanes), BF16),
+            pltpu.VMEM((tokens, lanes), F32),
+            pltpu.VMEM((tokens, lanes), F32),
+        ],
+        compiler_params=pltpu.CompilerParams(vmem_limit_bytes=VMEM_LIMIT),
+        name="back",
+    )(lens, x, dy, gain, shift, q, k, v, o, do, lse, qkv_weight, qkv_weight, qkv_weight)
+
+
+def reduce_kernel(
+    go_ref, gf_ref, gq_ref, gk_ref, gv_ref, gp_ref, small_ref,
+    out_ref, small_out,
+    work, recv0, recv1, recv2, recv3, part, sums, small_recv, line,
+    send_sem, recv_sem, copy_sem, load_sem, small_send, small_recv_sem,
+):
+    place = Place()
+    units = work.shape[0]
+    feed_units = units - 2
+    loads = [(go_ref.at[f], (f, 0)) for f in range(feed_units)]
+    loads += [(gf_ref.at[f], (f, 1)) for f in range(feed_units)]
+    loads += [(gq_ref, (feed_units, 0)), (gk_ref, (feed_units, 1)), (gv_ref, (feed_units + 1, 0)), (gp_ref, (feed_units + 1, 1))]
+    copies = [pltpu.make_async_copy(source, work.at[u, p], load_sem.at[u, p]) for source, (u, p) in loads]
+    for copy in copies:
+        copy.start()
+    sums[0] = small_ref[...]
+    place.greet()
+    small = SmallReducer(place, sums, small_recv, line, small_send, small_recv_sem)
+    main = Reducer(place, work, recv0, recv1, recv2, recv3, part, out_ref, send_sem, recv_sem, copy_sem)
+    for copy in copies:
+        copy.wait()
+    small.step(0)
+
+    def tick(t, carry):
+        for phase in range(8, -1, -1):
+            u = t - phase
+
+            @pl.when((u >= 0) & (u < units))
+            def _():
+                main.step(phase, u)
+
+        return carry
+
+    lax.fori_loop(0, units + 8, tick, 0)
+    for phase in range(1, 5):
+        small.step(phase)
+    small_out[...] = small.total()
+
+
+def all_reduce(go, gf, gq, gk, gv, gp, small):
+    units, width = go.shape[0] + 2, gp.shape[0]
+    vmem = lambda *shape: pltpu.VMEM(shape, BF16)
+    sem = lambda *shape: pltpu.SemaphoreType.DMA(shape)
+    return pl.pallas_call(
+        reduce_kernel,
+        out_shape=(
+            jax.ShapeDtypeStruct((units, 2, width, width), BF16),
+            jax.ShapeDtypeStruct(small.shape, F32),
+        ),
+        in_specs=[pl.BlockSpec(memory_space=pl.ANY)] * 6 + [pl.BlockSpec(memory_space=pltpu.VMEM)],
+        out_specs=[pl.BlockSpec(memory_space=pl.ANY), pl.BlockSpec(memory_space=pltpu.VMEM)],
+        scratch_shapes=[
+            vmem(units, 2, width, width),
+            vmem(units, 2, width // 2, width),
+            vmem(units, 2, width // 4, width),
+            vmem(units, 2, width // 8, width),
+            vmem(units, 3, width // 16, width),
+            vmem(units, width // 16, width),
+            pltpu.VMEM((4,) + small.shape, F32),
+            pltpu.VMEM((3,) + small.shape, F32),
+            pltpu.VMEM((4,) + small.shape, F32),
+            sem(units, 12), sem(units, 12), sem(units), sem(units, 2), sem(6), sem(6),
+        ],
+        compiler_params=pltpu.CompilerParams(
+            collective_id=0, has_side_effects=True, vmem_limit_bytes=VMEM_LIMIT
+        ),
+        name="all_reduce",
+    )(go, gf, gq, gk, gv, gp, small)
+
+
+def spread_kernel(lo_ref, dx_ref, lo_out, dx_out, send_sem, recv_sem, copy_sem):
+    place = Place()
+    place.greet_plane()
+    sources, targets = (dx_ref, lo_ref), (dx_out, lo_out)
+
+    def outgoing(which, hop):
+        other, row = place.in_plane(hop)
+        return row, send(
+            sources[which].at[other[1]], targets[which].at[place.my_row],
+            send_sem.at[which, hop - 1], recv_sem.at[which, hop - 1], other,
+        )
+
+    def local(which):
+        return pltpu.make_async_copy(
+            sources[which].at[place.seq], targets[which].at[place.my_row], copy_sem.at[which]
+        )
+
+    for which in (0, 1):
+        for hop in (1, 2, 3):
+            row, copy = outgoing(which, hop)
+            pl.when(place.active)(copy.start)
+        pl.when(place.active)(local(which).start)
+    for which in (0, 1):
+        for hop in (1, 2, 3):
+            row, copy = outgoing(which, hop)
+            pl.when(place.active)(copy.wait_send)
+            pl.when(row < 3)(copy.wait_recv)
+        pl.when(place.active)(local(which).wait)
+
+
+def spread(lo, dx, rows):
+    spans, span, width = lo.shape
+    out = jax.ShapeDtypeStruct((rows, span, width), BF16)
+    sem = lambda *shape: pltpu.SemaphoreType.DMA(shape)
+    return pl.pallas_call(
+        spread_kernel,
+        out_shape=(out, out),
+        in_specs=[pl.BlockSpec(memory_space=pl.ANY)] * 2,
+        out_specs=[pl.BlockSpec(memory_space=pl.ANY)] * 2,
+        scratch_shapes=[sem(2, 3), sem(2, 3), sem(2)],
+        compiler_params=pltpu.CompilerParams(collective_id=2, has_side_effects=True),
+        name="spread",
+    )(lo, dx)
+
+
+def by_rows(
+    tokens_in, lengths, ln1_gain, ln1_bias, qkv_weight, qv_bias, proj_weight, proj_bias,
+    ln2_gain, ln2_bias, fc_weight, fc_bias, out_weight, out_bias, cotangent,
+):
+    rows, span, width = tokens_in.shape
+    flat = lambda array: array.reshape(1, -1)
+    q, k, v, o, lse, x, cot = front(
+        lengths, tokens_in, cotangent, flat(ln1_gain), flat(ln1_bias), qkv_weight, flat(qv_bias)
+    )
+    lo, dy, do, gp, gf, go, gbf, small2 = feed(
+        lengths, o, x, cot.reshape(x.shape), proj_weight, flat(proj_bias), flat(ln2_gain), flat(ln2_bias),
+        fc_weight, flat(fc_bias), out_weight, flat(out_bias),
+    )
+    dx, gq, gk, gv, gb, small1 = back(
+        lengths, x, dy, flat(ln1_gain), flat(ln1_bias), q, k, v, o, do, lse, qkv_weight
+    )
+    small = jnp.concatenate(
+        [small1[0:2], gb[0:2], small2[0:4], gbf[0].reshape(-1, width), jnp.zeros((4, width), F32)]
+    )
+    whole, small = all_reduce(go, gf, gq, gk, gv, gp, small)
+    layer_out, input_grad = spread(
+        lo.reshape(-1, span, width), dx.reshape(-1, span, width), rows
+    )
+    whole = whole.astype(F32)
+    steps = go.shape[0]
+    return (
+        layer_out,
+        input_grad.astype(F32),
+        small[0],
+        small[1],
+        jnp.concatenate([whole[steps, 0], whole[steps, 1], whole[steps + 1, 0]], axis=1),
+        small[2:4].reshape(-1),
+        whole[steps + 1, 1],
+        small[7],
+        small[5],
+        small[6],
+        whole[:steps, 1].transpose(1, 0, 2).reshape(width, -1),
+        small[8 : 8 + steps].reshape(-1),
+        whole[:steps, 0].reshape(-1, width),
+        small[4],
+    )
 
 
 def layer_norm(values, gain, shift):
@@ -409,4 +1246,5 @@
         P(),
         P(),
     )
-    return jax.shard_map(local, mesh=mesh, in_specs=in_specs, out_specs=out_specs, check_vma=False)
+    own_rows = mesh.shape["row"] == 8 and mesh.shape["seq"] == 4
+    return jax.shard_map(by_rows if own_rows else local, mesh=mesh, in_specs=in_specs, out_specs=out_specs, check_vma=False)

time: 766 us -> 443 us (0.58)
  Pallas kernels: 0 us -> 363 us
  waiting for transfers between devices: 250 us -> 0 us
  matrix products: 219 us -> 0 us
  blocking collectives: 109 us -> 0 us
  other arithmetic: 96.3 us -> 16.3 us
  between operations: 18 us -> 0.72 us
    pallas_call x0 -> x5, Pallas kernels: none -> 363 us  [the longest x1 166 us: all_reduce(): pl.pallas_call(reduce_kernel, out_shape=(jax.ShapeDtypeStruct((units, 2,...]
    dot_general x19 -> x0, matrix products: 219 us -> none  [the longest x4 32.9 us: left_dot(): lax.dot_general(left, right, (((0,), (0,)), ((), ())), preferred_element_...]
    all_gather x8 -> x0, waiting for transfers between devices: 107 us -> none  [the longest x1 59.4 us: local(): key_piece = lax.all_gather(keys, 'seq', axis=1, tiled=True)]
    reduce_scatter x4 -> x0, waiting for transfers between devices: 73.3 us -> none  [the longest x1 45.1 us: local(): lax.psum_scatter(local_grads[2].astype(jnp.bfloat16), 'row', scatter_dime...]
    psum x1 -> x0, waiting for transfers between devices: 67.1 us -> none  [local(): lax.psum(shares[2].astype(jnp.bfloat16), 'seq').astype(jnp.float32)]
    unnamed x2 -> x0, blocking collectives: 58.6 us -> none
    reduce_sum x11 -> x0, other arithmetic: 35.7 us -> none  [the longest x1 18.3 us: forward_update(): total = jnp.sum(weights, axis=-1)]
    convert_element_type x20 -> x2, other arithmetic: 42.9 us -> 11.4 us  [the longest x1 9.77 us: by_rows(): whole = whole.astype(F32)]
  transfers between devices with their start and end apart: 13 -> 0, of which waited for: 5 -> 0; matrix products, arithmetic and copies ran while one was open for 47% -> 0% of each run, Pallas kernels for 0% -> 0%
where the time goes in v1:
time: 443 us; the launch traced here: 442 us
  Pallas kernels  363 us (82%)
  local copies, waits for them, and re-layouts  61.9 us (14%)
  other arithmetic  16.3 us (4%)
    pallas_call x1, Pallas kernels, all_reduce(): pl.pallas_call(reduce_kernel, out_shape=(jax.ShapeDtypeStruct((units, 2,...  166 us
    pallas_call x1, Pallas kernels, front(): pl.pallas_call(front_kernel, grid=(groups,), out_shape=(act, act, act, ac...  61.6 us
    pallas_call x1, Pallas kernels, feed(): pl.pallas_call(feed_kernel, grid=(steps,), out_shape=(shape((tokens, widt...  55.3 us
    pallas_call x1, Pallas kernels, back(): pl.pallas_call(back_kernel, grid=(groups,), out_shape=(shape((tokens, wid...  46.7 us
    pallas_call x1, Pallas kernels, spread(): pl.pallas_call(spread_kernel, out_shape=(out, out), in_specs=[pl.BlockSpe...  34 us
    transpose x2, local copies, waits for them, and re-layouts, by_rows(): whole[:steps, 1].transpose(1, 0, 2).reshape(width, -1)  17.7 us
    unnamed x10, local copies, waits for them, and re-layouts  12.4 us
    convert_element_type x1, other arithmetic, by_rows(): whole = whole.astype(F32)  9.77 us

profile of v1, /device:TPU:0, one launch (start us, length us, event | category | flops | bytes accessed | tf_op | source)
XLA Modules:
  0.0 442.2 jit_solution(4708294946136787534)
XLA Ops:
  0.6 1.3 reshape.72.gain_ref
  1.9 1.3 reshape.73.shift_ref
  3.2 1.3 reshape.76.bp_ref
  4.4 1.3 reshape.77.gain_ref
  5.7 1.3 reshape.78.shift_ref
  7.0 1.3 reshape.80.bo_ref
  8.2 1.3 reshape.74.bq_ref.bv_ref
  9.5 61.6 %front.1 = (bf16[1024,768]{1,0:T(8,128)(2,1)}, bf16[1024,768]{1,0:T(8,128)(2,1)}, bf16[1024,768]{1,0:T(8,128)(2,1)}, bf16[1024,768]{1,0:T(8,128)(2,1)}, f32[3,8,...) custom-call(s32[3,8]{1,0:T(4,128)} %lens_ref.5, bf16[3,256,768]{2,1,0:T(8,128)(2,1)} %tokens_ref.1, ...), custom_call_target="tpu_custom_call" | custom-call | tf_op jit(solution)/shard_map/front/pallas_call | solution.py:370
  71.1 55.3 %feed.1 = (bf16[1024,768]{1,0:T(8,128)(2,1)}, f32[1024,768]{1,0:T(8,128)}, bf16[1024,768]{1,0:T(8,128)(2,1)}, bf16[768,768]{1,0:T(8,128)(2,1)}, bf16[4,768,768]{...) custom-call(s32[3,8]{1,0:T(4,128)} %lens_ref.5, ...), custom_call_target="tpu_custom_call" | custom-call | tf_op jit(solution)/shard_map/feed/pallas_call | solution.py:513
  126.4 46.7 %back.1 = (bf16[1024,768]{1,0:T(8,128)(2,1)}, bf16[768,768]{1,0:T(8,128)(2,1)}, bf16[768,768]{1,0:T(8,128)(2,1)}, bf16[768,768]{1,0:T(8,128)(2,1)}, f32[8,768]{1,0:T(8,128)}, /*index=5*/f32[8,768]{1,0:T(8,128)}) custom-call(s32[3,8]{1,0:T(4,128)} %lens_ref.5, bf16[1024,768]{1,0:T(8,128)(2,1)} %get-tuple-element.40.x_ref, ...), custom_call_target="tpu_custom_call" | custom-call | tf_op jit(solution)/shard_map/back/pallas_call | solution.py:663
  173.2 34.0 %spread.1 = (bf16[3,256,768]{2,1,0:T(8,128)(2,1)}, bf16[3,256,768]{2,1,0:T(8,128)(2,1)}) custom-call(bf16[4,256,768]{2,1,0:T(8,128)(2,1)} %bitcast.21, bf16[4,256,768]{2,1,0:T(8,128)(2,1)} %bitcast.22), custom_call_target="tpu_custom_call" | custom-call | tf_op jit(solution)/shard_map/spread/pallas_call | solution.py:797
  209.6 1.3 concatenate.6.small_ref
  210.9 165.6 %all_reduce.1 = (bf16[6,2,768,768]{3,2,1,0:T(8,128)(2,1)}, f32[16,768]{1,0:T(8,128)}) custom-call(bf16[4,768,768]{2,1,0:T(8,128)(2,1)} %get-tuple-element.52.go_ref, bf16[4,768,768]{2,1,0:T(8,128)(2,1)} %get-tuple-element.53.gf_ref, bf16[768,768]{1,0:T(8,128)(2,1)} %get-tuple-element.54.gq_ref, bf16[768,768]{1,0:T(8,128)(2,1)} %get-tuple-element.55.gk_ref, ...), custom_call_target="tpu_custom_call" | custom-call | tf_op jit(solution)/shard_map/all_reduce/pallas_call | solution.py:736
  378.6 1.6 slice_reduce_fusion.1
  380.9 1.6 convert_element_type.6
  382.5 8.1 %slice.77 = f32[4,1,768,768]{3,2,1,0:T(8,128)} slice(bf16[6,2,768,768]{3,2,1,0:T(8,128)(2,1)} %get-tuple-element.63), slice={[0:4], [0:1], [0:768], [0:768]} | slice | bytes 18874368 | tf_op jit(solution)/shard_map/slice | solution.py:846
  390.6 1.8 copy-done
  392.3 9.8 %convert_element_type.7 = f32[6,2,768,768]{3,2,1,0:T(8,128)} convert(bf16[6,2,768,768]{3,2,1,0:T(8,128)(2,1)S(1)} %copy-done) | non-fusion elementwise | flops 7077888 | bytes 42467328 | tf_op jit(solution)/shard_map/convert_element_type | solution.py:831
  402.1 8.0 %slice_bitcast_fusion = f32[768,4,768]{2,0,1:T(8,128)} fusion(f32[6,2,768,768]{3,2,1,0:T(8,128)} %convert_element_type.7), kind=kLoop, calls=%fused_computation | loop fusion | bytes 18874368 | tf_op jit(solution)/shard_map/transpose | solution.py:844
  410.1 6.9 %slice_bitcast_fusion.1 = (f32[768,768]{1,0:T(8,128)}, f32[768,768]{1,0:T(8,128)S(1)}, f32[768,768]{1,0:T(8,128)}, f32[768,768]{1,0:T(8,128)}) fusion(f32[6,2,768,768]{3,2,1,0:T(8,128)} %convert_element_type.7), kind=kLoop, calls=%fused_computation.2 | loop fusion | bytes 18874368 | tf_op jit(solution)/shard_map/squeeze | solution.py:840
  417.0 9.7 %copy.29 = f32[768,4,768]{0,2,1:T(8,128)} copy(f32[768,4,768]{2,0,1:T(8,128)} %slice_bitcast_fusion) | data formatting | bytes 18874368 | tf_op jit(solution)/shard_map/transpose | solution.py:844
  426.7 9.6 %copy.30 = f32[768,3072]{1,0:T(8,128)} copy(f32[768,3072]{0,1:T(8,128)} %bitcast.18) | data formatting | bytes 18874368
  436.2 4.9 %pad_maximum_fusion = f32[768,2304]{1,0:T(8,128)} fusion(f32[768,768]{1,0:T(8,128)S(1)} %get-tuple-element.85, f32[768,768]{1,0:T(8,128)} %get-tuple-element.86, f32[768,768]{1,0:T(8,128)} %get-tuple-element.87), kind=kLoop, calls=%fused_computation.1 | loop fusion | flops 3538944 | bytes 14155776 | tf_op jit(solution)/shard_map/concatenate | solution.py:838
  441.2 1.0 copy.32
  (17 shorter events, 5.1 us)
Async XLA Ops:
  173.2 35.5 %copy-start.3 = (f32[8,768]{1,0:T(8,128)S(1)}, f32[8,768]{1,0:T(8,128)}, u32[]{:S(2)}) copy-start(f32[8,768]{1,0:T(8,128)} %get-tuple-element.60) | copy-start | bytes 73732
  210.9 170.0 %copy-start.1 = (bf16[3,256,768]{2,1,0:T(8,128)(2,1)S(1)}, bf16[3,256,768]{2,1,0:T(8,128)(2,1)}, u32[]{:S(2)}) copy-start(bf16[3,256,768]{2,1,0:T(8,128)(2,1)} %get-tuple-element.51) | copy-start | bytes 3538948
  382.5 9.8 %copy-start = (bf16[6,2,768,768]{3,2,1,0:T(8,128)(2,1)S(1)}, bf16[6,2,768,768]{3,2,1,0:T(8,128)(2,1)}, u32[]{:S(2)}) copy-start(bf16[6,2,768,768]{3,2,1,0:T(8,128)(2,1)} %get-tuple-element.63) | copy-start | bytes 42467332
  436.2 4.9 %copy-start.2 = (bf16[3,256,768]{2,1,0:T(8,128)(2,1)S(1)}, bf16[3,256,768]{2,1,0:T(8,128)(2,1)}, u32[]{:S(2)}) copy-start(bf16[3,256,768]{2,1,0:T(8,128)(2,1)} %get-tuple-element.102) | copy-start | bytes 3538948

commit v2 on v0

--- a/solution.py
+++ b/solution.py
@@ -1,14 +1,918 @@
+import functools
+
 import jax
 import jax.numpy as jnp
 from jax import lax
+from jax.experimental import pallas as pl
+from jax.experimental.pallas import tpu as pltpu
 from jax.sharding import PartitionSpec as P
 
 HEAD = 64
-
-
 branch_scale = 12.0 ** (-0.5)
 masked_value = -1e30
 norm_eps = 1e-05
+F32, BF16 = jnp.float32, jnp.bfloat16
+VMEM_LIMIT = 60 * 1024 * 1024
+
+
+MESH = pl.DeviceIdType.MESH
+
+
+class Place:
+    def __init__(self):
+        row, seq = lax.axis_index("row"), lax.axis_index("seq")
+        self.row, self.seq = row, seq
+        self.core, self.z = lax.rem(row, 2), lax.div(row, 2)
+        self.x, self.y = lax.rem(seq, 2), lax.div(seq, 2)
+        self.sibling = (row + 1 - 2 * self.core, seq)
+        self.across_x = (row, seq + 1 - 2 * self.x)
+        self.across_y = (row, seq + 2 - 4 * self.y)
+        step_x, step_y = 1 - 2 * self.x, 2 - 4 * self.y
+        self.first_bit = self.x + self.core * (self.y - self.x)
+        self.second_bit = self.y + self.core * (self.x - self.y)
+        self.first = (row, seq + step_x + self.core * (step_y - step_x))
+        self.second = (row, seq + step_y + self.core * (step_x - step_y))
+
+        own = seq + self.core * (3 - 2 * seq)
+        self.active = own < 3
+        self.my_row = jnp.minimum(own, 2)
+
+    def in_plane(self, hop):
+        across_x, across_y = hop % 2, hop // 2
+        x = self.x + across_x * (1 - 2 * self.x)
+        y = self.y + across_y * (1 - 2 * self.y)
+        seq = 2 * y + x
+        return (self.row, seq), seq + self.core * (3 - 2 * seq)
+
+    def greet_plane(self):
+        barrier = pltpu.get_barrier_semaphore()
+        for hop in (1, 2, 3):
+            pl.semaphore_signal(barrier, inc=1, device_id=self.in_plane(hop)[0], device_id_type=MESH)
+        pl.semaphore_wait(barrier, 3)
+
+    def along_z(self, hop):
+        return (2 * lax.rem(self.z + hop, 4) + self.core, self.seq)
+
+    def greet(self):
+        barrier = pltpu.get_barrier_semaphore()
+        others = [self.sibling, self.across_x, self.across_y] + [self.along_z(hop) for hop in (1, 2, 3)]
+        for other in others:
+            pl.semaphore_signal(barrier, inc=1, device_id=other, device_id_type=MESH)
+        pl.semaphore_wait(barrier, len(others))
+
+
+def send(source, target, send_sem, recv_sem, device):
+    return pltpu.make_async_remote_copy(
+        src_ref=source, dst_ref=target, send_sem=send_sem, recv_sem=recv_sem,
+        device_id=device, device_id_type=MESH,
+    )
+
+
+class SmallReducer:
+    def __init__(self, place, sums, recv, line, send_sem, recv_sem):
+        self.place, self.sums, self.recv, self.line = place, sums, recv, line
+        self.send_sem, self.recv_sem = send_sem, recv_sem
+
+    def copies(self, phase):
+        place = self.place
+        if phase < 3:
+            other = (place.sibling, place.across_x, place.across_y)[phase]
+            return [send(self.sums.at[phase], self.recv.at[phase], self.send_sem.at[phase], self.recv_sem.at[phase], other)]
+        return [
+            send(self.sums.at[3], self.line.at[place.z], self.send_sem.at[2 + hop], self.recv_sem.at[2 + hop], place.along_z(hop))
+            for hop in (1, 2, 3)
+        ]
+
+    def step(self, phase):
+        if phase > 0:
+            for copy in self.copies(phase - 1):
+                copy.wait()
+        if 0 < phase < 4:
+            self.sums[phase] = self.sums[phase - 1] + self.recv[phase - 1]
+        if phase < 4:
+            for copy in self.copies(phase):
+                copy.start()
+        if phase == 3:
+            self.line[self.place.z] = self.sums[3]
+
+    def total(self):
+        return (self.line[0] + self.line[1]) + (self.line[2] + self.line[3])
+
+
+def dot_nn(left, right):
+    return lax.dot_general(left, right, (((1,), (0,)), ((), ())), preferred_element_type=F32)
+
+
+def dot_nt(left, right):
+    return lax.dot_general(left, right, (((1,), (1,)), ((), ())), preferred_element_type=F32)
+
+
+def dot_tn(left, right):
+    return lax.dot_general(left, right, (((0,), (0,)), ((), ())), preferred_element_type=F32)
+
+
+def row_mean(values):
+    return jnp.mean(values, axis=-1, keepdims=True)
+
+
+def normalise(values):
+    center = values - row_mean(values)
+    inverse = lax.rsqrt(row_mean(center * center) + norm_eps)
+    return center * inverse, inverse
+
+
+def fill_bias(lens_ref, row, bias_ref, block):
+    tokens = bias_ref.shape[0]
+    ends, total = [], jnp.int32(0)
+    for j in range(lens_ref.shape[1]):
+        total = total + lens_ref[row, j]
+        ends.append(total)
+    query_pos = lax.broadcasted_iota(jnp.int32, (1, tokens), 1)
+    query_seg = jnp.zeros((1, tokens), jnp.int32)
+    for end in ends:
+        query_seg = query_seg + (query_pos >= end).astype(jnp.int32)
+
+    def one(i, carry):
+        start = pl.multiple_of(i * block, block)
+        key_pos = start + lax.broadcasted_iota(jnp.int32, (block, 1), 0)
+        key_seg = jnp.zeros((block, 1), jnp.int32)
+        for end in ends:
+            key_seg = key_seg + (key_pos >= end).astype(jnp.int32)
+        allowed = (key_pos <= query_pos) & (key_seg == query_seg)
+        bias_ref[pl.ds(start, block), :] = jnp.where(allowed, 0.0, masked_value)
+        return carry
+
+    lax.fori_loop(0, tokens // block, one, 0)
+
+
+def keep_column(lens_ref, row, start, block):
+    total = jnp.int32(0)
+    for j in range(lens_ref.shape[1]):
+        total = total + lens_ref[row, j]
+    pos = start + lax.broadcasted_iota(jnp.int32, (block, 1), 0)
+    return (pos < total).astype(F32)
+
+
+def head_row(h, value):
+    lane = lax.broadcasted_iota(jnp.int32, (1, 2 * HEAD), 1)
+    low = h % 2 * HEAD
+    return jnp.where((lane >= low) & (lane < low + HEAD), value, 0.0).astype(BF16)
+
+
+def front_kernel(
+    lens_ref, tokens_ref, cot_in_ref, gain_ref, shift_ref, wq_ref, wk_ref, wv_ref, bq_ref, bv_ref,
+    q_ref, k_ref, v_ref, o_ref, lse_ref, x_ref, cot_ref,
+    arrived, normed, bias, value_t, out_t, send_sem, recv_sem, copy_sem,
+):
+    tokens, width = x_ref.shape
+    lanes = wq_ref.shape[1]
+    block = tokens_ref.shape[1]
+    blocks = tokens // block
+    place = Place()
+    mine = pl.ds(place.seq, 1)
+    sources, targets = (tokens_ref, cot_in_ref), (arrived, cot_ref)
+
+    def outgoing(which, hop):
+        other, row = place.in_plane(hop)
+        return row, send(
+            sources[which].at[jnp.minimum(row, 2)], targets[which].at[place.seq],
+            send_sem.at[which, hop - 1], recv_sem.at[which, hop - 1], other,
+        )
+
+    def local(which):
+        return pltpu.make_async_copy(
+            sources[which].at[place.my_row], targets[which].at[place.seq], copy_sem.at[which]
+        )
+
+    def start(which):
+        for hop in (1, 2, 3):
+            row, copy = outgoing(which, hop)
+            pl.when(row < 3)(copy.start)
+        pl.when(place.active)(local(which).start)
+
+    def finish(which):
+        for hop in (1, 2, 3):
+            row, copy = outgoing(which, hop)
+            pl.when(row < 3)(copy.wait_send)
+            pl.when(place.active)(copy.wait_recv)
+        pl.when(place.active)(local(which).wait)
+
+    @pl.when(pl.program_id(0) == 0)
+    def _():
+        place.greet_plane()
+        start(0)
+        start(1)
+        fill_bias(lens_ref, place.my_row, bias, block)
+
+        @pl.when(jnp.logical_not(place.active))
+        def _():
+            arrived[...] = jnp.zeros_like(arrived)
+
+        finish(0)
+
+        def one(i, carry):
+            rows = pl.ds(pl.multiple_of(i * block, block), block)
+            x = arrived[i]
+            x_ref[rows, :] = x
+            unit, _ = normalise(x.astype(F32))
+            normed[rows, :] = (unit * gain_ref[...] + shift_ref[...]).astype(BF16)
+            return carry
+
+        lax.fori_loop(0, blocks, one, 0)
+
+    def project(i, carry):
+        rows = pl.ds(pl.multiple_of(i * block, block), block)
+        h1 = normed[rows, :]
+        q_ref[rows, :] = (dot_nn(h1, wq_ref[...]) + bq_ref[...]).astype(BF16)
+        k_ref[rows, :] = dot_nn(h1, wk_ref[...]).astype(BF16)
+        values = dot_nn(h1, wv_ref[...]) + bv_ref[...]
+        v_ref[rows, :] = values.astype(BF16)
+        value_t[:, rows] = values.T.astype(BF16)
+        return carry
+
+    lax.fori_loop(0, blocks, project, 0)
+
+    for i in range(blocks):
+        rows = slice(i * block, (i + 1) * block)
+        count = (i + 1) * block
+        for h in range(lanes // HEAD):
+            pair = slice(h // 2 * 2 * HEAD, (h // 2 + 1) * 2 * HEAD)
+            own = slice(h * HEAD, (h + 1) * HEAD)
+            queries = q_ref[rows, pair] * head_row(h, HEAD ** (-0.5))
+            scores = dot_nt(k_ref[:count, pair], queries) + bias[:count, rows]
+            top = jnp.max(scores, axis=0, keepdims=True)
+            probs = jnp.exp(scores - top)
+            total = jnp.sum(probs, axis=0, keepdims=True)
+            mixed = dot_nn(value_t[own, :count], probs.astype(BF16))
+            out_t[own, :] = mixed * (1.0 / total)
+            lse_ref[0, h : h + 1, rows] = top + jnp.log(total)
+        o_ref[rows, :] = out_t[...].T.astype(BF16)
+
+    @pl.when(pl.program_id(0) == pl.num_programs(0) - 1)
+    def _():
+        finish(1)
+
+        @pl.when(jnp.logical_not(place.active))
+        def _():
+            copy = pltpu.make_async_copy(arrived, cot_ref, copy_sem.at[1])
+            copy.start()
+            copy.wait()
+
+
+def front(lens, tokens_in, cotangent, gain, shift, qkv_weight, qv_bias):
+    rows, span, width = tokens_in.shape
+    spans = lax.axis_size("seq")
+    tokens = spans * span
+    lanes = 256 if width > 256 else 128
+    groups = width // lanes
+    heads = max(8, lanes // HEAD)
+    whole = lambda shape: pl.BlockSpec(shape, lambda g: (0,) * len(shape))
+    columns = lambda shape, first: pl.BlockSpec(shape, lambda g: (0, first + g))
+    act = jax.ShapeDtypeStruct((tokens, width), BF16)
+    sem = lambda *shape: pltpu.SemaphoreType.DMA(shape)
+    return pl.pallas_call(
+        front_kernel,
+        grid=(groups,),
+        out_shape=(
+            act, act, act, act, jax.ShapeDtypeStruct((groups, heads, tokens), F32), act,
+            jax.ShapeDtypeStruct((spans, span, width), BF16),
+        ),
+        in_specs=[
+            pl.BlockSpec(memory_space=pltpu.SMEM),
+            pl.BlockSpec(memory_space=pl.ANY),
+            pl.BlockSpec(memory_space=pl.ANY),
+            whole((1, width)),
+            whole((1, width)),
+            columns((width, lanes), 0),
+            columns((width, lanes), groups),
+            columns((width, lanes), 2 * groups),
+            columns((1, lanes), 0),
+            columns((1, lanes), groups),
+        ],
+        out_specs=[columns((tokens, lanes), 0)] * 4
+        + [
+            pl.BlockSpec((1, heads, tokens), lambda g: (g, 0, 0)),
+            whole((tokens, width)),
+            pl.BlockSpec(memory_space=pl.ANY),
+        ],
+        scratch_shapes=[
+            pltpu.VMEM((spans, span, width), BF16),
+            pltpu.VMEM((tokens, width), BF16),
+            pltpu.VMEM((tokens, tokens), F32),
+            pltpu.VMEM((lanes, tokens), BF16),
+            pltpu.VMEM((lanes, span), F32),
+            sem(2, 3), sem(2, 3), sem(2),
+        ],
+        compiler_params=pltpu.CompilerParams(
+            collective_id=1, has_side_effects=True, vmem_limit_bytes=VMEM_LIMIT
+        ),
+        name="front",
+    )(lens, tokens_in, cotangent, gain, shift, qkv_weight, qkv_weight, qkv_weight, qv_bias, qv_bias)
+
+
+class Unit:
+    slots = (0, 1, 4, 5, 8, 11, 12, 15)
+
+    def __init__(self, place, line, fresh, recv, part, out, send_sem, recv_sem, copy_sem):
+        self.place, self.line, self.fresh, self.recv, self.part, self.out = place, line, fresh, recv, part, out
+        self.send_sem, self.recv_sem, self.copy_sem = send_sem, recv_sem, copy_sem
+        _, rows, columns = fresh.shape
+        self.half, self.wide = rows // 2, columns // 2
+        self.own = place.core * self.half
+        self.away = self.half - self.own
+
+    @staticmethod
+    def scratch(line, n, rows, columns):
+        vmem = lambda *shape: pltpu.VMEM(shape, BF16)
+        wide = columns // 2
+        if line:
+            shapes = ((rows // 2, columns), (3, rows // 8, columns), (rows // 16, columns), (rows // 16, wide))
+        else:
+            shapes = ((rows // 2, columns), (rows // 4, columns), (rows // 8, columns), (3, rows // 16, wide))
+        return [vmem(*shape[:-2], n, *shape[-2:]) for shape in shapes] + [vmem(n, rows // 16, wide)]
+
+    def rows(self, start, count):
+        return pl.ds(pl.multiple_of(start, self.half // 8), count)
+
+    def columns(self, which):
+        return pl.ds(pl.multiple_of(which * self.wide, self.wide), self.wide)
+
+    def stage(self, number):
+        place, half = self.place, self.half
+        bit1, bit2 = place.first_bit, place.second_bit
+        every = slice(None)
+        if self.line:
+            if number == 1:
+                size = half // 4
+                part = lambda z: (self.rows(z * size, size), every)
+                others = [(place.along_z(hop), part(lax.rem(place.z + hop, 4))) for hop in (1, 2, 3)]
+                return others, part(place.z)
+            if number == 2:
+                size = half // 8
+                return [(place.first, (self.rows((1 - bit1) * size, size), every))], (self.rows(bit1 * size, size), every)
+            return [(place.second, (every, self.columns(1 - bit2)))], (every, self.columns(bit2))
+        if number < 3:
+            size = half // 2 ** number
+            bit, other = ((bit1, place.first), (bit2, place.second))[number - 1]
+            return [(other, (self.rows((1 - bit) * size, size), every))], (self.rows(bit * size, size), every)
+        size = half // 8
+        part = lambda z: (self.rows(lax.div(z, 2) * size, size), self.columns(lax.rem(z, 2)))
+        others = [(place.along_z(hop), part(lax.rem(place.z + hop, 4))) for hop in (1, 2, 3)]
+        return others, part(place.z)
+
+    def region(self, number):
+        place, half = self.place, self.half
+        every = slice(None)
+        if number == 0:
+            return self.rows(self.own, half), every
+        if self.line:
+            start = self.own + place.z * (half // 4)
+            if number == 1:
+                return self.rows(start, half // 4), every
+            rows = self.rows(start + place.first_bit * (half // 8), half // 8)
+            return rows, every if number == 2 else self.columns(place.second_bit)
+        start = self.own + place.first_bit * (half // 2)
+        if number == 1:
+            return self.rows(start, half // 2), every
+        start = start + place.second_bit * (half // 4)
+        if number == 2:
+            return self.rows(start, half // 4), every
+        return self.rows(start + lax.div(place.z, 2) * (half // 8), half // 8), self.columns(lax.rem(place.z, 2))
+
+    def held(self, number):
+        if number == 1 and self.line:
+            return self.recv[1].at[0]
+        return self.recv[number]
+
+    def copies(self, phase):
+        first = self.slots[phase]
+        sems = lambda i: (self.send_sem.at[first + i], self.recv_sem.at[first + i])
+        if phase == 0:
+            return [send(self.fresh.at[:, self.rows(self.away, self.half)], self.recv[0], *sems(0), self.place.sibling)]
+        if phase < 4:
+            others, _ = self.stage(phase)
+            source, target = self.held(phase - 1), self.recv[phase]
+            return [
+                send(source.at[:, *part], target.at[i] if len(others) > 1 else target, *sems(i), other)
+                for i, (other, part) in enumerate(others)
+            ]
+        if phase == 7:
+            others = [(self.place.sibling, None)]
+        else:
+            others, _ = self.stage(7 - phase)
+        where = self.out.at[:, *self.region(7 - phase)]
+        source = self.part if phase == 4 else where
+        return [send(source, where, *sems(i), other) for i, (other, _) in enumerate(others)]
+
+    def local(self):
+        return pltpu.make_async_copy(self.part, self.out.at[:, *self.region(3)], self.copy_sem)
+
+    def add(self, phase):
+        if phase == 0:
+            source, target, more = self.fresh.at[:, self.rows(self.own, self.half)], self.recv[0], []
+        else:
+            others, part = self.stage(phase)
+            source, target, more = self.held(phase - 1).at[:, *part], self.recv[phase], []
+            if len(others) > 1:
+                target, more = self.recv[phase].at[0], [self.recv[phase].at[1], self.recv[phase].at[2]]
+        result = self.part if phase == 3 else target
+        n, count, _ = target.shape
+        step = self.half // 8
+
+        def one(i, carry):
+            rows = self.rows(i * step, step)
+            for panel in range(n):
+                total = source[panel, rows, :].astype(F32) + target[panel, rows, :].astype(F32)
+                for other in more:
+                    total = total + other[panel, rows, :].astype(F32)
+                result[panel, rows, :] = total.astype(BF16)
+            return carry
+
+        if count == step:
+            one(0, 0)
+        else:
+            lax.fori_loop(0, count // step, one, 0)
+
+    def step(self, phase):
+        if phase > 0:
+            for copy in self.copies(phase - 1):
+                copy.wait()
+            if phase == 5:
+                self.local().wait()
+        if 0 < phase < 5:
+            self.add(phase - 1)
+        if phase < 8:
+            for copy in self.copies(phase):
+                copy.start()
+        if phase == 4:
+            self.local().start()
+
+
+class Exchange:
+    def __init__(self, place, source, target, send_sem, recv_sem, copy_sem):
+        self.place, self.source, self.target = place, source, target
+        self.send_sem, self.recv_sem, self.copy_sem = send_sem, recv_sem, copy_sem
+        self.span = target.shape[1]
+
+    def block(self, seq):
+        return self.source.at[pl.ds(pl.multiple_of(seq * self.span, self.span), self.span)]
+
+    def outgoing(self, hop):
+        other, row = self.place.in_plane(hop)
+        return row, send(
+            self.block(other[1]), self.target.at[self.place.my_row],
+            self.send_sem.at[hop - 1], self.recv_sem.at[hop - 1], other,
+        )
+
+    def local(self):
+        return pltpu.make_async_copy(self.block(self.place.seq), self.target.at[self.place.my_row], self.copy_sem)
+
+    def start(self):
+        for hop in (3, 1, 2):
+            pl.when(self.place.active)(self.outgoing(hop)[1].start)
+        pl.when(self.place.active)(self.local().start)
+
+    def finish(self):
+        for hop in (1, 2, 3):
+            row, copy = self.outgoing(hop)
+            pl.when(self.place.active)(copy.wait_send)
+            pl.when(row < 3)(copy.wait_recv)
+        pl.when(self.place.active)(self.local().wait)
+
+
+def plan(hooks, sizes, lines, made):
+    free = {"core": 0.0, "plane": 0.0, "line": 0.0}
+    now, flight, plans, ready = 0.0, {}, {}, {}
+
+    def work(unit, phase):
+        size, line = sizes[unit], lines[unit]
+        if phase in (0, 7):
+            return "core", size / 2 / 0.6
+        stage = phase if phase < 4 else 7 - phase
+        if line:
+            return (("line", size / 0.094), ("plane", size / 16 / 0.094), ("plane", size / 32 / 0.094))[stage - 1]
+        return (("plane", size / 4 / 0.094), ("plane", size / 8 / 0.094), ("line", size / 4 / 0.094))[stage - 1]
+
+    def go(unit, phase):
+        nonlocal now
+        now += 0.1 + (sizes[unit] / 2 ** phase * 0.5 if 0 < phase < 4 else 0.0)
+        if phase == 8:
+            del flight[unit]
+            return
+        kind, time = work(unit, phase)
+        begin = max(now, free[kind])
+        free[kind] = begin + time
+        flight[unit] = (phase, begin + time + 1.5)
+
+    for name, compute in hooks:
+        now += compute
+        plans[name] = []
+        for unit in sorted(flight):
+            phase, end = flight[unit]
+            if end <= now + 0.3:
+                plans[name].append((unit, phase + 1))
+                go(unit, phase + 1)
+        for unit, hook in made.items():
+            if hook == name:
+                plans[name].append((unit, 0))
+                go(unit, 0)
+                ready[unit] = now
+        if name in ("lo", "dx"):
+            free["plane"] = max(now, free["plane"]) + 16.0
+    tail = []
+    while flight:
+        unit = min(flight, key=lambda u: flight[u][1])
+        phase, end = flight[unit]
+        now = max(now, end)
+        tail.append((unit, phase + 1))
+        go(unit, phase + 1)
+    return plans, tail, now
+
+
+def body_kernel(
+    steps, groups, lines,
+    lens_ref, o_ref, x_ref, cot_ref, wp_ref, bp_ref, gain2_ref, shift2_ref, wf_ref, bf_ref, wo_ref, bo_ref,
+    gain1_ref, shift1_ref, q_ref, k_ref, v_ref, lse_ref, wq_ref, wk_ref, wv_ref,
+    lo_out, dx_out, feed_out, proj_out, qkv_out, small_out,
+    middle, normed, normed_t, cot_low, out_acc, back_acc, hidden, back_low, bias, key_t, grad_q_t,
+    fresh_feed, fresh_proj, fresh_qkv, sums, small_recv, line_sums,
+    unit_send, unit_recv, unit_copy, small_send, small_recv_sem, out_send, out_recv, out_copy,
+    *unit_scratch,
+):
+    tokens, width = x_ref.shape
+    lanes = wq_ref.shape[1]
+    span = lo_out.shape[1]
+    blocks = tokens // span
+    step = pl.program_id(0)
+    place = Place()
+    acc = sums.at[0]
+
+    units = []
+    for u in range(steps + 1 + groups):
+        if u < steps:
+            fresh, out = fresh_feed, feed_out.at[u]
+        elif u == steps:
+            fresh, out = fresh_proj, proj_out
+        else:
+            fresh, out = fresh_qkv, qkv_out.at[u - steps - 1]
+        buffers = unit_scratch[5 * u : 5 * u + 5]
+        units.append(Unit(
+            place, lines[u], fresh, buffers[:4], buffers[4], out, unit_send.at[u], unit_recv.at[u], unit_copy.at[u]
+        ))
+    small = SmallReducer(place, sums, small_recv, line_sums, small_send, small_recv_sem)
+    lo_back = Exchange(place, normed, lo_out, out_send.at[0], out_recv.at[0], out_copy.at[0])
+    dx_back = Exchange(place, cot_low, dx_out, out_send.at[1], out_recv.at[1], out_copy.at[1])
+
+    hooks = []
+    for s in range(steps):
+        if s == 0:
+            hooks.append(("begin", 5.0))
+        hooks += [((s, i), 2.0) for i in range(blocks)] + [((s, "made"), 3.0)]
+        if s == steps - 1:
+            hooks += [("lo", 5.0), ("proj", 2.0)]
+    for s in range(steps, steps + groups):
+        if s == steps:
+            hooks.append(("turn", 2.0))
+        hooks += [((s, i), 1.0 * (i + 1)) for i in range(blocks)] + [((s, "made"), 4.5)]
+    hooks.append(("dx", 2.0))
+    made = {u: (u, "made") for u in range(steps)}
+    made[steps] = "proj"
+    made.update({steps + 1 + g: (steps + g, "made") for g in range(groups)})
+    megabytes = lambda ref: ref.shape[0] * ref.shape[1] * ref.shape[2] * 2e-6
+    plans, tail, _ = plan(hooks, [megabytes(unit.fresh) for unit in units], lines, made)
+    order = [name for name, _ in hooks]
+    first = {u: order.index(name) for name, actions in plans.items() for u, phase in actions if phase == 1}
+    for u in [*range(steps - 1), *range(steps + 1, steps + groups)]:
+        assert first[u] < order.index(made[u + 1])
+
+    def hook(name, where=None):
+        actions = plans[name if where is None else (where, name)]
+        if not actions:
+            return
+
+        def act():
+            for u, phase in actions:
+                units[u].step(phase)
+
+        if where is None:
+            act()
+        else:
+            pl.when(step == where)(act)
+
+    def row_block(i):
+        return slice(i * span, (i + 1) * span)
+
+    def column_sum(values):
+        return jnp.sum(values, axis=0, keepdims=True)
+
+    @pl.when(step == 0)
+    def _():
+        place.greet()
+        place_sums = jnp.zeros_like(acc)
+        acc[...] = place_sums
+        for i in range(blocks):
+            rows = row_block(i)
+            attn = dot_nn(o_ref[rows, :], wp_ref[...]) + bp_ref[...]
+            mid = x_ref[rows, :].astype(F32) + branch_scale * attn
+            middle[rows, :] = mid
+            unit, _ = normalise(mid)
+            h2 = unit * gain2_ref[...] + shift2_ref[...]
+            normed[rows, :] = h2.astype(BF16)
+            normed_t[:, rows] = h2.T.astype(BF16)
+            keep = keep_column(lens_ref, place.my_row, i * span, span)
+            low = (branch_scale * (keep * cot_ref[rows, :].astype(F32))).astype(BF16)
+            cot_low[rows, :] = low
+            acc[4:5, :] += column_sum(low.astype(F32))
+            out_acc[rows, :] = jnp.zeros((span, width), F32)
+            back_acc[rows, :] = jnp.zeros((span, width), F32)
+
+    @pl.when(step < steps)
+    def _():
+        for i in range(blocks):
+            rows = row_block(i)
+            pre = dot_nn(normed[rows, :], wf_ref[...]) + bf_ref[...]
+            back = dot_nt(cot_low[rows, :], wo_ref[...])
+            square = pre * pre
+            root = (2.0 / jnp.pi) ** 0.5
+            bend = jnp.tanh(pre * (root + (root * 0.044715) * square))
+            half = 0.5 * pre
+            hid = (half + half * bend).astype(BF16)
+            slope = (0.5 + 0.5 * bend) + half * (1.0 - bend * bend) * (root + (3.0 * root * 0.044715) * square)
+            grad = (back * slope).astype(BF16)
+            hidden[rows, :] = hid
+            back_low[rows, :] = grad
+            acc[pl.ds(8 + step, 1), :] += column_sum(grad.astype(F32))
+            out_acc[rows, :] += dot_nn(hid, wo_ref[...])
+            back_acc[rows, :] += dot_nt(grad, wf_ref[...])
+            for s in range(steps):
+                hook(i, s)
+        fresh_feed[0] = dot_tn(hidden[...], cot_low[...]).astype(BF16)
+        fresh_feed[1] = dot_nn(normed_t[...], back_low[...]).astype(BF16)
+        for s in range(steps):
+            hook("made", s)
+
+    @pl.when(step == steps - 1)
+    def _():
+        for i in range(blocks):
+            rows = row_block(i)
+            keep = keep_column(lens_ref, place.my_row, i * span, span)
+            mid = middle[rows, :]
+            normed[rows, :] = (
+                keep * (mid + branch_scale * (out_acc[rows, :] + bo_ref[...]))
+            ).astype(BF16)
+            unit, inverse = normalise(mid)
+            back = back_acc[rows, :]
+            back_acc[rows, :] = jnp.zeros((span, width), F32)
+            acc[5:6, :] += column_sum(back * unit)
+            acc[6:7, :] += column_sum(back)
+            scaled = back * gain2_ref[...]
+            grad = keep * cot_ref[rows, :].astype(F32) + inverse * (
+                scaled - row_mean(scaled) - unit * row_mean(scaled * unit)
+            )
+            middle[rows, :] = grad
+            low = (branch_scale * grad).astype(BF16)
+            hidden[rows, :] = low
+            acc[7:8, :] += column_sum(low.astype(F32))
+            back_low[rows, :] = dot_nt(low, wp_ref[...]).astype(BF16)
+        hook("lo")
+        lo_back.start()
+        fresh_proj[0] = dot_tn(o_ref[...], hidden[...]).astype(BF16)
+        hook("proj")
+
+    @pl.when(step == steps)
+    def _():
+        fill_bias(lens_ref, place.my_row, bias, span)
+        for i in range(blocks):
+            rows = row_block(i)
+            unit, _ = normalise(x_ref[rows, :].astype(F32))
+            normed_t[:, rows] = (unit * gain1_ref[...] + shift1_ref[...]).T.astype(BF16)
+        hook("turn")
+
+    @pl.when(step >= steps)
+    def _():
+        group = pl.ds(pl.multiple_of((step - steps) * lanes, lanes), lanes)
+        grad_k, grad_v = out_acc.at[:, :lanes], out_acc.at[:, lanes : 2 * lanes]
+        grad_q = hidden.at[:, :lanes]
+        grad_k[...] = jnp.zeros_like(grad_k)
+        grad_v[...] = jnp.zeros_like(grad_v)
+        key_t[...] = k_ref[...].astype(F32).T.astype(BF16)
+        head_id = lax.broadcasted_iota(jnp.int32, (8, lanes), 0)
+        lane_id = lax.broadcasted_iota(jnp.int32, (8, lanes), 1)
+        member = ((lane_id >= head_id * HEAD) & (lane_id < (head_id + 1) * HEAD)).astype(F32)
+        for i in range(blocks):
+            rows = row_block(i)
+            count = (i + 1) * span
+            d_out = back_low[rows, group]
+            product = d_out.astype(F32) * o_ref[rows, group].astype(F32)
+            delta = lax.dot_general(
+                member, product, (((1,), (1,)), ((), ())),
+                precision=lax.Precision.HIGHEST, preferred_element_type=F32,
+            )
+            for h in range(lanes // HEAD):
+                pair = slice(h // 2 * 2 * HEAD, (h // 2 + 1) * 2 * HEAD)
+                own = slice(h * HEAD, (h + 1) * HEAD)
+                queries = q_ref[rows, pair] * head_row(h, HEAD ** (-0.5))
+                grads = d_out[:, pair] * head_row(h, 1.0)
+                scores = dot_nt(k_ref[:count, pair], queries) + bias[:count, rows]
+                probs = jnp.exp(scores - lse_ref[0, h : h + 1, rows])
+                grad_probs = dot_nt(v_ref[:count, pair], grads)
+                grad_scores = (probs * (grad_probs - delta[h : h + 1, :])).astype(BF16)
+                grad_v[:count, pair] += dot_nn(probs.astype(BF16), grads)
+                grad_k[:count, pair] += dot_nn(grad_scores, queries)
+                grad_q_t[own, rows] = dot_nn(key_t[own, :count], grad_scores)
+            for s in range(steps, steps + groups):
+                hook(i, s)
+        for i in range(blocks):
+            rows = row_block(i)
+            dq = (grad_q_t[:, rows].T * HEAD ** (-0.5)).astype(BF16)
+            grad_q[rows, :] = dq
+            dk = grad_k[rows, :].astype(BF16)
+            dv = grad_v[rows, :].astype(BF16)
+            acc[2:3, group] += column_sum(dq.astype(F32))
+            acc[3:4, group] += column_sum(dv.astype(F32))
+            back_acc[rows, :] += dot_nt(dq, wq_ref[...]) + dot_nt(dk, wk_ref[...]) + dot_nt(dv, wv_ref[...])
+        fresh_qkv[0] = dot_nn(normed_t[...], grad_q[...]).astype(BF16)
+        fresh_qkv[1] = dot_nn(normed_t[...], grad_k[...].astype(BF16)).astype(BF16)
+        fresh_qkv[2] = dot_nn(normed_t[...], grad_v[...].astype(BF16)).astype(BF16)
+        for s in range(steps, steps + groups):
+            hook("made", s)
+
+    @pl.when(step == steps + groups - 1)
+    def _():
+        for i in range(blocks):
+            rows = row_block(i)
+            unit, inverse = normalise(x_ref[rows, :].astype(F32))
+            back = back_acc[rows, :]
+            acc[0:1, :] += column_sum(back * unit)
+            acc[1:2, :] += column_sum(back)
+            scaled = back * gain1_ref[...]
+            grad = middle[rows, :] + inverse * (
+                scaled - row_mean(scaled) - unit * row_mean(scaled * unit)
+            )
+            cot_low[rows, :] = grad.astype(BF16)
+        dx_back.start()
+        hook("dx")
+        small.step(0)
+        for turn, (u, phase) in enumerate(tail):
+            units[u].step(phase)
+            if turn < 4:
+                small.step(turn + 1)
+        for turn in range(min(len(tail), 4), 4):
+            small.step(turn + 1)
+        small_out[...] = small.total()
+        lo_back.finish()
+        dx_back.finish()
+
+
+def body(
+    lens, o, x, cot, q, k, v, lse, rows, span, lines,
+    ln1_gain, ln1_bias, qkv_weight, proj_weight, proj_bias, ln2_gain, ln2_bias, fc_weight, fc_bias, out_weight, out_bias,
+):
+    tokens, width = x.shape
+    groups, heads, _ = lse.shape
+    lanes = width // groups
+    steps = fc_weight.shape[1] // width
+    shape = jax.ShapeDtypeStruct
+    once = pl.Buffered(1)
+    whole = lambda *dims: pl.BlockSpec(dims, lambda s: (0,) * len(dims), pipeline_mode=once)
+    act, vec, mat = whole(tokens, width), whole(1, width), whole(width, width)
+    feed_step = lambda s: jnp.minimum(s, steps - 1)
+    back_step = lambda s: jnp.maximum(s - steps, 0)
+    columns = lambda dims, first: pl.BlockSpec(dims, lambda s: (0, first + back_step(s)))
+    anywhere = pl.BlockSpec(memory_space=pl.ANY)
+    f32 = lambda *dims: pltpu.VMEM(dims, F32)
+    bf16 = lambda *dims: pltpu.VMEM(dims, BF16)
+    sem = lambda *dims: pltpu.SemaphoreType.DMA(dims)
+    unit_shapes = [(2, width, width)] * steps + [(1, width, width)] + [(3, width, lanes)] * groups
+    count = len(unit_shapes)
+    unit_scratch = []
+    for line, unit_shape in zip(lines, unit_shapes):
+        unit_scratch += Unit.scratch(line, *unit_shape)
+    return pl.pallas_call(
+        functools.partial(body_kernel, steps, groups, lines),
+        grid=(steps + groups,),
+        out_shape=(
+            shape((rows, span, width), BF16),
+            shape((rows, span, width), BF16),
+            shape((steps, 2, width, width), BF16),
+            shape((1, width, width), BF16),
+            shape((groups, 3, width, lanes), BF16),
+            shape((16, width), F32),
+        ),
+        in_specs=[
+            pl.BlockSpec(memory_space=pltpu.SMEM),
+            act, act, act, mat, vec, vec, vec,
+            pl.BlockSpec((width, width), lambda s: (0, feed_step(s))),
+            pl.BlockSpec((1, width), lambda s: (0, feed_step(s))),
+            pl.BlockSpec((width, width), lambda s: (feed_step(s), 0)),
+            vec, vec, vec,
+            columns((tokens, lanes), 0), columns((tokens, lanes), 0), columns((tokens, lanes), 0),
+            pl.BlockSpec((1, heads, tokens), lambda s: (back_step(s), 0, 0)),
+            columns((width, lanes), 0), columns((width, lanes), groups), columns((width, lanes), 2 * groups),
+        ],
+        out_specs=[anywhere] * 5 + [pl.BlockSpec((16, width), lambda s: (0, 0))],
+        scratch_shapes=[
+            f32(tokens, width), bf16(tokens, width), bf16(width, tokens), bf16(tokens, width),
+            f32(tokens, width), f32(tokens, width), bf16(tokens, width), bf16(tokens, width),
+            f32(tokens, tokens), bf16(lanes, tokens), f32(lanes, tokens),
+            bf16(2, width, width), bf16(1, width, width), bf16(3, width, lanes),
+            f32(4, 16, width), f32(3, 16, width), f32(4, 16, width),
+            sem(count, 16), sem(count, 16), sem(count), sem(6), sem(6), sem(2, 3), sem(2, 3), sem(2),
+        ] + unit_scratch,
+        compiler_params=pltpu.CompilerParams(
+            collective_id=0, has_side_effects=True, vmem_limit_bytes=VMEM_LIMIT
+        ),
+        name="body",
+    )(
+        lens, o, x, cot, proj_weight, proj_bias, ln2_gain, ln2_bias, fc_weight, fc_bias, out_weight, out_bias,
+        ln1_gain, ln1_bias, q, k, v, lse, qkv_weight, qkv_weight, qkv_weight,
+    )
+
+
+def finish_kernel(
+    feed_ref, proj_ref, qkv_ref, small_ref, dx_ref,
+    ln1_gain, ln1_bias, qkv_weight, qv_bias, proj_weight, proj_bias,
+    ln2_gain, ln2_bias, fc_weight, fc_bias, out_weight, out_bias, input_grad,
+):
+    width = small_ref.shape[1]
+    groups, _, _, lanes = qkv_ref.shape
+    out_weight[...] = feed_ref[0, 0].astype(F32)
+    fc_weight[...] = feed_ref[0, 1].astype(F32)
+    for g in range(groups):
+        qkv_weight[:, g * lanes : (g + 1) * lanes] = qkv_ref[g, 0].astype(F32)
+    proj_weight[...] = proj_ref[0].astype(F32)
+    input_grad[...] = dx_ref[...].astype(F32)
+
+    @pl.when((pl.program_id(0) == 0) & (pl.program_id(1) == 0))
+    def _():
+        for ref, first in (
+            (ln1_gain, 0), (ln1_bias, 1), (qv_bias, 2), (out_bias, 4),
+            (ln2_gain, 5), (ln2_bias, 6), (proj_bias, 7), (fc_bias, 8),
+        ):
+            for i in range(ref.shape[0] // width):
+                ref[i * width : (i + 1) * width] = small_ref[first + i]
+
+
+def finish(feed_sums, proj_sums, qkv_sums, small, dx):
+    steps, _, width, _ = feed_sums.shape
+    groups, _, _, lanes = qkv_sums.shape
+    rows, span, _ = dx.shape
+    half = width // 2
+    shape = lambda *dims: jax.ShapeDtypeStruct(dims, F32)
+    flat = lambda n: pl.BlockSpec((n * width,), lambda f, r: (0,))
+    third = lambda f: jnp.minimum(f, 2)
+    row = pl.BlockSpec((1, span // 2, width), lambda f, r: (jnp.minimum(f, rows - 1), jnp.where(f > rows - 1, 1, r), 0))
+    return pl.pallas_call(
+        finish_kernel,
+        grid=(steps, 2),
+        out_shape=(
+            shape(width), shape(width), shape(width, 3 * width), shape(2 * width),
+            shape(width, width), shape(width), shape(width), shape(width),
+            shape(width, steps * width), shape(steps * width), shape(steps * width, width), shape(width),
+            shape(rows, span, width),
+        ),
+        in_specs=[
+            pl.BlockSpec((1, 2, half, width), lambda f, r: (f, 0, r, 0)),
+            pl.BlockSpec((1, half, width), lambda f, r: (0, jnp.where(f == steps - 1, r, 0), 0)),
+            pl.BlockSpec((groups, 1, half, lanes), lambda f, r: (0, third(f), jnp.where(f > 2, 1, r), 0)),
+            pl.BlockSpec((16, width), lambda f, r: (0, 0)),
+            row,
+        ],
+        out_specs=[
+            flat(1), flat(1),
+            pl.BlockSpec((half, width), lambda f, r: (jnp.where(f > 2, 1, r), third(f))),
+            flat(2),
+            pl.BlockSpec((half, width), lambda f, r: (jnp.where(f == steps - 1, r, 0), 0)),
+            flat(1), flat(1), flat(1),
+            pl.BlockSpec((half, width), lambda f, r: (r, f)),
+            flat(steps),
+            pl.BlockSpec((half, width), lambda f, r: (2 * f + r, 0)),
+            flat(1),
+            row,
+        ],
+        compiler_params=pltpu.CompilerParams(vmem_limit_bytes=VMEM_LIMIT),
+        name="finish",
+    )(feed_sums, proj_sums, qkv_sums, small, dx)
+
+
+def by_rows(
+    tokens_in, lengths, ln1_gain, ln1_bias, qkv_weight, qv_bias, proj_weight, proj_bias,
+    ln2_gain, ln2_bias, fc_weight, fc_bias, out_weight, out_bias, cotangent,
+):
+    rows, span, width = tokens_in.shape
+    flat = lambda array: array.reshape(1, -1)
+    q, k, v, o, lse, x, cot = front(
+        lengths, tokens_in, cotangent, flat(ln1_gain), flat(ln1_bias), qkv_weight, flat(qv_bias)
+    )
+    steps, groups = fc_weight.shape[1] // width, lse.shape[0]
+    lines = (False,) * (steps + 1 + groups)
+    layer_out, dx, feed_sums, proj_sums, qkv_sums, small = body(
+        lengths, o, x, cot.reshape(x.shape), q, k, v, lse, rows, span, lines,
+        flat(ln1_gain), flat(ln1_bias), qkv_weight, proj_weight, flat(proj_bias), flat(ln2_gain), flat(ln2_bias),
+        fc_weight, flat(fc_bias), out_weight, flat(out_bias),
+    )
+    *grads, input_grad = finish(feed_sums, proj_sums, qkv_sums, small, dx)
+    return (layer_out, input_grad, *grads)
 
 
 def layer_norm(values, gain, shift):
@@ -409,4 +1313,5 @@
         P(),
         P(),
     )
-    return jax.shard_map(local, mesh=mesh, in_specs=in_specs, out_specs=out_specs, check_vma=False)
+    own_rows = mesh.shape["row"] == 8 and mesh.shape["seq"] == 4
+    return jax.shard_map(by_rows if own_rows else local, mesh=mesh, in_specs=in_specs, out_specs=out_specs, check_vma=False)

time: 766 us -> 340 us (0.44)
  Pallas kernels: 0 us -> 323 us
  waiting for transfers between devices: 250 us -> 0 us
  matrix products: 219 us -> 0 us
  blocking collectives: 109 us -> 0 us
  other arithmetic: 96.3 us -> 0 us
  local copies, waits for them, and re-layouts: 66.6 us -> 9.91 us
  between operations: 18 us -> 1.06 us
    pallas_call x0 -> x3, Pallas kernels: none -> 323 us  [the longest x1 244 us: body(): pl.pallas_call(functools.partial(body_kernel, steps, groups, lines), grid...]
    dot_general x19 -> x0, matrix products: 219 us -> none  [the longest x4 32.9 us: left_dot(): lax.dot_general(left, right, (((0,), (0,)), ((), ())), preferred_element_...]
    all_gather x8 -> x0, waiting for transfers between devices: 107 us -> none  [the longest x1 59.4 us: local(): key_piece = lax.all_gather(keys, 'seq', axis=1, tiled=True)]
    reduce_scatter x4 -> x0, waiting for transfers between devices: 73.3 us -> none  [the longest x1 45.1 us: local(): lax.psum_scatter(local_grads[2].astype(jnp.bfloat16), 'row', scatter_dime...]
    psum x1 -> x0, waiting for transfers between devices: 67.1 us -> none  [local(): lax.psum(shares[2].astype(jnp.bfloat16), 'seq').astype(jnp.float32)]
    unnamed x2 -> x0, blocking collectives: 58.6 us -> none
    convert_element_type x20 -> x0, other arithmetic: 42.9 us -> none  [the longest x1 7.37 us: local(): lax.all_gather(totals[8].astype(jnp.bfloat16), 'row', axis=0, tiled=True)]
    reduce_sum x11 -> x0, other arithmetic: 35.7 us -> none  [the longest x1 18.3 us: forward_update(): total = jnp.sum(weights, axis=-1)]
  transfers between devices with their start and end apart: 13 -> 0, of which waited for: 5 -> 0; matrix products, arithmetic and copies ran while one was open for 47% -> 0% of each run, Pallas kernels for 0% -> 0%
where the time goes in v2:
time: 340 us; the launch traced here: 334 us
  Pallas kernels  323 us (95%)
  local copies, waits for them, and re-layouts  9.91 us (3%)
    pallas_call x1, Pallas kernels, body(): pl.pallas_call(functools.partial(body_kernel, steps, groups, lines), grid...  244 us
    pallas_call x1, Pallas kernels, front(): pl.pallas_call(front_kernel, grid=(groups,), out_shape=(act, act, act, ac...  61.6 us
    pallas_call x1, Pallas kernels, finish(): pl.pallas_call(finish_kernel, grid=(steps, 2), out_shape=(shape(width), s...  17.4 us
    reshape x7, local copies, waits for them, and re-layouts, by_rows(): flat = lambda array: array.reshape(1, -1)  8.89 us

profile of v2, /device:TPU:0, one launch (start us, length us, event | category | flops | bytes accessed | tf_op | source)
XLA Modules:
  0.0 333.8 jit_solution(5118654973034264716)
XLA Ops:
  0.6 1.3 reshape.57.gain_ref.gain1_ref
  1.9 1.3 reshape.58.shift_ref.shift1_ref
  3.2 1.3 reshape.61.bp_ref
  4.4 1.3 reshape.62.gain2_ref
  5.7 1.3 reshape.63.shift2_ref
  7.0 1.3 reshape.65.bo_ref
  8.2 1.3 reshape.59.bq_ref.bv_ref
  9.5 61.6 %front.1 = (bf16[1024,768]{1,0:T(8,128)(2,1)}, bf16[1024,768]{1,0:T(8,128)(2,1)}, bf16[1024,768]{1,0:T(8,128)(2,1)}, bf16[1024,768]{1,0:T(8,128)(2,1)}, f32[3,8,...) custom-call(s32[3,8]{1,0:T(4,128)} %lens_ref.3, bf16[3,256,768]{2,1,0:T(8,128)(2,1)} %tokens_ref.1, ...), custom_call_target="tpu_custom_call" | custom-call | tf_op jit(solution)/shard_map/front/pallas_call | solution.py:273
  71.2 243.8 %body.1 = (bf16[3,256,768]{2,1,0:T(8,128)(2,1)}, bf16[3,256,768]{2,1,0:T(8,128)(2,1)}, bf16[4,2,768,768]{3,2,1,0:T(8,128)(2,1)}, bf16[1,768,768]{2,1,0:T(8,128)(...) custom-call(s32[3,8]{1,0:T(4,128)} %lens_ref.3, bf16[1024,768]{1,0:T(8,128)(2,1)} %get-tuple-element.40.o_ref, ...), custom_call_target="tpu_custom_call" | custom-call | tf_op jit(solution)/shard_map/body/pallas_call | solution.py:791
  315.0 0.0 copy-start
  315.0 17.4 %finish.1 = (f32[768]{0:T(1024)}, f32[768]{0:T(1024)}, f32[768,2304]{1,0:T(8,128)}, f32[1536]{0:T(1024)}, f32[768,768]{1,0:T(8,128)}, /*index=5*/f32[768]{0:T(10...) custom-call(bf16[4,2,768,768]{3,2,1,0:T(8,128)(2,1)} %get-tuple-elem, ...), custom_call_target="tpu_custom_call" | custom-call | tf_op jit(solution)/shard_map/finish/pallas_call | solution.py:865
  332.4 0.0 copy-done
  332.4 1.0 copy.30
Async XLA Ops:
  315.0 17.4 %copy-start = (bf16[3,256,768]{2,1,0:T(8,128)(2,1)S(1)}, bf16[3,256,768]{2,1,0:T(8,128)(2,1)}, u32[]{:S(2)}) copy-start(bf16[3,256,768]{2,1,0:T(8,128)(2,1)} %get-tuple-element.80) | copy-start | bytes 3538948

commit v3 on v2

--- a/solution.py
+++ b/solution.py
@@ -160,9 +160,9 @@
 
 
 def front_kernel(
-    lens_ref, tokens_ref, cot_in_ref, gain_ref, shift_ref, wq_ref, wk_ref, wv_ref, bq_ref, bv_ref,
+    lens_ref, tokens_ref, cot_in_ref, gain_ref, shift_ref, qv_bias_ref, wq_ref, wk_ref, wv_ref,
     q_ref, k_ref, v_ref, o_ref, lse_ref, x_ref, cot_ref,
-    arrived, normed, bias, value_t, out_t, send_sem, recv_sem, copy_sem,
+    arrived, normed, bias, value_t, out_t, vectors, send_sem, recv_sem, copy_sem,
 ):
     tokens, width = x_ref.shape
     lanes = wq_ref.shape[1]
@@ -201,7 +201,10 @@
     def _():
         place.greet_plane()
         start(0)
-        start(1)
+        vectors[0:1, :] = gain_ref[...].reshape(1, width)
+        vectors[1:2, :] = shift_ref[...].reshape(1, width)
+        for i in range(2):
+            vectors[2 + i : 3 + i, :] = qv_bias_ref[i * width : (i + 1) * width].reshape(1, width)
         fill_bias(lens_ref, place.my_row, bias, block)
 
         @pl.when(jnp.logical_not(place.active))
@@ -209,44 +212,61 @@
             arrived[...] = jnp.zeros_like(arrived)
 
         finish(0)
+        start(1)
 
         def one(i, carry):
             rows = pl.ds(pl.multiple_of(i * block, block), block)
             x = arrived[i]
             x_ref[rows, :] = x
             unit, _ = normalise(x.astype(F32))
-            normed[rows, :] = (unit * gain_ref[...] + shift_ref[...]).astype(BF16)
+            normed[rows, :] = (unit * vectors[0:1, :] + vectors[1:2, :]).astype(BF16)
             return carry
 
         lax.fori_loop(0, blocks, one, 0)
+
+    group = pl.ds(pl.multiple_of(pl.program_id(0) * lanes, lanes), lanes)
 
     def project(i, carry):
         rows = pl.ds(pl.multiple_of(i * block, block), block)
         h1 = normed[rows, :]
-        q_ref[rows, :] = (dot_nn(h1, wq_ref[...]) + bq_ref[...]).astype(BF16)
+        q_ref[rows, :] = (dot_nn(h1, wq_ref[...]) + vectors[2:3, group]).astype(BF16)
         k_ref[rows, :] = dot_nn(h1, wk_ref[...]).astype(BF16)
-        values = dot_nn(h1, wv_ref[...]) + bv_ref[...]
+        values = dot_nn(h1, wv_ref[...]) + vectors[3:4, group]
         v_ref[rows, :] = values.astype(BF16)
         value_t[:, rows] = values.T.astype(BF16)
         return carry
 
     lax.fori_loop(0, blocks, project, 0)
 
-    for i in range(blocks):
-        rows = slice(i * block, (i + 1) * block)
-        count = (i + 1) * block
-        for h in range(lanes // HEAD):
-            pair = slice(h // 2 * 2 * HEAD, (h // 2 + 1) * 2 * HEAD)
-            own = slice(h * HEAD, (h + 1) * HEAD)
-            queries = q_ref[rows, pair] * head_row(h, HEAD ** (-0.5))
-            scores = dot_nt(k_ref[:count, pair], queries) + bias[:count, rows]
-            top = jnp.max(scores, axis=0, keepdims=True)
-            probs = jnp.exp(scores - top)
-            total = jnp.sum(probs, axis=0, keepdims=True)
-            mixed = dot_nn(value_t[own, :count], probs.astype(BF16))
-            out_t[own, :] = mixed * (1.0 / total)
-            lse_ref[0, h : h + 1, rows] = top + jnp.log(total)
-        o_ref[rows, :] = out_t[...].T.astype(BF16)
+    heads = lanes // HEAD
+    turns = [(i, h) for i in range(blocks) for h in range(heads)]
+
+    def score(i, h):
+        rows, count = slice(i * block, (i + 1) * block), (i + 1) * block
+        pair = slice(h // 2 * 2 * HEAD, (h // 2 + 1) * 2 * HEAD)
+        queries = q_ref[rows, pair] * head_row(h, HEAD ** (-0.5))
+        return dot_nt(k_ref[:count, pair], queries) + bias[:count, rows]
+
+    def mix(i, h, probs, total):
+        rows, count = slice(i * block, (i + 1) * block), (i + 1) * block
+        own = slice(h * HEAD, (h + 1) * HEAD)
+        out_t[own, :] = dot_nn(value_t[own, :count], probs) * (1.0 / total)
+        if h == heads - 1:
+            o_ref[rows, :] = out_t[...].T.astype(BF16)
+
+    following, waiting = score(*turns[0]), None
+    for turn, (i, h) in enumerate(turns):
+        scores = following
+        if turn + 1 < len(turns):
+            following = score(*turns[turn + 1])
+        if waiting is not None:
+            mix(*waiting)
+        top = jnp.max(scores, axis=0, keepdims=True)
+        probs = jnp.exp(scores - top)
+        total = jnp.sum(probs, axis=0, keepdims=True)
+        lse_ref[0, h : h + 1, i * block : (i + 1) * block] = top + jnp.log(total)
+        waiting = (i, h, probs.astype(BF16), total)
+    mix(*waiting)
 
     @pl.when(pl.program_id(0) == pl.num_programs(0) - 1)
     def _():
@@ -263,7 +283,7 @@
     rows, span, width = tokens_in.shape
     spans = lax.axis_size("seq")
     tokens = spans * span
-    lanes = 256 if width > 256 else 128
+    lanes = width // 3
     groups = width // lanes
     heads = max(8, lanes // HEAD)
     whole = lambda shape: pl.BlockSpec(shape, lambda g: (0,) * len(shape))
@@ -281,13 +301,12 @@
             pl.BlockSpec(memory_space=pltpu.SMEM),
             pl.BlockSpec(memory_space=pl.ANY),
             pl.BlockSpec(memory_space=pl.ANY),
-            whole((1, width)),
-            whole((1, width)),
+            whole((width,)),
+            whole((width,)),
+            whole((2 * width,)),
             columns((width, lanes), 0),
             columns((width, lanes), groups),
             columns((width, lanes), 2 * groups),
-            columns((1, lanes), 0),
-            columns((1, lanes), groups),
         ],
         out_specs=[columns((tokens, lanes), 0)] * 4
         + [
@@ -301,151 +320,115 @@
             pltpu.VMEM((tokens, tokens), F32),
             pltpu.VMEM((lanes, tokens), BF16),
             pltpu.VMEM((lanes, span), F32),
+            pltpu.VMEM((8, width), F32),
             sem(2, 3), sem(2, 3), sem(2),
         ],
         compiler_params=pltpu.CompilerParams(
             collective_id=1, has_side_effects=True, vmem_limit_bytes=VMEM_LIMIT
         ),
         name="front",
-    )(lens, tokens_in, cotangent, gain, shift, qkv_weight, qkv_weight, qkv_weight, qv_bias, qv_bias)
-
-
-class Unit:
-    slots = (0, 1, 4, 5, 8, 11, 12, 15)
-
-    def __init__(self, place, line, fresh, recv, part, out, send_sem, recv_sem, copy_sem):
-        self.place, self.line, self.fresh, self.recv, self.part, self.out = place, line, fresh, recv, part, out
+    )(lens, tokens_in, cotangent, gain, shift, qv_bias, qkv_weight, qkv_weight, qkv_weight)
+
+
+class Units:
+    slots = (0, 1, 2, 3, 6, 9, 10, 11)
+
+    def __init__(self, place, fresh, out, recv0, recv1, recv2, recv3, part, send_sem, recv_sem, copy_sem):
+        self.place, self.fresh, self.out, self.part = place, fresh, out, part
+        self.recv = (recv0, recv1, recv2, recv3)
         self.send_sem, self.recv_sem, self.copy_sem = send_sem, recv_sem, copy_sem
         _, rows, columns = fresh.shape
-        self.half, self.wide = rows // 2, columns // 2
-        self.own = place.core * self.half
-        self.away = self.half - self.own
+        self.size = (rows // 2, rows // 4, rows // 8, rows // 16)
+        self.wide = columns // 2
+        bits = (place.core, place.first_bit, place.second_bit)
+        self.own = [bit * size for bit, size in zip(bits, self.size)]
+        self.away = [(1 - bit) * size for bit, size in zip(bits, self.size)]
 
     @staticmethod
-    def scratch(line, n, rows, columns):
+    def scratch(count, n, rows, columns):
         vmem = lambda *shape: pltpu.VMEM(shape, BF16)
-        wide = columns // 2
-        if line:
-            shapes = ((rows // 2, columns), (3, rows // 8, columns), (rows // 16, columns), (rows // 16, wide))
-        else:
-            shapes = ((rows // 2, columns), (rows // 4, columns), (rows // 8, columns), (3, rows // 16, wide))
-        return [vmem(*shape[:-2], n, *shape[-2:]) for shape in shapes] + [vmem(n, rows // 16, wide)]
+        sem = lambda *shape: pltpu.SemaphoreType.DMA(shape)
+        return [
+            vmem(count, n, rows // 2, columns), vmem(count, n, rows // 4, columns), vmem(count, n, rows // 8, columns),
+            vmem(count, 3, n, rows // 16, columns // 2), vmem(count, n, rows // 16, columns // 2),
+            sem(count, 12), sem(count, 12), sem(count),
+        ]
 
     def rows(self, start, count):
-        return pl.ds(pl.multiple_of(start, self.half // 8), count)
-
-    def columns(self, which):
-        return pl.ds(pl.multiple_of(which * self.wide, self.wide), self.wide)
-
-    def stage(self, number):
-        place, half = self.place, self.half
-        bit1, bit2 = place.first_bit, place.second_bit
-        every = slice(None)
-        if self.line:
-            if number == 1:
-                size = half // 4
-                part = lambda z: (self.rows(z * size, size), every)
-                others = [(place.along_z(hop), part(lax.rem(place.z + hop, 4))) for hop in (1, 2, 3)]
-                return others, part(place.z)
-            if number == 2:
-                size = half // 8
-                return [(place.first, (self.rows((1 - bit1) * size, size), every))], (self.rows(bit1 * size, size), every)
-            return [(place.second, (every, self.columns(1 - bit2)))], (every, self.columns(bit2))
-        if number < 3:
-            size = half // 2 ** number
-            bit, other = ((bit1, place.first), (bit2, place.second))[number - 1]
-            return [(other, (self.rows((1 - bit) * size, size), every))], (self.rows(bit * size, size), every)
-        size = half // 8
-        part = lambda z: (self.rows(lax.div(z, 2) * size, size), self.columns(lax.rem(z, 2)))
-        others = [(place.along_z(hop), part(lax.rem(place.z + hop, 4))) for hop in (1, 2, 3)]
-        return others, part(place.z)
-
-    def region(self, number):
-        place, half = self.place, self.half
-        every = slice(None)
-        if number == 0:
-            return self.rows(self.own, half), every
-        if self.line:
-            start = self.own + place.z * (half // 4)
-            if number == 1:
-                return self.rows(start, half // 4), every
-            rows = self.rows(start + place.first_bit * (half // 8), half // 8)
-            return rows, every if number == 2 else self.columns(place.second_bit)
-        start = self.own + place.first_bit * (half // 2)
-        if number == 1:
-            return self.rows(start, half // 2), every
-        start = start + place.second_bit * (half // 4)
-        if number == 2:
-            return self.rows(start, half // 4), every
-        return self.rows(start + lax.div(place.z, 2) * (half // 8), half // 8), self.columns(lax.rem(place.z, 2))
-
-    def held(self, number):
-        if number == 1 and self.line:
-            return self.recv[1].at[0]
-        return self.recv[number]
-
-    def copies(self, phase):
+        return pl.ds(pl.multiple_of(start, self.size[3]), count)
+
+    def piece(self, start, z):
+        columns = pl.ds(pl.multiple_of(lax.rem(z, 2) * self.wide, self.wide), self.wide)
+        return self.rows(start + lax.div(z, 2) * self.size[3], self.size[3]), columns
+
+    def copies(self, phase, u):
+        place, out, size, own = self.place, self.out, self.size, self.own
         first = self.slots[phase]
-        sems = lambda i: (self.send_sem.at[first + i], self.recv_sem.at[first + i])
+        sems = lambda i: (self.send_sem.at[u, first + i], self.recv_sem.at[u, first + i])
+        hops = (1, 2, 3)
         if phase == 0:
-            return [send(self.fresh.at[:, self.rows(self.away, self.half)], self.recv[0], *sems(0), self.place.sibling)]
-        if phase < 4:
-            others, _ = self.stage(phase)
-            source, target = self.held(phase - 1), self.recv[phase]
+            return [send(self.fresh.at[:, self.rows(self.away[0], size[0])], self.recv[0].at[u], *sems(0), place.sibling)]
+        if phase < 3:
+            source = self.recv[phase - 1].at[u, :, self.rows(self.away[phase], size[phase])]
+            return [send(source, self.recv[phase].at[u], *sems(0), (place.first, place.second)[phase - 1])]
+        if phase == 3:
             return [
-                send(source.at[:, *part], target.at[i] if len(others) > 1 else target, *sems(i), other)
-                for i, (other, part) in enumerate(others)
+                send(
+                    self.recv[2].at[u, :, *self.piece(0, lax.rem(place.z + hop, 4))], self.recv[3].at[u, hop - 1],
+                    *sems(hop - 1), place.along_z(hop),
+                )
+                for hop in hops
             ]
-        if phase == 7:
-            others = [(self.place.sibling, None)]
-        else:
-            others, _ = self.stage(7 - phase)
-        where = self.out.at[:, *self.region(7 - phase)]
-        source = self.part if phase == 4 else where
-        return [send(source, where, *sems(i), other) for i, (other, _) in enumerate(others)]
-
-    def local(self):
-        return pltpu.make_async_copy(self.part, self.out.at[:, *self.region(3)], self.copy_sem)
-
-    def add(self, phase):
-        if phase == 0:
-            source, target, more = self.fresh.at[:, self.rows(self.own, self.half)], self.recv[0], []
-        else:
-            others, part = self.stage(phase)
-            source, target, more = self.held(phase - 1).at[:, *part], self.recv[phase], []
-            if len(others) > 1:
-                target, more = self.recv[phase].at[0], [self.recv[phase].at[1], self.recv[phase].at[2]]
-        result = self.part if phase == 3 else target
-        n, count, _ = target.shape
-        step = self.half // 8
+        if phase == 4:
+            where = out.at[u, :, *self.piece(own[0] + own[1] + own[2], place.z)]
+            return [send(self.part.at[u], where, *sems(hop - 1), place.along_z(hop)) for hop in hops]
+        start, count, other = {
+            5: (own[0] + own[1] + own[2], size[2], place.second),
+            6: (own[0] + own[1], size[1], place.first),
+            7: (own[0], size[0], place.sibling),
+        }[phase]
+        where = out.at[u, :, self.rows(start, count)]
+        return [send(where, where, *sems(0), other)]
+
+    def local(self, u):
+        where = self.out.at[u, :, *self.piece(self.own[0] + self.own[1] + self.own[2], self.place.z)]
+        return pltpu.make_async_copy(self.part.at[u], where, self.copy_sem.at[u])
+
+    def add(self, phase, u):
+        step = self.size[3]
+        if phase == 3:
+            rows, columns = self.piece(0, self.place.z)
+            total = self.recv[2][u, :, rows, columns].astype(F32)
+            for hop in range(3):
+                total = total + self.recv[3][u, hop].astype(F32)
+            self.part[u] = total.astype(BF16)
+            return
+        source = self.fresh if phase == 0 else self.recv[phase - 1].at[u]
+        target = self.recv[phase].at[u]
 
         def one(i, carry):
-            rows = self.rows(i * step, step)
-            for panel in range(n):
-                total = source[panel, rows, :].astype(F32) + target[panel, rows, :].astype(F32)
-                for other in more:
-                    total = total + other[panel, rows, :].astype(F32)
-                result[panel, rows, :] = total.astype(BF16)
+            here = self.rows(i * step, step)
+            there = self.rows(self.own[phase] + i * step, step)
+            for panel in range(self.fresh.shape[0]):
+                total = source[panel, there, :].astype(F32) + target[panel, here, :].astype(F32)
+                target[panel, here, :] = total.astype(BF16)
             return carry
 
-        if count == step:
-            one(0, 0)
-        else:
-            lax.fori_loop(0, count // step, one, 0)
-
-    def step(self, phase):
+        lax.fori_loop(0, self.size[phase] // step, one, 0)
+
+    def step(self, phase, u):
         if phase > 0:
-            for copy in self.copies(phase - 1):
+            for copy in self.copies(phase - 1, u):
                 copy.wait()
             if phase == 5:
-                self.local().wait()
+                self.local(u).wait()
         if 0 < phase < 5:
-            self.add(phase - 1)
+            self.add(phase - 1, u)
         if phase < 8:
-            for copy in self.copies(phase):
+            for copy in self.copies(phase, u):
                 copy.start()
         if phase == 4:
-            self.local().start()
+            self.local(u).start()
 
 
 class Exchange:
@@ -480,64 +463,62 @@
         pl.when(self.place.active)(self.local().wait)
 
 
-def plan(hooks, sizes, lines, made):
+def plan(hooks, sizes, made):
     free = {"core": 0.0, "plane": 0.0, "line": 0.0}
-    now, flight, plans, ready = 0.0, {}, {}, {}
-
-    def work(unit, phase):
-        size, line = sizes[unit], lines[unit]
-        if phase in (0, 7):
-            return "core", size / 2 / 0.6
-        stage = phase if phase < 4 else 7 - phase
-        if line:
-            return (("line", size / 0.094), ("plane", size / 16 / 0.094), ("plane", size / 32 / 0.094))[stage - 1]
-        return (("plane", size / 4 / 0.094), ("plane", size / 8 / 0.094), ("line", size / 4 / 0.094))[stage - 1]
+    delay = {"core": 1.5, "plane": 3.5, "line": 3.0}
+    now, flight, plans = 0.0, {}, {}
 
     def go(unit, phase):
         nonlocal now
-        now += 0.1 + (sizes[unit] / 2 ** phase * 0.5 if 0 < phase < 4 else 0.0)
+        now += 0.3
         if phase == 8:
-            del flight[unit]
+            flight[unit] = (8, 1e9)
             return
-        kind, time = work(unit, phase)
+        kind = ("core", "plane", "plane", "line")[min(phase, 7 - phase)]
+        time = sizes[unit] * (0.5 / 0.6, 0.25 / 0.094, 0.125 / 0.094, 0.25 / 0.094)[min(phase, 7 - phase)]
         begin = max(now, free[kind])
         free[kind] = begin + time
-        flight[unit] = (phase, begin + time + 1.5)
+        flight[unit] = (phase, begin + time + delay[kind])
 
     for name, compute in hooks:
         now += compute
         plans[name] = []
-        for unit in sorted(flight):
+        for unit in sorted(flight, key=lambda u: flight[u][1]):
             phase, end = flight[unit]
-            if end <= now + 0.3:
+            if end <= now + 0.5:
                 plans[name].append((unit, phase + 1))
                 go(unit, phase + 1)
         for unit, hook in made.items():
             if hook == name:
                 plans[name].append((unit, 0))
                 go(unit, 0)
-                ready[unit] = now
         if name in ("lo", "dx"):
             free["plane"] = max(now, free["plane"]) + 16.0
-    tail = []
-    while flight:
-        unit = min(flight, key=lambda u: flight[u][1])
-        phase, end = flight[unit]
-        now = max(now, end)
-        tail.append((unit, phase + 1))
-        go(unit, phase + 1)
-    return plans, tail, now
+    return plans, {unit: phase + 1 for unit, (phase, _) in flight.items()}, now
+
+
+def timetable(steps, groups):
+    hooks = []
+    for s in range(steps):
+        hooks += [(("early", s), 14.0 if s == 0 else 3.0), (("late", s), 3.0), (("fed", s), 2.6)]
+    hooks += [("lo", 7.0), ("proj", 1.5), ("turn", 3.0)]
+    for s in range(steps, steps + groups):
+        hooks += [(("low", s), 5.0), (("high", s), 3.5), (("made", s), 2.5)]
+    hooks.append(("dx", 3.0))
+    made = {s: ("fed", s) for s in range(steps)}
+    made[steps] = "proj"
+    made.update({steps + 1 + g: ("made", steps + g) for g in range(groups)})
+    return hooks, made
 
 
 def body_kernel(
-    steps, groups, lines,
+    steps, groups,
     lens_ref, o_ref, x_ref, cot_ref, wp_ref, bp_ref, gain2_ref, shift2_ref, wf_ref, bf_ref, wo_ref, bo_ref,
     gain1_ref, shift1_ref, q_ref, k_ref, v_ref, lse_ref, wq_ref, wk_ref, wv_ref,
-    lo_out, dx_out, feed_out, proj_out, qkv_out, small_out,
-    middle, normed, normed_t, cot_low, out_acc, back_acc, hidden, back_low, bias, key_t, grad_q_t,
-    fresh_feed, fresh_proj, fresh_qkv, sums, small_recv, line_sums,
-    unit_send, unit_recv, unit_copy, small_send, small_recv_sem, out_send, out_recv, out_copy,
-    *unit_scratch,
+    lo_out, dx_out, feed_out, rest_out, small_out,
+    middle, normed, normed_t, cot_low, out_acc, back_acc, hidden, back_low, bias, key_t, grad_q_t, delta, vectors,
+    fresh_feed, fresh_rest, sums, small_recv, line_sums,
+    small_send, small_recv_sem, out_send, out_recv, out_copy, *unit_scratch,
 ):
     tokens, width = x_ref.shape
     lanes = wq_ref.shape[1]
@@ -547,60 +528,51 @@
     place = Place()
     acc = sums.at[0]
 
-    units = []
-    for u in range(steps + 1 + groups):
-        if u < steps:
-            fresh, out = fresh_feed, feed_out.at[u]
-        elif u == steps:
-            fresh, out = fresh_proj, proj_out
-        else:
-            fresh, out = fresh_qkv, qkv_out.at[u - steps - 1]
-        buffers = unit_scratch[5 * u : 5 * u + 5]
-        units.append(Unit(
-            place, lines[u], fresh, buffers[:4], buffers[4], out, unit_send.at[u], unit_recv.at[u], unit_copy.at[u]
-        ))
+    fed = Units(place, fresh_feed, feed_out, *unit_scratch[:8])
+    rest = Units(place, fresh_rest, rest_out, *unit_scratch[8:])
     small = SmallReducer(place, sums, small_recv, line_sums, small_send, small_recv_sem)
     lo_back = Exchange(place, normed, lo_out, out_send.at[0], out_recv.at[0], out_copy.at[0])
     dx_back = Exchange(place, cot_low, dx_out, out_send.at[1], out_recv.at[1], out_copy.at[1])
 
-    hooks = []
-    for s in range(steps):
-        if s == 0:
-            hooks.append(("begin", 5.0))
-        hooks += [((s, i), 2.0) for i in range(blocks)] + [((s, "made"), 3.0)]
-        if s == steps - 1:
-            hooks += [("lo", 5.0), ("proj", 2.0)]
-    for s in range(steps, steps + groups):
-        if s == steps:
-            hooks.append(("turn", 2.0))
-        hooks += [((s, i), 1.0 * (i + 1)) for i in range(blocks)] + [((s, "made"), 4.5)]
-    hooks.append(("dx", 2.0))
-    made = {u: (u, "made") for u in range(steps)}
-    made[steps] = "proj"
-    made.update({steps + 1 + g: (steps + g, "made") for g in range(groups)})
-    megabytes = lambda ref: ref.shape[0] * ref.shape[1] * ref.shape[2] * 2e-6
-    plans, tail, _ = plan(hooks, [megabytes(unit.fresh) for unit in units], lines, made)
+    hooks, made = timetable(steps, groups)
+    panel = width * width * 2e-6
+    count = steps + 1 + groups
+    plans, left, _ = plan(hooks, [2 * panel] * steps + [panel] * (1 + groups), made)
     order = [name for name, _ in hooks]
-    first = {u: order.index(name) for name, actions in plans.items() for u, phase in actions if phase == 1}
-    for u in [*range(steps - 1), *range(steps + 1, steps + groups)]:
-        assert first[u] < order.index(made[u + 1])
-
-    def hook(name, where=None):
-        actions = plans[name if where is None else (where, name)]
-        if not actions:
+    freed = {u: order.index(name) for name, actions in plans.items() for u, phase in actions if phase == 1}
+    for u in [*range(steps - 1), *range(steps, steps + groups)]:
+        assert freed[u] < order.index(made[u + 1])
+
+    def chosen(pairs, index):
+        value, found = jnp.int32(0), jnp.int32(0)
+        for key, item in pairs:
+            hit = (index == key).astype(jnp.int32)
+            value, found = value + hit * item, found + hit
+        return value, found > 0
+
+    def hook(name):
+        if name in plans:
+            for u, phase in plans[name]:
+                units, index = (fed, u) if u < steps else (rest, u - steps)
+                units.step(phase, index)
             return
-
-        def act():
-            for u, phase in actions:
-                units[u].step(phase)
-
-        if where is None:
-            act()
-        else:
-            pl.when(step == where)(act)
-
-    def row_block(i):
-        return slice(i * span, (i + 1) * span)
+        seen, bodies = {}, {}
+        for s in range(steps + groups):
+            for place_in_list, (u, phase) in enumerate(plans.get((name, s), [])):
+                kind = (u < steps, phase)
+                turn = seen[kind, s] = seen.get((kind, s), -1) + 1
+                bodies.setdefault((*kind, turn), []).append((s, u if u < steps else u - steps))
+        for (is_fed, phase, _), pairs in sorted(bodies.items(), key=lambda item: -item[0][1]):
+            index, found = chosen(pairs, step)
+            pl.when(found)(functools.partial((fed if is_fed else rest).step, phase, index))
+
+    def each(body, first=0, last=blocks):
+        def run(i, carry):
+            start = pl.multiple_of(i * span, span)
+            body(start, pl.ds(start, span))
+            return carry
+
+        lax.fori_loop(first, last, run, 0)
 
     def column_sum(values):
         return jnp.sum(values, axis=0, keepdims=True)
@@ -608,29 +580,33 @@
     @pl.when(step == 0)
     def _():
         place.greet()
-        place_sums = jnp.zeros_like(acc)
-        acc[...] = place_sums
-        for i in range(blocks):
-            rows = row_block(i)
-            attn = dot_nn(o_ref[rows, :], wp_ref[...]) + bp_ref[...]
+        acc[...] = jnp.zeros_like(acc)
+        for i, ref in enumerate((bp_ref, gain2_ref, shift2_ref, bo_ref, gain1_ref, shift1_ref)):
+            vectors[i : i + 1, :] = ref[...].reshape(1, width)
+        for f in range(steps):
+            vectors[8 + f : 9 + f, :] = bf_ref[f * width : (f + 1) * width].reshape(1, width)
+
+        def begin(start, rows):
+            attn = dot_nn(o_ref[rows, :], wp_ref[...]) + vectors[0:1, :]
             mid = x_ref[rows, :].astype(F32) + branch_scale * attn
             middle[rows, :] = mid
             unit, _ = normalise(mid)
-            h2 = unit * gain2_ref[...] + shift2_ref[...]
+            h2 = unit * vectors[1:2, :] + vectors[2:3, :]
             normed[rows, :] = h2.astype(BF16)
             normed_t[:, rows] = h2.T.astype(BF16)
-            keep = keep_column(lens_ref, place.my_row, i * span, span)
+            keep = keep_column(lens_ref, place.my_row, start, span)
             low = (branch_scale * (keep * cot_ref[rows, :].astype(F32))).astype(BF16)
             cot_low[rows, :] = low
             acc[4:5, :] += column_sum(low.astype(F32))
             out_acc[rows, :] = jnp.zeros((span, width), F32)
             back_acc[rows, :] = jnp.zeros((span, width), F32)
 
+        each(begin)
+
     @pl.when(step < steps)
     def _():
-        for i in range(blocks):
-            rows = row_block(i)
-            pre = dot_nn(normed[rows, :], wf_ref[...]) + bf_ref[...]
+        def chunk(start, rows):
+            pre = dot_nn(normed[rows, :], wf_ref[...]) + vectors[pl.ds(8 + step, 1), :]
             back = dot_nt(cot_low[rows, :], wo_ref[...])
             square = pre * pre
             root = (2.0 / jnp.pi) ** 0.5
@@ -644,28 +620,29 @@
             acc[pl.ds(8 + step, 1), :] += column_sum(grad.astype(F32))
             out_acc[rows, :] += dot_nn(hid, wo_ref[...])
             back_acc[rows, :] += dot_nt(grad, wf_ref[...])
-            for s in range(steps):
-                hook(i, s)
+
+        each(chunk, 0, blocks // 2)
+        hook("early")
+        each(chunk, blocks // 2, blocks)
+        hook("late")
         fresh_feed[0] = dot_tn(hidden[...], cot_low[...]).astype(BF16)
         fresh_feed[1] = dot_nn(normed_t[...], back_low[...]).astype(BF16)
-        for s in range(steps):
-            hook("made", s)
+        hook("fed")
 
     @pl.when(step == steps - 1)
     def _():
-        for i in range(blocks):
-            rows = row_block(i)
-            keep = keep_column(lens_ref, place.my_row, i * span, span)
+        def end(start, rows):
+            keep = keep_column(lens_ref, place.my_row, start, span)
             mid = middle[rows, :]
             normed[rows, :] = (
-                keep * (mid + branch_scale * (out_acc[rows, :] + bo_ref[...]))
+                keep * (mid + branch_scale * (out_acc[rows, :] + vectors[3:4, :]))
             ).astype(BF16)
             unit, inverse = normalise(mid)
             back = back_acc[rows, :]
             back_acc[rows, :] = jnp.zeros((span, width), F32)
             acc[5:6, :] += column_sum(back * unit)
             acc[6:7, :] += column_sum(back)
-            scaled = back * gain2_ref[...]
+            scaled = back * vectors[1:2, :]
             grad = keep * cot_ref[rows, :].astype(F32) + inverse * (
                 scaled - row_mean(scaled) - unit * row_mean(scaled * unit)
             )
@@ -674,56 +651,83 @@
             hidden[rows, :] = low
             acc[7:8, :] += column_sum(low.astype(F32))
             back_low[rows, :] = dot_nt(low, wp_ref[...]).astype(BF16)
+
+        each(end)
         hook("lo")
         lo_back.start()
-        fresh_proj[0] = dot_tn(o_ref[...], hidden[...]).astype(BF16)
+        fresh_rest[0] = dot_tn(o_ref[...], hidden[...]).astype(BF16)
         hook("proj")
 
     @pl.when(step == steps)
     def _():
         fill_bias(lens_ref, place.my_row, bias, span)
-        for i in range(blocks):
-            rows = row_block(i)
+
+        def turn(start, rows):
             unit, _ = normalise(x_ref[rows, :].astype(F32))
-            normed_t[:, rows] = (unit * gain1_ref[...] + shift1_ref[...]).T.astype(BF16)
+            normed_t[:, rows] = (unit * vectors[4:5, :] + vectors[5:6, :]).T.astype(BF16)
+
+        each(turn)
         hook("turn")
 
     @pl.when(step >= steps)
     def _():
         group = pl.ds(pl.multiple_of((step - steps) * lanes, lanes), lanes)
         grad_k, grad_v = out_acc.at[:, :lanes], out_acc.at[:, lanes : 2 * lanes]
-        grad_q = hidden.at[:, :lanes]
+        grad_q, d_out = hidden.at[:, :lanes], hidden.at[:, lanes : 2 * lanes]
         grad_k[...] = jnp.zeros_like(grad_k)
         grad_v[...] = jnp.zeros_like(grad_v)
+        grad_q_t[...] = jnp.zeros_like(grad_q_t)
         key_t[...] = k_ref[...].astype(F32).T.astype(BF16)
         head_id = lax.broadcasted_iota(jnp.int32, (8, lanes), 0)
         lane_id = lax.broadcasted_iota(jnp.int32, (8, lanes), 1)
         member = ((lane_id >= head_id * HEAD) & (lane_id < (head_id + 1) * HEAD)).astype(F32)
-        for i in range(blocks):
-            rows = row_block(i)
-            count = (i + 1) * span
-            d_out = back_low[rows, group]
-            product = d_out.astype(F32) * o_ref[rows, group].astype(F32)
-            delta = lax.dot_general(
+
+        def prepare(start, rows):
+            grads = back_low[rows, group]
+            d_out[rows, :] = grads
+            product = grads.astype(F32) * o_ref[rows, group].astype(F32)
+            delta[:, rows] = lax.dot_general(
                 member, product, (((1,), (1,)), ((), ())),
                 precision=lax.Precision.HIGHEST, preferred_element_type=F32,
             )
-            for h in range(lanes // HEAD):
+
+        each(prepare)
+        heads = lanes // HEAD
+
+        def tile(t, carry):
+            i = sum((t >= b * (b + 1) // 2).astype(jnp.int32) for b in range(1, blocks))
+            first = pl.multiple_of(i * span, span)
+            key_first = pl.multiple_of((t - lax.div(i * (i + 1), 2)) * span, span)
+            rows, keys = pl.ds(first, span), pl.ds(key_first, span)
+            mask = bias[keys, rows]
+
+            def start(h):
+                pair = slice(h // 2 * 2 * HEAD, (h // 2 + 1) * 2 * HEAD)
+                queries = q_ref[rows, pair] * head_row(h, HEAD ** (-0.5))
+                grads = d_out[rows, pair] * head_row(h, 1.0)
+                return queries, grads, dot_nt(k_ref[keys, pair], queries) + mask, dot_nt(v_ref[keys, pair], grads)
+
+            following = start(0)
+            for h in range(heads):
                 pair = slice(h // 2 * 2 * HEAD, (h // 2 + 1) * 2 * HEAD)
                 own = slice(h * HEAD, (h + 1) * HEAD)
-                queries = q_ref[rows, pair] * head_row(h, HEAD ** (-0.5))
-                grads = d_out[:, pair] * head_row(h, 1.0)
-                scores = dot_nt(k_ref[:count, pair], queries) + bias[:count, rows]
+                queries, grads, scores, grad_probs = following
+                if h + 1 < heads:
+                    following = start(h + 1)
                 probs = jnp.exp(scores - lse_ref[0, h : h + 1, rows])
-                grad_probs = dot_nt(v_ref[:count, pair], grads)
-                grad_scores = (probs * (grad_probs - delta[h : h + 1, :])).astype(BF16)
-                grad_v[:count, pair] += dot_nn(probs.astype(BF16), grads)
-                grad_k[:count, pair] += dot_nn(grad_scores, queries)
-                grad_q_t[own, rows] = dot_nn(key_t[own, :count], grad_scores)
-            for s in range(steps, steps + groups):
-                hook(i, s)
-        for i in range(blocks):
-            rows = row_block(i)
+                grad_scores = (probs * (grad_probs - delta[h : h + 1, rows])).astype(BF16)
+                grad_v[keys, pair] += dot_nn(probs.astype(BF16), grads)
+                grad_k[keys, pair] += dot_nn(grad_scores, queries)
+                grad_q_t[own, rows] += dot_nn(key_t[own, keys], grad_scores)
+            return carry
+
+        tiles = blocks * (blocks + 1) // 2
+        lax.fori_loop(0, tiles - blocks, tile, 0)
+        hook("low")
+        lax.fori_loop(tiles - blocks, tiles, tile, 0)
+        hook("high")
+
+        def close(start, rows):
             dq = (grad_q_t[:, rows].T * HEAD ** (-0.5)).astype(BF16)
             grad_q[rows, :] = dq
             dk = grad_k[rows, :].astype(BF16)
@@ -731,41 +735,51 @@
             acc[2:3, group] += column_sum(dq.astype(F32))
             acc[3:4, group] += column_sum(dv.astype(F32))
             back_acc[rows, :] += dot_nt(dq, wq_ref[...]) + dot_nt(dk, wk_ref[...]) + dot_nt(dv, wv_ref[...])
-        fresh_qkv[0] = dot_nn(normed_t[...], grad_q[...]).astype(BF16)
-        fresh_qkv[1] = dot_nn(normed_t[...], grad_k[...].astype(BF16)).astype(BF16)
-        fresh_qkv[2] = dot_nn(normed_t[...], grad_v[...].astype(BF16)).astype(BF16)
-        for s in range(steps, steps + groups):
-            hook("made", s)
+
+        each(close)
+        for p, grad in enumerate((grad_q, grad_k, grad_v)):
+            fresh_rest[0, :, p * lanes : (p + 1) * lanes] = dot_nn(normed_t[...], grad[...].astype(BF16)).astype(BF16)
+        hook("made")
 
     @pl.when(step == steps + groups - 1)
     def _():
-        for i in range(blocks):
-            rows = row_block(i)
+        def last(start, rows):
             unit, inverse = normalise(x_ref[rows, :].astype(F32))
             back = back_acc[rows, :]
             acc[0:1, :] += column_sum(back * unit)
             acc[1:2, :] += column_sum(back)
-            scaled = back * gain1_ref[...]
+            scaled = back * vectors[4:5, :]
             grad = middle[rows, :] + inverse * (
                 scaled - row_mean(scaled) - unit * row_mean(scaled * unit)
             )
             cot_low[rows, :] = grad.astype(BF16)
+
+        each(last)
         dx_back.start()
         hook("dx")
         small.step(0)
-        for turn, (u, phase) in enumerate(tail):
-            units[u].step(phase)
-            if turn < 4:
-                small.step(turn + 1)
-        for turn in range(min(len(tail), 4), 4):
-            small.step(turn + 1)
+
+        def round_of(turn, carry):
+            for units, first, number in ((fed, 0, steps), (rest, steps, 1 + groups)):
+                def unit(u, carry):
+                    phase, _ = chosen([(w, left[first + w]) for w in range(number)], u)
+                    for p in range(1, 9):
+                        pl.when(phase + turn == p)(functools.partial(units.step, p, u))
+                    return carry
+
+                lax.fori_loop(0, number, unit, 0)
+            for p in range(1, 5):
+                pl.when(turn == p - 1)(functools.partial(small.step, p))
+            return carry
+
+        lax.fori_loop(0, max(4, 9 - min(left.values())), round_of, 0)
         small_out[...] = small.total()
         lo_back.finish()
         dx_back.finish()
 
 
 def body(
-    lens, o, x, cot, q, k, v, lse, rows, span, lines,
+    lens, o, x, cot, q, k, v, lse, rows, span,
     ln1_gain, ln1_bias, qkv_weight, proj_weight, proj_bias, ln2_gain, ln2_bias, fc_weight, fc_bias, out_weight, out_bias,
 ):
     tokens, width = x.shape
@@ -775,7 +789,7 @@
     shape = jax.ShapeDtypeStruct
     once = pl.Buffered(1)
     whole = lambda *dims: pl.BlockSpec(dims, lambda s: (0,) * len(dims), pipeline_mode=once)
-    act, vec, mat = whole(tokens, width), whole(1, width), whole(width, width)
+    act, vec, mat = whole(tokens, width), whole(width), whole(width, width)
     feed_step = lambda s: jnp.minimum(s, steps - 1)
     back_step = lambda s: jnp.maximum(s - steps, 0)
     columns = lambda dims, first: pl.BlockSpec(dims, lambda s: (0, first + back_step(s)))
@@ -783,42 +797,36 @@
     f32 = lambda *dims: pltpu.VMEM(dims, F32)
     bf16 = lambda *dims: pltpu.VMEM(dims, BF16)
     sem = lambda *dims: pltpu.SemaphoreType.DMA(dims)
-    unit_shapes = [(2, width, width)] * steps + [(1, width, width)] + [(3, width, lanes)] * groups
-    count = len(unit_shapes)
-    unit_scratch = []
-    for line, unit_shape in zip(lines, unit_shapes):
-        unit_scratch += Unit.scratch(line, *unit_shape)
     return pl.pallas_call(
-        functools.partial(body_kernel, steps, groups, lines),
+        functools.partial(body_kernel, steps, groups),
         grid=(steps + groups,),
         out_shape=(
             shape((rows, span, width), BF16),
             shape((rows, span, width), BF16),
             shape((steps, 2, width, width), BF16),
-            shape((1, width, width), BF16),
-            shape((groups, 3, width, lanes), BF16),
+            shape((1 + groups, 1, width, width), BF16),
             shape((16, width), F32),
         ),
         in_specs=[
             pl.BlockSpec(memory_space=pltpu.SMEM),
             act, act, act, mat, vec, vec, vec,
             pl.BlockSpec((width, width), lambda s: (0, feed_step(s))),
-            pl.BlockSpec((1, width), lambda s: (0, feed_step(s))),
+            whole(steps * width),
             pl.BlockSpec((width, width), lambda s: (feed_step(s), 0)),
             vec, vec, vec,
             columns((tokens, lanes), 0), columns((tokens, lanes), 0), columns((tokens, lanes), 0),
             pl.BlockSpec((1, heads, tokens), lambda s: (back_step(s), 0, 0)),
             columns((width, lanes), 0), columns((width, lanes), groups), columns((width, lanes), 2 * groups),
         ],
-        out_specs=[anywhere] * 5 + [pl.BlockSpec((16, width), lambda s: (0, 0))],
+        out_specs=[anywhere] * 4 + [pl.BlockSpec((16, width), lambda s: (0, 0))],
         scratch_shapes=[
             f32(tokens, width), bf16(tokens, width), bf16(width, tokens), bf16(tokens, width),
             f32(tokens, width), f32(tokens, width), bf16(tokens, width), bf16(tokens, width),
-            f32(tokens, tokens), bf16(lanes, tokens), f32(lanes, tokens),
-            bf16(2, width, width), bf16(1, width, width), bf16(3, width, lanes),
-            f32(4, 16, width), f32(3, 16, width), f32(4, 16, width),
-            sem(count, 16), sem(count, 16), sem(count), sem(6), sem(6), sem(2, 3), sem(2, 3), sem(2),
-        ] + unit_scratch,
+            f32(tokens, tokens), bf16(lanes, tokens), f32(lanes, tokens), f32(8, tokens), f32(16, width),
+            bf16(2, width, width), bf16(1, width, width), f32(4, 16, width), f32(3, 16, width), f32(4, 16, width),
+            sem(6), sem(6), sem(2, 3), sem(2, 3), sem(2),
+            *Units.scratch(steps, 2, width, width), *Units.scratch(1 + groups, 1, width, width),
+        ],
         compiler_params=pltpu.CompilerParams(
             collective_id=0, has_side_effects=True, vmem_limit_bytes=VMEM_LIMIT
         ),
@@ -835,12 +843,13 @@
     ln2_gain, ln2_bias, fc_weight, fc_bias, out_weight, out_bias, input_grad,
 ):
     width = small_ref.shape[1]
-    groups, _, _, lanes = qkv_ref.shape
+    lanes = qkv_ref.shape[3]
+    groups = width // lanes
     out_weight[...] = feed_ref[0, 0].astype(F32)
     fc_weight[...] = feed_ref[0, 1].astype(F32)
     for g in range(groups):
-        qkv_weight[:, g * lanes : (g + 1) * lanes] = qkv_ref[g, 0].astype(F32)
-    proj_weight[...] = proj_ref[0].astype(F32)
+        qkv_weight[:, g * lanes : (g + 1) * lanes] = qkv_ref[1 + g, 0].astype(F32)
+    proj_weight[...] = proj_ref[0, 0].astype(F32)
     input_grad[...] = dx_ref[...].astype(F32)
 
     @pl.when((pl.program_id(0) == 0) & (pl.program_id(1) == 0))
@@ -853,9 +862,10 @@
                 ref[i * width : (i + 1) * width] = small_ref[first + i]
 
 
-def finish(feed_sums, proj_sums, qkv_sums, small, dx):
+def finish(feed_sums, rest_sums, small, dx):
     steps, _, width, _ = feed_sums.shape
-    groups, _, _, lanes = qkv_sums.shape
+    groups = rest_sums.shape[0] - 1
+    lanes = width // groups
     rows, span, _ = dx.shape
     half = width // 2
     shape = lambda *dims: jax.ShapeDtypeStruct(dims, F32)
@@ -873,8 +883,8 @@
         ),
         in_specs=[
             pl.BlockSpec((1, 2, half, width), lambda f, r: (f, 0, r, 0)),
-            pl.BlockSpec((1, half, width), lambda f, r: (0, jnp.where(f == steps - 1, r, 0), 0)),
-            pl.BlockSpec((groups, 1, half, lanes), lambda f, r: (0, third(f), jnp.where(f > 2, 1, r), 0)),
+            pl.BlockSpec((1, 1, half, width), lambda f, r: (0, 0, jnp.where(f == steps - 1, r, 0), 0)),
+            pl.BlockSpec((1 + groups, 1, half, lanes), lambda f, r: (0, 0, jnp.where(f > 2, 1, r), third(f))),
             pl.BlockSpec((16, width), lambda f, r: (0, 0)),
             row,
         ],
@@ -892,7 +902,7 @@
         ],
         compiler_params=pltpu.CompilerParams(vmem_limit_bytes=VMEM_LIMIT),
         name="finish",
-    )(feed_sums, proj_sums, qkv_sums, small, dx)
+    )(feed_sums, rest_sums, rest_sums, small, dx)
 
 
 def by_rows(
@@ -900,18 +910,15 @@
     ln2_gain, ln2_bias, fc_weight, fc_bias, out_weight, out_bias, cotangent,
 ):
     rows, span, width = tokens_in.shape
-    flat = lambda array: array.reshape(1, -1)
     q, k, v, o, lse, x, cot = front(
-        lengths, tokens_in, cotangent, flat(ln1_gain), flat(ln1_bias), qkv_weight, flat(qv_bias)
-    )
-    steps, groups = fc_weight.shape[1] // width, lse.shape[0]
-    lines = (False,) * (steps + 1 + groups)
-    layer_out, dx, feed_sums, proj_sums, qkv_sums, small = body(
-        lengths, o, x, cot.reshape(x.shape), q, k, v, lse, rows, span, lines,
-        flat(ln1_gain), flat(ln1_bias), qkv_weight, proj_weight, flat(proj_bias), flat(ln2_gain), flat(ln2_bias),
-        fc_weight, flat(fc_bias), out_weight, flat(out_bias),
-    )
-    *grads, input_grad = finish(feed_sums, proj_sums, qkv_sums, small, dx)
+        lengths, tokens_in, cotangent, ln1_gain, ln1_bias, qkv_weight, qv_bias
+    )
+    layer_out, dx, feed_sums, rest_sums, small = body(
+        lengths, o, x, cot.reshape(x.shape), q, k, v, lse, rows, span,
+        ln1_gain, ln1_bias, qkv_weight, proj_weight, proj_bias, ln2_gain, ln2_bias,
+        fc_weight, fc_bias, out_weight, out_bias,
+    )
+    *grads, input_grad = finish(feed_sums, rest_sums, small, dx)
     return (layer_out, input_grad, *grads)
 
 

time: 340 us -> 264 us (0.78); the launches traced: 334 us -> 264 us
  Pallas kernels: 323 us -> 262 us
  local copies, waits for them, and re-layouts: 9.91 us -> 1.02 us
    pallas_call x1, Pallas kernels: 244 us -> 200 us  [body(): pl.pallas_call(functools.partial(body_kernel, steps, groups), grid=(steps...]
    pallas_call x1, Pallas kernels: 61.6 us -> 44.5 us  [front(): pl.pallas_call(front_kernel, grid=(groups,), out_shape=(act, act, act, ac...]
    reshape x7 -> x0, local copies, waits for them, and re-layouts: 8.89 us -> none  [by_rows(): flat = lambda array: array.reshape(1, -1)]
where the time goes in v3:
time: 264 us
  Pallas kernels  262 us (99%)
    pallas_call x1, Pallas kernels, body(): pl.pallas_call(functools.partial(body_kernel, steps, groups), grid=(steps...  200 us
    pallas_call x1, Pallas kernels, front(): pl.pallas_call(front_kernel, grid=(groups,), out_shape=(act, act, act, ac...  44.5 us
    pallas_call x1, Pallas kernels, finish(): pl.pallas_call(finish_kernel, grid=(steps, 2), out_shape=(shape(width), s...  17.9 us

profile of v3, /device:TPU:0, one launch (start us, length us, event | category | flops | bytes accessed | tf_op | source)
XLA Modules:
  0.0 264.2 jit_solution(1569167829793276266)
XLA Ops:
  0.6 44.5 %front.1 = (bf16[1024,768]{1,0:T(8,128)(2,1)}, bf16[1024,768]{1,0:T(8,128)(2,1)}, bf16[1024,768]{1,0:T(8,128)(2,1)}, bf16[1024,768]{1,0:T(8,128)(2,1)}, f32[3,8,...) custom-call(s32[3,8]{1,0:T(4,128)} %lens_ref.3, bf16[3,256,768]{2,1,0:T(8,128)(2,1)} %tokens_ref.1, ...), custom_call_target="tpu_custom_call" | custom-call | tf_op jit(solution)/shard_map/front/pallas_call | solution.py:293
  45.2 200.1 %body.1 = (bf16[3,256,768]{2,1,0:T(8,128)(2,1)}, bf16[3,256,768]{2,1,0:T(8,128)(2,1)}, bf16[4,2,768,768]{3,2,1,0:T(8,128)(2,1)}, bf16[4,1,768,768]{3,2,1,0:T(8,128)(2,1)}, f32[16,768]{1,0:T(8,128)}) custom-call(s32[3,8]{1,0:T(4,128)} %lens_ref.3, bf16[1024,768]{1,0:T(8,128)(2,1)} %get-tuple-element.39.o_ref, bf16[1024,768]{1,0:T(8,128)(2,1)} %get-tuple-element.40.x_ref, ...), custom_call_target="tpu_custom_call" | custom-call | tf_op jit(solution)/shard_map/body/pallas_call | solution.py:800
  245.3 0.0 copy-start
  245.3 17.9 %finish.1 = (f32[768]{0:T(1024)}, f32[768]{0:T(1024)}, f32[768,2304]{1,0:T(8,128)}, f32[1536]{0:T(1024)}, f32[768,768]{1,0:T(8,128)}, /*index=5*/f32[768]{0:T(10...) custom-call(bf16[4,2,768,768]{3,2,1,0:T(8,128)(2,1)} %get-tuple-elem, ...), custom_call_target="tpu_custom_call" | custom-call | tf_op jit(solution)/shard_map/finish/pallas_call | solution.py:875
  263.2 0.0 copy-done
  263.2 1.0 copy.30
Async XLA Ops:
  245.3 17.9 %copy-start = (bf16[3,256,768]{2,1,0:T(8,128)(2,1)S(1)}, bf16[3,256,768]{2,1,0:T(8,128)(2,1)}, u32[]{:S(2)}) copy-start(bf16[3,256,768]{2,1,0:T(8,128)(2,1)} %get-tuple-element.78) | copy-start | bytes 3538948

commit v4 on v3

--- a/solution.py
+++ b/solution.py
@@ -33,6 +33,8 @@
         self.first = (row, seq + step_x + self.core * (step_y - step_x))
         self.second = (row, seq + step_y + self.core * (step_x - step_y))
 
+        self.next_z = (row + 2 - 4 * lax.rem(self.z, 2), seq)
+        self.far_z = (row + 4 - 8 * lax.div(self.z, 2), seq)
         own = seq + self.core * (3 - 2 * seq)
         self.active = own < 3
         self.my_row = jnp.minimum(own, 2)
@@ -190,12 +192,16 @@
             pl.when(row < 3)(copy.start)
         pl.when(place.active)(local(which).start)
 
-    def finish(which):
+    def arrive(which, hop):
+        if hop == 0:
+            pl.when(place.active)(local(which).wait)
+        else:
+            pl.when(place.active)(outgoing(which, hop)[1].wait_recv)
+
+    def leave(which):
         for hop in (1, 2, 3):
             row, copy = outgoing(which, hop)
             pl.when(row < 3)(copy.wait_send)
-            pl.when(place.active)(copy.wait_recv)
-        pl.when(place.active)(local(which).wait)
 
     @pl.when(pl.program_id(0) == 0)
     def _():
@@ -211,18 +217,17 @@
         def _():
             arrived[...] = jnp.zeros_like(arrived)
 
-        finish(0)
-        start(1)
-
-        def one(i, carry):
+        for hop in range(4):
+            arrive(0, hop)
+            if hop == 3:
+                start(1)
+            i = place.in_plane(hop)[0][1]
             rows = pl.ds(pl.multiple_of(i * block, block), block)
             x = arrived[i]
             x_ref[rows, :] = x
             unit, _ = normalise(x.astype(F32))
             normed[rows, :] = (unit * vectors[0:1, :] + vectors[1:2, :]).astype(BF16)
-            return carry
-
-        lax.fori_loop(0, blocks, one, 0)
+        leave(0)
 
     group = pl.ds(pl.multiple_of(pl.program_id(0) * lanes, lanes), lanes)
 
@@ -270,7 +275,9 @@
 
     @pl.when(pl.program_id(0) == pl.num_programs(0) - 1)
     def _():
-        finish(1)
+        for hop in range(4):
+            arrive(1, hop)
+        leave(1)
 
         @pl.when(jnp.logical_not(place.active))
         def _():
@@ -331,84 +338,61 @@
 
 
 class Units:
-    slots = (0, 1, 2, 3, 6, 9, 10, 11)
-
-    def __init__(self, place, fresh, out, recv0, recv1, recv2, recv3, part, send_sem, recv_sem, copy_sem):
+    def __init__(self, place, fresh, out, recv0, recv1, recv2, recv3, recv4, part, send_sem, recv_sem, copy_sem):
         self.place, self.fresh, self.out, self.part = place, fresh, out, part
-        self.recv = (recv0, recv1, recv2, recv3)
+        self.recv = (recv0, recv1, recv2, recv3, recv4)
         self.send_sem, self.recv_sem, self.copy_sem = send_sem, recv_sem, copy_sem
         _, rows, columns = fresh.shape
         self.size = (rows // 2, rows // 4, rows // 8, rows // 16)
         self.wide = columns // 2
-        bits = (place.core, place.first_bit, place.second_bit)
-        self.own = [bit * size for bit, size in zip(bits, self.size)]
-        self.away = [(1 - bit) * size for bit, size in zip(bits, self.size)]
+        self.bits = (place.core, place.first_bit, lax.rem(place.z, 2), lax.div(place.z, 2), place.second_bit)
+        self.partners = (place.sibling, place.first, place.next_z, place.far_z, place.second)
 
     @staticmethod
     def scratch(count, n, rows, columns):
-        vmem = lambda *shape: pltpu.VMEM(shape, BF16)
-        sem = lambda *shape: pltpu.SemaphoreType.DMA(shape)
-        return [
-            vmem(count, n, rows // 2, columns), vmem(count, n, rows // 4, columns), vmem(count, n, rows // 8, columns),
-            vmem(count, 3, n, rows // 16, columns // 2), vmem(count, n, rows // 16, columns // 2),
-            sem(count, 12), sem(count, 12), sem(count),
+        vmem = lambda *shape: pltpu.VMEM((count, n, *shape), BF16)
+        sem = pltpu.SemaphoreType.DMA
+        return [vmem(rows // 2 ** k, columns) for k in range(1, 5)] + [
+            vmem(rows // 16, columns // 2), vmem(rows // 16, columns // 2),
+            sem((count, 10)), sem((count, 10)), sem((count,)),
         ]
 
-    def rows(self, start, count):
-        return pl.ds(pl.multiple_of(start, self.size[3]), count)
-
-    def piece(self, start, z):
-        columns = pl.ds(pl.multiple_of(lax.rem(z, 2) * self.wide, self.wide), self.wide)
-        return self.rows(start + lax.div(z, 2) * self.size[3], self.size[3]), columns
-
-    def copies(self, phase, u):
-        place, out, size, own = self.place, self.out, self.size, self.own
-        first = self.slots[phase]
-        sems = lambda i: (self.send_sem.at[u, first + i], self.recv_sem.at[u, first + i])
-        hops = (1, 2, 3)
-        if phase == 0:
-            return [send(self.fresh.at[:, self.rows(self.away[0], size[0])], self.recv[0].at[u], *sems(0), place.sibling)]
-        if phase < 3:
-            source = self.recv[phase - 1].at[u, :, self.rows(self.away[phase], size[phase])]
-            return [send(source, self.recv[phase].at[u], *sems(0), (place.first, place.second)[phase - 1])]
-        if phase == 3:
-            return [
-                send(
-                    self.recv[2].at[u, :, *self.piece(0, lax.rem(place.z + hop, 4))], self.recv[3].at[u, hop - 1],
-                    *sems(hop - 1), place.along_z(hop),
-                )
-                for hop in hops
-            ]
-        if phase == 4:
-            where = out.at[u, :, *self.piece(own[0] + own[1] + own[2], place.z)]
-            return [send(self.part.at[u], where, *sems(hop - 1), place.along_z(hop)) for hop in hops]
-        start, count, other = {
-            5: (own[0] + own[1] + own[2], size[2], place.second),
-            6: (own[0] + own[1], size[1], place.first),
-            7: (own[0], size[0], place.sibling),
-        }[phase]
-        where = out.at[u, :, self.rows(start, count)]
-        return [send(where, where, *sems(0), other)]
+    def part_of(self, stage, bit):
+        if stage == 4:
+            return slice(None), pl.ds(pl.multiple_of(bit * self.wide, self.wide), self.wide)
+        size = self.size[stage]
+        return pl.ds(pl.multiple_of(bit * size, size), size), slice(None)
+
+    def region(self, stage):
+        start = sum(bit * size for bit, size in zip(self.bits[: min(stage, 3) + 1], self.size))
+        size = self.size[min(stage, 3)]
+        rows = pl.ds(pl.multiple_of(start, size), size)
+        return rows, self.part_of(4, self.bits[4])[1] if stage == 4 else slice(None)
+
+    def copy(self, phase, u):
+        sems = self.send_sem.at[u, phase], self.recv_sem.at[u, phase]
+        if phase < 5:
+            source = self.fresh if phase == 0 else self.recv[phase - 1].at[u]
+            source = source.at[:, *self.part_of(phase, 1 - self.bits[phase])]
+            return send(source, self.recv[phase].at[u], *sems, self.partners[phase])
+        where = self.out.at[u, :, *self.region(9 - phase)]
+        return send(self.part.at[u] if phase == 5 else where, where, *sems, self.partners[9 - phase])
 
     def local(self, u):
-        where = self.out.at[u, :, *self.piece(self.own[0] + self.own[1] + self.own[2], self.place.z)]
-        return pltpu.make_async_copy(self.part.at[u], where, self.copy_sem.at[u])
+        return pltpu.make_async_copy(self.part.at[u], self.out.at[u, :, *self.region(4)], self.copy_sem.at[u])
 
     def add(self, phase, u):
-        step = self.size[3]
-        if phase == 3:
-            rows, columns = self.piece(0, self.place.z)
-            total = self.recv[2][u, :, rows, columns].astype(F32)
-            for hop in range(3):
-                total = total + self.recv[3][u, hop].astype(F32)
-            self.part[u] = total.astype(BF16)
-            return
         source = self.fresh if phase == 0 else self.recv[phase - 1].at[u]
         target = self.recv[phase].at[u]
+        step = self.size[3]
+        if phase == 4:
+            own = source[:, :, self.part_of(4, self.bits[4])[1]].astype(F32)
+            self.part[u] = (own + target[...].astype(F32)).astype(BF16)
+            return
 
         def one(i, carry):
-            here = self.rows(i * step, step)
-            there = self.rows(self.own[phase] + i * step, step)
+            here = pl.ds(pl.multiple_of(i * step, step), step)
+            there = pl.ds(pl.multiple_of(self.bits[phase] * self.size[phase] + i * step, step), step)
             for panel in range(self.fresh.shape[0]):
                 total = source[panel, there, :].astype(F32) + target[panel, here, :].astype(F32)
                 target[panel, here, :] = total.astype(BF16)
@@ -418,16 +402,14 @@
 
     def step(self, phase, u):
         if phase > 0:
-            for copy in self.copies(phase - 1, u):
-                copy.wait()
-            if phase == 5:
+            self.copy(phase - 1, u).wait()
+            if phase == 6:
                 self.local(u).wait()
-        if 0 < phase < 5:
+        if 0 < phase < 6:
             self.add(phase - 1, u)
-        if phase < 8:
-            for copy in self.copies(phase, u):
-                copy.start()
-        if phase == 4:
+        if phase < 10:
+            self.copy(phase, u).start()
+        if phase == 5:
             self.local(u).start()
 
 
@@ -450,10 +432,10 @@
     def local(self):
         return pltpu.make_async_copy(self.block(self.place.seq), self.target.at[self.place.my_row], self.copy_sem)
 
-    def start(self):
-        for hop in (3, 1, 2):
-            pl.when(self.place.active)(self.outgoing(hop)[1].start)
-        pl.when(self.place.active)(self.local().start)
+    def start(self, hop):
+        pl.when(self.place.active)(self.outgoing(hop)[1].start)
+        if hop == 3:
+            pl.when(self.place.active)(self.local().start)
 
     def finish(self):
         for hop in (1, 2, 3):
@@ -464,47 +446,69 @@
 
 
 def plan(hooks, sizes, made):
-    free = {"core": 0.0, "plane": 0.0, "line": 0.0}
-    delay = {"core": 1.5, "plane": 3.5, "line": 3.0}
-    now, flight, plans = 0.0, {}, {}
+    free = {"core": 0.0, "plane": 0.0, "near": 0.0, "far": 0.0}
+    delay = {"core": 1.5, "plane": 3.5, "near": 3.0, "far": 3.5}
+    now, flight, plans, spare = 0.0, {}, {}, []
+    small = len(sizes)
 
     def go(unit, phase):
         nonlocal now
         now += 0.3
-        if phase == 8:
-            flight[unit] = (8, 1e9)
+        if phase == (4 if unit == small else 10):
+            del flight[unit]
             return
-        kind = ("core", "plane", "plane", "line")[min(phase, 7 - phase)]
-        time = sizes[unit] * (0.5 / 0.6, 0.25 / 0.094, 0.125 / 0.094, 0.25 / 0.094)[min(phase, 7 - phase)]
+        if unit == small:
+            kind, time = ("core", "plane", "plane", "far")[phase], 0.3
+        else:
+            stage = min(phase, 9 - phase)
+            kind = ("core", "plane", "near", "far", "plane")[stage]
+            time = sizes[unit] * (0.5 / 0.6, 0.25 / 0.094, 0.25 / 0.094, 0.25 / 0.094, 0.03125 / 0.094)[stage]
         begin = max(now, free[kind])
         free[kind] = begin + time
+        if kind == "far":
+            free["near"] = max(now, free["near"]) + time / 2
         flight[unit] = (phase, begin + time + delay[kind])
+
+    def fill(items):
+        if spare and free["plane"] <= now + 4.0:
+            free["plane"] = now + 5.3
+            items.append(spare.pop(0))
 
     for name, compute in hooks:
         now += compute
-        plans[name] = []
+        items = plans[name] = []
         for unit in sorted(flight, key=lambda u: flight[u][1]):
             phase, end = flight[unit]
             if end <= now + 0.5:
-                plans[name].append((unit, phase + 1))
+                items.append((unit, phase + 1))
                 go(unit, phase + 1)
         for unit, hook in made.items():
             if hook == name:
-                plans[name].append((unit, 0))
+                items.append((unit, 0))
                 go(unit, 0)
         if name in ("lo", "dx"):
-            free["plane"] = max(now, free["plane"]) + 16.0
-    return plans, {unit: phase + 1 for unit, (phase, _) in flight.items()}, now
+            spare += [(name, hop) for hop in (3, 1, 2)]
+        fill(items)
+    tail = [(small, 0)]
+    go(small, 0)
+    while flight:
+        unit = min(flight, key=lambda u: flight[u][1])
+        phase, end = flight[unit]
+        now = max(now, end)
+        tail.append((unit, phase + 1))
+        go(unit, phase + 1)
+        fill(tail)
+    return plans, tail + spare, max(now, free["plane"] + 3.5)
 
 
 def timetable(steps, groups):
     hooks = []
     for s in range(steps):
-        hooks += [(("early", s), 14.0 if s == 0 else 3.0), (("late", s), 3.0), (("fed", s), 2.6)]
+        hooks += [(("early", s), 18.0 if s == 0 else 3.0), (("late", s), 3.0), (("fed", s), 2.6)]
     hooks += [("lo", 7.0), ("proj", 1.5), ("turn", 3.0)]
     for s in range(steps, steps + groups):
-        hooks += [(("low", s), 5.0), (("high", s), 3.5), (("made", s), 2.5)]
-    hooks.append(("dx", 3.0))
+        hooks += [(("low", s), 6.0 + 1.2 * (s > steps)), (("high", s), 4.0), (("made", s), 1.8)]
+    hooks.append(("dx", 4.2))
     made = {s: ("fed", s) for s in range(steps)}
     made[steps] = "proj"
     made.update({steps + 1 + g: ("made", steps + g) for g in range(groups)})
@@ -528,18 +532,20 @@
     place = Place()
     acc = sums.at[0]
 
-    fed = Units(place, fresh_feed, feed_out, *unit_scratch[:8])
-    rest = Units(place, fresh_rest, rest_out, *unit_scratch[8:])
+    sets = [
+        Units(place, fresh_feed, feed_out, *unit_scratch[:9]), Units(place, fresh_rest, rest_out, *unit_scratch[9:])
+    ]
     small = SmallReducer(place, sums, small_recv, line_sums, small_send, small_recv_sem)
     lo_back = Exchange(place, normed, lo_out, out_send.at[0], out_recv.at[0], out_copy.at[0])
     dx_back = Exchange(place, cot_low, dx_out, out_send.at[1], out_recv.at[1], out_copy.at[1])
+    exchanges = {"lo": lo_back, "dx": dx_back}
 
     hooks, made = timetable(steps, groups)
     panel = width * width * 2e-6
     count = steps + 1 + groups
-    plans, left, _ = plan(hooks, [2 * panel] * steps + [panel] * (1 + groups), made)
+    plans, tail, _ = plan(hooks, [2 * panel] * steps + [panel] * (1 + groups), made)
     order = [name for name, _ in hooks]
-    freed = {u: order.index(name) for name, actions in plans.items() for u, phase in actions if phase == 1}
+    freed = {u: order.index(name) for name, items in plans.items() for u, phase in items if phase == 1}
     for u in [*range(steps - 1), *range(steps, steps + groups)]:
         assert freed[u] < order.index(made[u + 1])
 
@@ -550,21 +556,36 @@
             value, found = value + hit * item, found + hit
         return value, found > 0
 
+    def start(item, index=None):
+        u, phase = item
+        if u in exchanges:
+            return functools.partial(exchanges[u].start, phase)
+        if u == count:
+            return functools.partial(small.step, phase)
+        return functools.partial(sets[u >= steps].step, phase, number(item) if index is None else index)
+
+    def kind(item):
+        u, phase = item
+        return (u if u in exchanges or u == count else int(u >= steps)), phase
+
+    def number(item):
+        u = item[0]
+        return 0 if u in exchanges or u == count else u - steps * (u >= steps)
+
     def hook(name):
         if name in plans:
-            for u, phase in plans[name]:
-                units, index = (fed, u) if u < steps else (rest, u - steps)
-                units.step(phase, index)
+            for item in plans[name]:
+                start(item)()
             return
-        seen, bodies = {}, {}
+        bodies = {}
         for s in range(steps + groups):
-            for place_in_list, (u, phase) in enumerate(plans.get((name, s), [])):
-                kind = (u < steps, phase)
-                turn = seen[kind, s] = seen.get((kind, s), -1) + 1
-                bodies.setdefault((*kind, turn), []).append((s, u if u < steps else u - steps))
-        for (is_fed, phase, _), pairs in sorted(bodies.items(), key=lambda item: -item[0][1]):
-            index, found = chosen(pairs, step)
-            pl.when(found)(functools.partial((fed if is_fed else rest).step, phase, index))
+            seen = {}
+            for item in plans.get((name, s), []):
+                turn = seen[kind(item)] = seen.get(kind(item), -1) + 1
+                bodies.setdefault((kind(item), turn), []).append((s, item))
+        for _, pairs in sorted(bodies.items(), key=lambda body: -body[0][0][1]):
+            index, found = chosen([(s, number(item)) for s, item in pairs], step)
+            pl.when(found)(start(pairs[0][1], index))
 
     def each(body, first=0, last=blocks):
         def run(i, carry):
@@ -593,7 +614,6 @@
             unit, _ = normalise(mid)
             h2 = unit * vectors[1:2, :] + vectors[2:3, :]
             normed[rows, :] = h2.astype(BF16)
-            normed_t[:, rows] = h2.T.astype(BF16)
             keep = keep_column(lens_ref, place.my_row, start, span)
             low = (branch_scale * (keep * cot_ref[rows, :].astype(F32))).astype(BF16)
             cot_low[rows, :] = low
@@ -626,7 +646,7 @@
         each(chunk, blocks // 2, blocks)
         hook("late")
         fresh_feed[0] = dot_tn(hidden[...], cot_low[...]).astype(BF16)
-        fresh_feed[1] = dot_nn(normed_t[...], back_low[...]).astype(BF16)
+        fresh_feed[1] = dot_tn(normed[...], back_low[...]).astype(BF16)
         hook("fed")
 
     @pl.when(step == steps - 1)
@@ -654,7 +674,6 @@
 
         each(end)
         hook("lo")
-        lo_back.start()
         fresh_rest[0] = dot_tn(o_ref[...], hidden[...]).astype(BF16)
         hook("proj")
 
@@ -730,16 +749,22 @@
         def close(start, rows):
             dq = (grad_q_t[:, rows].T * HEAD ** (-0.5)).astype(BF16)
             grad_q[rows, :] = dq
-            dk = grad_k[rows, :].astype(BF16)
-            dv = grad_v[rows, :].astype(BF16)
             acc[2:3, group] += column_sum(dq.astype(F32))
-            acc[3:4, group] += column_sum(dv.astype(F32))
-            back_acc[rows, :] += dot_nt(dq, wq_ref[...]) + dot_nt(dk, wk_ref[...]) + dot_nt(dv, wv_ref[...])
+            acc[3:4, group] += column_sum(grad_v[rows, :].astype(BF16).astype(F32))
 
         each(close)
         for p, grad in enumerate((grad_q, grad_k, grad_v)):
             fresh_rest[0, :, p * lanes : (p + 1) * lanes] = dot_nn(normed_t[...], grad[...].astype(BF16)).astype(BF16)
         hook("made")
+
+        def pull(start, rows):
+            back_acc[rows, :] += (
+                dot_nt(grad_q[rows, :], wq_ref[...])
+                + dot_nt(grad_k[rows, :].astype(BF16), wk_ref[...])
+                + dot_nt(grad_v[rows, :].astype(BF16), wv_ref[...])
+            )
+
+        each(pull)
 
     @pl.when(step == steps + groups - 1)
     def _():
@@ -755,24 +780,19 @@
             cot_low[rows, :] = grad.astype(BF16)
 
         each(last)
-        dx_back.start()
         hook("dx")
-        small.step(0)
-
-        def round_of(turn, carry):
-            for units, first, number in ((fed, 0, steps), (rest, steps, 1 + groups)):
-                def unit(u, carry):
-                    phase, _ = chosen([(w, left[first + w]) for w in range(number)], u)
-                    for p in range(1, 9):
-                        pl.when(phase + turn == p)(functools.partial(units.step, p, u))
-                    return carry
-
-                lax.fori_loop(0, number, unit, 0)
-            for p in range(1, 5):
-                pl.when(turn == p - 1)(functools.partial(small.step, p))
+        kinds = sorted({kind(item) for item in tail}, key=str)
+        codes = [(t, kinds.index(kind(item)) * count + number(item)) for t, item in enumerate(tail)]
+
+        def turn(t, carry):
+            code, _ = chosen(codes, t)
+            which, index = lax.div(code, count), lax.rem(code, count)
+            for k, this in enumerate(kinds):
+                item = next(item for item in tail if kind(item) == this)
+                pl.when(which == k)(start(item, index))
             return carry
 
-        lax.fori_loop(0, max(4, 9 - min(left.values())), round_of, 0)
+        lax.fori_loop(0, len(tail), turn, 0)
         small_out[...] = small.total()
         lo_back.finish()
         dx_back.finish()
@@ -867,14 +887,15 @@
     groups = rest_sums.shape[0] - 1
     lanes = width // groups
     rows, span, _ = dx.shape
-    half = width // 2
+    cuts = 1
+    half = width // cuts
     shape = lambda *dims: jax.ShapeDtypeStruct(dims, F32)
     flat = lambda n: pl.BlockSpec((n * width,), lambda f, r: (0,))
     third = lambda f: jnp.minimum(f, 2)
-    row = pl.BlockSpec((1, span // 2, width), lambda f, r: (jnp.minimum(f, rows - 1), jnp.where(f > rows - 1, 1, r), 0))
+    row = pl.BlockSpec((1, span // cuts, width), lambda f, r: (jnp.minimum(f, rows - 1), jnp.where(f > rows - 1, cuts - 1, r), 0))
     return pl.pallas_call(
         finish_kernel,
-        grid=(steps, 2),
+        grid=(steps, cuts),
         out_shape=(
             shape(width), shape(width), shape(width, 3 * width), shape(2 * width),
             shape(width, width), shape(width), shape(width), shape(width),
@@ -884,19 +905,19 @@
         in_specs=[
             pl.BlockSpec((1, 2, half, width), lambda f, r: (f, 0, r, 0)),
             pl.BlockSpec((1, 1, half, width), lambda f, r: (0, 0, jnp.where(f == steps - 1, r, 0), 0)),
-            pl.BlockSpec((1 + groups, 1, half, lanes), lambda f, r: (0, 0, jnp.where(f > 2, 1, r), third(f))),
+            pl.BlockSpec((1 + groups, 1, half, lanes), lambda f, r: (0, 0, jnp.where(f > 2, cuts - 1, r), third(f))),
             pl.BlockSpec((16, width), lambda f, r: (0, 0)),
             row,
         ],
         out_specs=[
             flat(1), flat(1),
-            pl.BlockSpec((half, width), lambda f, r: (jnp.where(f > 2, 1, r), third(f))),
+            pl.BlockSpec((half, width), lambda f, r: (jnp.where(f > 2, cuts - 1, r), third(f))),
             flat(2),
             pl.BlockSpec((half, width), lambda f, r: (jnp.where(f == steps - 1, r, 0), 0)),
             flat(1), flat(1), flat(1),
             pl.BlockSpec((half, width), lambda f, r: (r, f)),
             flat(steps),
-            pl.BlockSpec((half, width), lambda f, r: (2 * f + r, 0)),
+            pl.BlockSpec((half, width), lambda f, r: (cuts * f + r, 0)),
             flat(1),
             row,
         ],

time: 264 us -> 247 us (0.936)
  Pallas kernels: 262 us -> 245 us
    pallas_call x1, Pallas kernels: 200 us -> 186 us  [body(): pl.pallas_call(functools.partial(body_kernel, steps, groups), grid=(steps...]
where the time goes in v4:
time: 247 us; the launch traced here: 246 us
  Pallas kernels  245 us (99%)
    pallas_call x1, Pallas kernels, body(): pl.pallas_call(functools.partial(body_kernel, steps, groups), grid=(steps...  186 us
    pallas_call x1, Pallas kernels, front(): pl.pallas_call(front_kernel, grid=(groups,), out_shape=(act, act, act, ac...  43.3 us
    pallas_call x1, Pallas kernels, finish(): pl.pallas_call(finish_kernel, grid=(steps, cuts), out_shape=(shape(width)...  15.5 us

profile of v4, /device:TPU:0, one launch (start us, length us, event | category | flops | bytes accessed | tf_op | source)
XLA Modules:
  0.0 246.4 jit_solution(6916066164241948706)
XLA Ops:
  0.6 43.3 %front.1 = (bf16[1024,768]{1,0:T(8,128)(2,1)}, bf16[1024,768]{1,0:T(8,128)(2,1)}, bf16[1024,768]{1,0:T(8,128)(2,1)}, bf16[1024,768]{1,0:T(8,128)(2,1)}, f32[3,8,...) custom-call(s32[3,8]{1,0:T(4,128)} %lens_ref.3, bf16[3,256,768]{2,1,0:T(8,128)(2,1)} %tokens_ref.1, ...), custom_call_target="tpu_custom_call" | custom-call | tf_op jit(solution)/shard_map/front/pallas_call | solution.py:300
  44.0 186.0 %body.1 = (bf16[3,256,768]{2,1,0:T(8,128)(2,1)}, bf16[3,256,768]{2,1,0:T(8,128)(2,1)}, bf16[4,2,768,768]{3,2,1,0:T(8,128)(2,1)}, bf16[4,1,768,768]{3,2,1,0:T(8,128)(2,1)}, f32[16,768]{1,0:T(8,128)}) custom-call(s32[3,8]{1,0:T(4,128)} %lens_ref.3, bf16[1024,768]{1,0:T(8,128)(2,1)} %get-tuple-element.39.o_ref, bf16[1024,768]{1,0:T(8,128)(2,1)} %get-tuple-element.40.x_ref, ...), custom_call_target="tpu_custom_call" | custom-call | tf_op jit(solution)/shard_map/body/pallas_call | solution.py:820
  229.9 0.0 copy-start
  230.0 15.5 %finish.1 = (f32[768]{0:T(1024)}, f32[768]{0:T(1024)}, f32[768,2304]{1,0:T(8,128)}, f32[1536]{0:T(1024)}, f32[768,768]{1,0:T(8,128)}, /*index=5*/f32[768]{0:T(10...) custom-call(bf16[4,2,768,768]{3,2,1,0:T(8,128)(2,1)} %get-tuple-elem, ...), custom_call_target="tpu_custom_call" | custom-call | tf_op jit(solution)/shard_map/finish/pallas_call | solution.py:896
  245.4 0.0 copy-done
  245.4 1.0 copy.30
Async XLA Ops:
  229.9 15.5 %copy-start = (bf16[3,256,768]{2,1,0:T(8,128)(2,1)S(1)}, bf16[3,256,768]{2,1,0:T(8,128)(2,1)}, u32[]{:S(2)}) copy-start(bf16[3,256,768]{2,1,0:T(8,128)(2,1)} %get-tuple-element.78) | copy-start | bytes 3538948

commit v5 on v4

--- a/solution.py
+++ b/solution.py
@@ -487,7 +487,7 @@
                 items.append((unit, 0))
                 go(unit, 0)
         if name in ("lo", "dx"):
-            spare += [(name, hop) for hop in (3, 1, 2)]
+            spare += [(name, hop) for hop in (3, 2, 1)]
         fill(items)
     tail = [(small, 0)]
     go(small, 0)

time: 247 us -> 246 us (level)
  no operation moved by 1% of the time
where the time goes in v5:
time: 246 us
  Pallas kernels  244 us (99%)
    pallas_call x1, Pallas kernels, body(): pl.pallas_call(functools.partial(body_kernel, steps, groups), grid=(steps...  186 us
    pallas_call x1, Pallas kernels, front(): pl.pallas_call(front_kernel, grid=(groups,), out_shape=(act, act, act, ac...  43.3 us
    pallas_call x1, Pallas kernels, finish(): pl.pallas_call(finish_kernel, grid=(steps, cuts), out_shape=(shape(width)...  15.5 us

profile of v5, /device:TPU:0, one launch (start us, length us, event | category | flops | bytes accessed | tf_op | source)
XLA Modules:
  0.0 246.1 jit_solution(10808658847667234433)
XLA Ops:
  0.6 43.3 %front.1 = (bf16[1024,768]{1,0:T(8,128)(2,1)}, bf16[1024,768]{1,0:T(8,128)(2,1)}, bf16[1024,768]{1,0:T(8,128)(2,1)}, bf16[1024,768]{1,0:T(8,128)(2,1)}, f32[3,8,...) custom-call(s32[3,8]{1,0:T(4,128)} %lens_ref.3, bf16[3,256,768]{2,1,0:T(8,128)(2,1)} %tokens_ref.1, ...), custom_call_target="tpu_custom_call" | custom-call | tf_op jit(solution)/shard_map/front/pallas_call | solution.py:300
  44.0 185.6 %body.1 = (bf16[3,256,768]{2,1,0:T(8,128)(2,1)}, bf16[3,256,768]{2,1,0:T(8,128)(2,1)}, bf16[4,2,768,768]{3,2,1,0:T(8,128)(2,1)}, bf16[4,1,768,768]{3,2,1,0:T(8,128)(2,1)}, f32[16,768]{1,0:T(8,128)}) custom-call(s32[3,8]{1,0:T(4,128)} %lens_ref.3, bf16[1024,768]{1,0:T(8,128)(2,1)} %get-tuple-element.39.o_ref, bf16[1024,768]{1,0:T(8,128)(2,1)} %get-tuple-element.40.x_ref, ...), custom_call_target="tpu_custom_call" | custom-call | tf_op jit(solution)/shard_map/body/pallas_call | solution.py:820
  229.6 0.0 copy-start
  229.6 15.5 %finish.1 = (f32[768]{0:T(1024)}, f32[768]{0:T(1024)}, f32[768,2304]{1,0:T(8,128)}, f32[1536]{0:T(1024)}, f32[768,768]{1,0:T(8,128)}, /*index=5*/f32[768]{0:T(10...) custom-call(bf16[4,2,768,768]{3,2,1,0:T(8,128)(2,1)} %get-tuple-elem, ...), custom_call_target="tpu_custom_call" | custom-call | tf_op jit(solution)/shard_map/finish/pallas_call | solution.py:896
  245.1 0.0 copy-done
  245.1 1.0 copy.30
Async XLA Ops:
  229.6 15.5 %copy-start = (bf16[3,256,768]{2,1,0:T(8,128)(2,1)S(1)}, bf16[3,256,768]{2,1,0:T(8,128)(2,1)}, u32[]{:S(2)}) copy-start(bf16[3,256,768]{2,1,0:T(8,128)(2,1)} %get-tuple-element.78) | copy-start | bytes 3538948
